TPU v7x, 32 devices: a whole 2x2x4 slice. The times are simulated.
32 devices in a mesh: tm: 8 (over z, x), mode: 4 (over y, core).
Axes of the slice: x: 2, y: 2, z: 4, core: 2. Of those that a mesh axis runs over, the one named last changes fastest.
Arguments:
- observations: bfloat16 [512, 2048], P('tm', 'mode'), may hold values from -6 to 6
- basis: bfloat16 [2048, 2048], P(None, 'mode'), may hold values from -0.125 to 0.125
- eigvals: float32 [2048], P('mode'), may hold values from 0.05 to 4
- lengths: float32 [2048], P('mode'), may hold values from 8 to 2048
- noise: float32 [1], replicated, may hold values from 0.3 to 1
Outputs:
- grad_obs: float32 [512, 2048], P('tm', 'mode')
All inputs are finite; a program needn't handle non-finite values.
Results may differ from a plain program's by a relative error of at most 0.0024.
Values may be sent and summed in bfloat16 or wider, within the bound.
No kernel may reach another device: no remote copies, remote signals or barrier semaphores. Data moves between devices by JAX's collectives and lax.ppermute only.
A program may use at most 64 MiB of HBM per device.

v0:
```python
import functools
import math

import jax
import jax.numpy as jnp
from jax import lax
from jax.experimental import pallas as pl
from jax.experimental.pallas import tpu as pltpu
from jax.sharding import PartitionSpec as P

F32 = jnp.float32
SUB = 8
VMEM_LIMIT = 24 * 1024 * 1024


def mat_mul(p, q):
    return (
        p[0] * q[0] + p[1] * q[2],
        p[0] * q[1] + p[1] * q[3],
        p[2] * q[0] + p[3] * q[2],
        p[2] * q[1] + p[3] * q[3],
    )


def mat_trans(p):
    return (p[0], p[2], p[1], p[3])


def mat_add(p, q):
    return tuple(a + b for a, b in zip(p, q))


def mat_sub(p, q):
    return tuple(a - b for a, b in zip(p, q))


def mat_pick(flag, p, q):
    return tuple(jnp.where(flag, a, b) for a, b in zip(p, q))


def full(s):
    return (s[0], s[1], s[1], s[2])


def congruence(s, f):
    t = (
        s[0] * f[0] + s[1] * f[2],
        s[0] * f[1] + s[1] * f[3],
        s[1] * f[0] + s[2] * f[2],
        s[1] * f[1] + s[2] * f[3],
    )
    return (f[0] * t[0] + f[2] * t[2], f[0] * t[1] + f[2] * t[3], f[1] * t[1] + f[3] * t[3])


def power(squares, exponent, like):
    one, zero = jnp.ones_like(like), jnp.zeros_like(like)
    out = None
    for bit, base in enumerate(squares):
        flag = (exponent & (1 << bit)) != 0
        if out is None:
            out = mat_pick(flag, base, (one, zero, zero, one))
        else:
            out = mat_pick(flag, mat_mul(out, base), out)
    return out


def gramian(squares, grams, count, like):
    zero = jnp.zeros_like(like)
    out = (zero, zero, zero)
    for bit, (base, gram) in enumerate(zip(squares, grams)):
        flag = (count & (1 << bit)) != 0
        out = mat_pick(flag, mat_add(gram, congruence(out, base)), out)
    return out


def steady_state(scale2, length, noise_var):
    lam = math.sqrt(3.0) / length
    decay = jnp.exp(-lam)
    twice = 2.0 * lam
    fall = jnp.exp(-twice)
    rho = scale2 / noise_var
    series = 1.0 / 604800.0
    for factor in (60480.0, 6720.0, 840.0, 120.0, 20.0, 4.0, 1.0):
        series = series * twice + 1.0 / factor
    lower = fall * twice * twice * twice * (1.0 / 6.0) * series
    loss = 1.0
    for order in (8, 7, 6, 5, 4, 3, 2):
        loss = 1.0 - lam * (1.0 / order) * loss
    loss = lam * loss
    q00 = rho * lower
    q01 = 2.0 * rho * lam * lam * fall
    q11 = rho * (lower + twice * fall)
    slope = decay * lam
    tilt = loss + slope
    g0 = q00 * tilt * tilt + 2.0 * slope * q01 * tilt + slope * slope * q11
    g1 = slope * q01 - decay * (1.0 - lam) * q00
    loss2 = loss * loss
    c2 = decay * decay
    u = (2.0 * decay * loss2 - g1) / c2
    v = (loss2 * loss2 + g0) / c2
    root = jnp.sqrt(v * (v + 4.0 * u + 16.0))
    product = 4.0 * v / (v + root + jnp.sqrt(2.0 * v * (v + 2.0 * u + root)))
    total = 0.5 * (jnp.sqrt(u * u + 4.0 * u - 2.0 * v + 2.0 * root) - u)
    gain0 = total - 2.0 * loss
    gain1 = (product - loss2 - gain0 * tilt) / slope
    inverse = (1.0 - total + product) / c2
    inn = c2 / (1.0 - total + product)
    closed = (1.0 + slope - loss - gain0, slope, -slope - gain1, decay * (1.0 - lam))
    p00 = inn * ((1.0 - lam) * gain0 - lam * gain1) / decay
    p01 = inn * (lam * gain0 + (1.0 + lam) * gain1) / decay
    p11 = (
        p01 * (loss * (1.0 + decay) + 2.0 * slope * slope)
        + slope * decay * (1.0 + lam) * p00
        - q01
        + gain0 * gain1 * inn
    ) / (slope * decay * (1.0 - lam))
    return closed, gain0, gain1, inverse, (rho - p00, -p01, rho - p11)


def coefficients_kernel(blocks, me_ref, noise_ref, *refs):
    arguments, (const_ref, w_ref, g_ref, merge_ref, basis_ref, obs_ref) = (
        refs[:4],
        refs[4:10],
    )
    scale_ref, length_ref, sems = refs[10:]
    copies = [
        pltpu.make_async_copy(source, target, sems.at[k])
        for k, (source, target) in enumerate(
            zip(arguments, (scale_ref, length_ref, obs_ref, basis_ref))
        )
    ]
    for copy in copies:
        copy.start()
    for copy in copies[:2]:
        copy.wait()
    steps = w_ref.shape[1]
    width = scale_ref.shape[1]
    tile = (SUB, width)
    me = me_ref[0]
    scale2 = jnp.broadcast_to(scale_ref[...], tile)
    length = jnp.broadcast_to(length_ref[...], tile)
    noise_var = jnp.full(tile, noise_ref[0], F32)
    closed, gain0, gain1, inverse, excess = steady_state(scale2, length, noise_var)
    zero = jnp.zeros(tile, F32)

    squares, grams = [closed], [(inverse, zero, zero)]
    doublings = (steps * blocks).bit_length() - 1
    for _ in range(doublings):
        base = squares[-1]
        grams.append(mat_add(grams[-1], congruence(grams[-1], base)))
        squares.append(mat_mul(base, base))
    local = steps.bit_length() - 1
    consts = closed + (gain0, gain1, inverse) + squares[3] + squares[4] + squares[5]
    for place, value in enumerate(consts):
        const_ref[place] = value
    const_ref[len(consts)] = -1.0 / noise_var
    for level in range(blocks.bit_length() - 1):
        for place, value in enumerate(squares[local + level] + grams[local + level]):
            merge_ref[7 * level + place : 7 * level + place + 1, :] = value[0:1, :]

    row = lax.broadcasted_iota(jnp.int32, tile, 0)
    small, gram_small = squares[:3], grams[:3]
    behind = power(small, 7 - row, zero)
    gram = gramian(small, gram_small, 7 - row, zero)
    eight, gram_eight = squares[3], grams[3]
    parts = steps // SUB
    for part in range(parts - 1, -1, -1):
        rows = pl.ds(part * SUB, SUB)
        w_ref[0, rows, :] = behind[0] * gain0 + behind[1] * gain1
        w_ref[1, rows, :] = behind[2] * gain0 + behind[3] * gain1
        k0 = gain0 * gram[0] + gain1 * gram[1]
        k1 = gain0 * gram[1] + gain1 * gram[2]
        w_ref[2, rows, :] = inverse - (k0 * closed[0] + k1 * closed[2])
        w_ref[3, rows, :] = -(k0 * closed[1] + k1 * closed[3])
        if part:
            behind = mat_mul(behind, eight)
            gram = mat_add(gram_eight, congruence(gram, eight))
    ahead = power(small, row, zero)
    for part in range(parts):
        rows = pl.ds(part * SUB, SUB)
        u0, u1 = w_ref[2, rows, :], w_ref[3, rows, :]
        w_ref[2, rows, :] = u0 * ahead[0] + u1 * ahead[2]
        w_ref[3, rows, :] = u0 * ahead[1] + u1 * ahead[3]
        if part < parts - 1:
            ahead = mat_mul(ahead, eight)

    s = grams[-1]
    left = (
        1.0 + excess[0] * s[0] + excess[1] * s[1],
        excess[0] * s[1] + excess[1] * s[2],
        excess[1] * s[0] + excess[2] * s[1],
        1.0 + excess[1] * s[1] + excess[2] * s[2],
    )
    determ = 1.0 / (left[0] * left[3] - left[1] * left[2])
    start = mat_mul((left[3], -left[1], -left[2], left[0]), full(excess))
    start = tuple(x * determ for x in start)
    block_squares, block_grams = squares[local:-1], grams[local:-1]
    mine = jnp.full(tile, me, jnp.int32)
    to_me = power(block_squares, mine, zero)
    rest = full(gramian(block_squares, block_grams, blocks - 1 - mine, zero))
    to_state = mat_mul(to_me, start)
    to_adjoint = mat_mul(mat_mul(rest, mat_mul(to_me, block_squares[0])), start)
    for group in range(g_ref.shape[1] // SUB):
        rows = row + group * SUB
        kind = rows & 3
        line = rows >> 2
        span = jnp.where(line < 4, 1, jnp.left_shift(1, jnp.maximum(line - 2, 0)))
        near_me = mine ^ jnp.where(line < 4, line, span)
        front = jnp.minimum((near_me // span) * span, blocks - 1)
        back = jnp.minimum(front + span - 1, blocks - 1)
        before, after = back < me, front > me
        gap = jnp.where(before, me - 1 - back, jnp.where(after, front - 1 - me, 0))
        reach = jnp.where(before, me - back, jnp.where(after, back - me, 0))
        near = power(block_squares, gap, zero)
        far = power(block_squares, reach, zero)
        origin = mat_trans(power(block_squares, front, zero))
        left_over = full(gramian(block_squares, block_grams, blocks - 1 - back, zero))
        end = mat_trans(mat_mul(power(block_squares, back, zero), block_squares[0]))
        first = mat_mul(end, left_over)
        state_b = mat_sub(mat_pick(before, near, (zero,) * 4), mat_mul(to_state, first))
        state_l = mat_mul(to_state, origin)
        cross = mat_pick(after, mat_mul(mat_trans(far), left_over), mat_mul(rest, far))
        adjoint_b = mat_sub(mat_mul(to_adjoint, first), cross)
        adjoint_l = mat_sub(
            mat_pick(after, mat_trans(near), (zero,) * 4), mat_mul(to_adjoint, origin)
        )
        place = pl.ds(group * SUB, SUB)
        for output, (from_b, from_l) in enumerate(
            ((adjoint_b[:2], adjoint_l[:2]), (adjoint_b[2:], adjoint_l[2:]),
             (state_b[:2], state_l[:2]), (state_b[2:], state_l[2:]))
        ):
            g_ref[output, place, :] = jnp.where(
                kind < 2,
                jnp.where(kind == 0, from_b[0], from_b[1]),
                jnp.where(kind == 2, from_l[0], from_l[1]),
            )
    for copy in copies[2:]:
        copy.wait()


def rotate_kernel(first, place_ref, *refs):
    pieces, others = first
    obs_refs, (basis_ref, *refs) = refs[: len(pieces)], refs[len(pieces) :]
    depth = obs_refs[0].shape[1]
    z = None if others is None else refs[0][...]
    for piece, obs_ref in zip(pieces, obs_refs):
        begin = pl.multiple_of((place_ref[0] ^ piece) * depth, depth)
        term = jnp.dot(
            obs_ref[...], basis_ref[pl.ds(begin, depth), :], preferred_element_type=F32
        )
        z = term if z is None else z + term
    if others is None:
        refs[0][...] = z
        return
    _, w_ref, z_ref, sum_ref = refs
    z_ref[...] = z
    for line in range(4):
        sum_ref[line : line + 1, :] = jnp.sum(w_ref[line] * z, axis=0, keepdims=True)


def merge(level, me, own, other, merge_ref):
    lower = jnp.full(own.shape, (me >> level) & 1, jnp.int32) == 0
    left, right = jnp.where(lower, own, other), jnp.where(lower, other, own)
    f00, f01, f10, f11, s00, s01, s11 = (
        merge_ref[7 * level + k : 7 * level + k + 1, :] for k in range(7)
    )
    b0, b1 = left[0:1, :], left[1:2, :]
    a0 = right[2:3, :] - s00 * b0 - s01 * b1
    a1 = right[3:4, :] - s01 * b0 - s11 * b1
    return jnp.concatenate(
        (
            right[0:1, :] + f00 * b0 + f01 * b1,
            right[1:2, :] + f10 * b0 + f11 * b1,
            left[2:3, :] + f00 * a0 + f10 * a1,
            left[3:4, :] + f01 * a0 + f11 * a1,
        ),
        axis=0,
    )


def merge_kernel(level, me_ref, merge_ref, *refs):
    *parts, out_ref = refs
    me = me_ref[0]
    parts = [ref[...] for ref in parts]
    if level:
        out_ref[...] = merge(level, me, parts[0], parts[1], merge_ref)
    else:
        near = merge(0, me, parts[0], parts[1], merge_ref)
        far = merge(0, me, parts[2], parts[3], merge_ref)
        out_ref[...] = merge(1, me, near, far, merge_ref)


def shift(value, by):
    rows = value.shape[0]
    row = lax.broadcasted_iota(jnp.int32, value.shape, 0)
    keep = row >= by if by > 0 else row < rows + by
    return jnp.where(keep, pltpu.roll(value, by % rows, 0), 0.0)


def local_kernel(z_ref, const_ref, r_ref, scratch):
    steps, width = z_ref.shape
    span = steps // SUB
    lanes = 128
    for chunk in range(width // lanes):
        cols = pl.ds(chunk * lanes, lanes)
        scratch[chunk] = z_ref[:, cols]
    for chunk in range(width // lanes):
        cols = pl.ds(chunk * lanes, lanes)
        const = [const_ref[k, :, cols] for k in range(19)]
        f, (k0, k1, inverse) = const[0:4], const[4:7]
        jumps = (const[7:11], const[11:15], const[15:19])
        zero = jnp.zeros((SUB, lanes), F32)
        x0, x1 = zero, zero
        vs = []
        for t in range(span):
            z = scratch[chunk, pl.ds(t, SUB, stride=span), :]
            vs.append(z - x0)
            x0, x1 = f[0] * x0 + f[1] * x1 + k0 * z, f[2] * x0 + f[3] * x1 + k1 * z
        for level, jump in enumerate(jumps):
            s0, s1 = shift(x0, 1 << level), shift(x1, 1 << level)
            x0, x1 = x0 + jump[0] * s0 + jump[1] * s1, x1 + jump[2] * s0 + jump[3] * s1
        x0, x1 = shift(x0, 1), shift(x1, 1)
        for t in range(span):
            vs[t] = (vs[t] - x0) * inverse
            x0, x1 = f[0] * x0 + f[1] * x1, f[2] * x0 + f[3] * x1
        a0, a1 = zero, zero
        for t in range(span - 1, -1, -1):
            a0, a1 = f[0] * a0 + f[2] * a1 + vs[t], f[1] * a0 + f[3] * a1
        for level, jump in enumerate(jumps):
            s0, s1 = shift(a0, -(1 << level)), shift(a1, -(1 << level))
            a0, a1 = a0 + jump[0] * s0 + jump[2] * s1, a1 + jump[1] * s0 + jump[3] * s1
        a0, a1 = shift(a0, -1), shift(a1, -1)
        for t in range(span - 1, -1, -1):
            r = vs[t] - k0 * a0 - k1 * a1
            a0, a1 = f[0] * a0 + f[2] * a1 + vs[t], f[1] * a0 + f[3] * a1
            scratch[chunk, pl.ds(t, SUB, stride=span), :] = r
        r_ref[:, cols] = scratch[chunk]


def rotate_back(residual, pieces, place_ref, basis_ref, outs):
    depth = outs[0].shape[1]
    for piece, out_ref in zip(pieces, outs):
        begin = pl.multiple_of((place_ref[0] ^ piece) * depth, depth)
        out_ref[...] = lax.dot_general(
            residual,
            basis_ref[pl.ds(begin, depth), :],
            (((1,), (1,)), ((), ())),
            preferred_element_type=F32,
        ).astype(out_ref.dtype)


def finish_kernel(pieces, place_ref, r_ref, w_ref, g_ref, const_ref, basis_ref, *refs):
    *sums, residual_ref = refs[: -len(pieces)]
    value = r_ref[...]
    for line in range(4):
        total = None
        for place, sum_ref in enumerate(sums):
            term = g_ref[line, pl.ds(4 * place, 4), :] * sum_ref[...]
            total = term if total is None else total + term
        value = value - w_ref[line] * jnp.sum(total, axis=0, keepdims=True)
    scale = const_ref[19, 0:1, :]
    residual = (value * scale).astype(jnp.bfloat16)
    residual_ref[...] = residual
    rotate_back(residual, pieces, place_ref, basis_ref, refs[-len(pieces) :])


def rest_kernel(pieces, place_ref, residual_ref, basis_ref, *outs):
    rotate_back(residual_ref[...], pieces, place_ref, basis_ref, outs)


def exchange(value, axis, count):
    out = [value]
    for step in range(1, count):
        out.append(lax.ppermute(value, axis, [(a, a ^ step) for a in range(count)]))
    return out


def shards(observations, basis, eigvals, lengths, noise):
    steps, depth = observations.shape
    width = basis.shape[1]
    blocks, pieces = lax.axis_size("tm"), lax.axis_size("mode")
    me = lax.axis_index("tm").astype(jnp.int32).reshape(1)
    place = lax.axis_index("mode").astype(jnp.int32).reshape(1)
    rounds = blocks.bit_length() - 1
    vmem = pl.BlockSpec(memory_space=pltpu.VMEM)
    smem = pl.BlockSpec(memory_space=pltpu.SMEM)
    params = pltpu.CompilerParams(vmem_limit_bytes=VMEM_LIMIT)

    def shape(*dims, dtype=F32):
        return jax.ShapeDtypeStruct(dims, dtype)

    obs = exchange(observations, "mode", pieces)
    const, w, g, merges, basis, obs[0] = pl.pallas_call(
        functools.partial(coefficients_kernel, blocks),
        out_shape=(
            shape(20, SUB, width),
            shape(4, steps, width),
            shape(4, -(-4 * (rounds + 2) // SUB) * SUB, width),
            shape(-(-7 * rounds // SUB) * SUB, width),
            shape(*basis.shape, dtype=basis.dtype),
            shape(steps, depth, dtype=observations.dtype),
        ),
        in_specs=[smem] * 2 + [pl.BlockSpec(memory_space=pltpu.HBM)] * 4,
        out_specs=(vmem,) * 6,
        scratch_shapes=[
            pltpu.VMEM((1, width), F32),
            pltpu.VMEM((1, width), F32),
            pltpu.SemaphoreType.DMA((4,)),
        ],
        compiler_params=params,
        cost_estimate=pl.CostEstimate(flops=20000000, bytes_accessed=2000000, transcendentals=0),
        name="coefficients",
    )(
        me,
        noise,
        *(
            pltpu.with_memory_space_constraint(x, pltpu.HBM)
            for x in (
                eigvals.reshape(1, width),
                lengths.reshape(1, width),
                observations,
                basis,
            )
        ),
    )
    last = pieces - 1
    early = [0, *range(2, last), 1]
    z = pl.pallas_call(
        functools.partial(rotate_kernel, (early, None)),
        out_shape=shape(steps, width),
        in_specs=[smem] + [vmem] * pieces,
        out_specs=vmem,
        compiler_params=params,
        name="rotate_early",
    )(place, *(obs[piece] for piece in early), basis)
    z, summary = pl.pallas_call(
        functools.partial(rotate_kernel, ([last], early)),
        out_shape=(shape(steps, width), shape(4, width)),
        in_specs=[smem] + [vmem] * 4,
        out_specs=(vmem,) * 2,
        compiler_params=params,
        name="rotate_last",
    )(place, obs[last], basis, z, w)
    sums = [summary]
    for step in range(1, 4):
        sums.append(lax.ppermute(summary, "tm", [(a, a ^ step) for a in range(blocks)]))
    for level in range(2, rounds):
        summary = pl.pallas_call(
            functools.partial(merge_kernel, 0 if level == 2 else level - 1),
            out_shape=shape(4, width),
            in_specs=[smem] + [vmem] * (5 if level == 2 else 3),
            out_specs=vmem,
            compiler_params=params,
            name="merge",
        )(me, merges, *(sums if level == 2 else (summary, sums[-1])))
        step = 1 << level
        sums.append(lax.ppermute(summary, "tm", [(a, a ^ step) for a in range(blocks)]))
    local = pl.pallas_call(
        local_kernel,
        out_shape=shape(steps, width),
        in_specs=[vmem] * 2,
        out_specs=vmem,
        scratch_shapes=[pltpu.VMEM((width // 128, steps, 128), F32)],
        compiler_params=params,
        cost_estimate=pl.CostEstimate(flops=10000000, bytes_accessed=1000000, transcendentals=0),
        name="local",
    )(z, const)
    far = list(range(2, pieces)) + [1]
    near = [0]
    residual, *parts = pl.pallas_call(
        functools.partial(finish_kernel, far),
        out_shape=(shape(steps, width, dtype=jnp.bfloat16),)
        + (shape(steps, depth, dtype=jnp.bfloat16),) * len(far),
        in_specs=[smem] + [vmem] * (5 + len(sums)),
        out_specs=(vmem,) * (1 + len(far)),
        compiler_params=params,
        name="finish",
    )(place, local, w, g, const, basis, *sums)
    arrived = [
        lax.ppermute(part, "mode", [(a, a ^ piece) for a in range(pieces)])
        for piece, part in zip(far, parts)
    ]
    grad_obs = pl.pallas_call(
        functools.partial(rest_kernel, near),
        out_shape=shape(steps, depth),
        in_specs=[smem] + [vmem] * 2,
        out_specs=vmem,
        compiler_params=params,
        cost_estimate=pl.CostEstimate(flops=80000000, bytes_accessed=1500000, transcendentals=0),
        name="rest",
    )(place, residual, basis)
    for part in arrived:
        grad_obs = grad_obs + part.astype(F32)
    return grad_obs


def solution(mesh):
    placed = (P("tm", "mode"), P(None, "mode"), P("mode"), P("mode"), P())
    return jax.shard_map(
        shards, mesh=mesh, in_specs=placed, out_specs=P("tm", "mode"), check_vma=False
    )
```

profile of v0, /device:TPU:0, one launch (start us, length us, event | category | flops | bytes accessed | tf_op | source)
XLA Modules:
  0.0 26.8 jit_solution(17993164890390200687)
XLA Ops:
  0.0 3.0 %collective-permute-start.1 = (bf16[64,512]{1,0:T(8,128)(2,1)}, bf16[64,512]{1,0:T(8,128)(2,1)S(1)}, u32[]{:S(2)}, u32[]{:S(2)}) collective-permute-start(bf16[64,512]{1,0:T(8,128)(2,1)} %refs_2_.1), channel_id=1, source_target_pairs={{0,2},{1,3},{2,0},{3,1},{4,6},{5,7},{6,4},{7,5},{8,10},{9,11},{10,... | collective-permute-start | bytes 196616 | tf_op jit(solution)/shard_map/ppermute | solution.py:374
  3.0 0.0 collective-permute-start.2
  3.0 0.1 collective-permute-start
  3.7 2.5 %coefficients.1 = (f32[20,8,512]{2,1,0:T(8,128)S(1)}, f32[4,64,512]{2,1,0:T(8,128)S(1)}, f32[4,24,512]{2,1,0:T(8,128)S(1)}, f32[24,512]{1,0:T(8,128)S(1)}, bf16[...) custom-call(s32[1]{0:T(128)} %bitcast.1.me_ref, f32[1]{0:T(128)S(6)} %copy.6.noise_ref, f32[1,512]{1,0:T(1,128)} %bitcast.4, ...), custom_call_target="tpu_custom_call" | custom-call | flops 20000000 | bytes 2000000 | tf_op jit(solution)/shard_map/coefficients/pallas_call | solution.py:393
  6.2 0.0 collective-permute-done.1.refs_1_
  6.2 0.0 collective-permute-done.2.refs_2_
  6.2 0.4 %rotate_early.1.refs_2_ = f32[64,512]{1,0:T(8,128)S(1)} custom-call(s32[1]{0:T(128)} %bitcast.place_ref, bf16[64,512]{1,0:T(8,128)(2,1)S(1)} %get-tuple-element.18.refs_0_, bf16[64,512]{1,0:T(8,128)(2,1)S(1)} %collective-permute-done.1.refs_1_, bf16[64,512]{1,0:T(8,128)(2,1)S(1)} %collective-permute-done.2.refs_2_, ...), custom_call_target="tpu_custom_call" | custom-call | tf_op jit(solution)/shard_map/rotate_early/pallas_call | solution.py:428
  6.6 0.3 %collective-permute-done.refs_0_ = bf16[64,512]{1,0:T(8,128)(2,1)S(1)} collective-permute-done((bf16[64,512]{1,0:T(8,128)(2,1)}, bf16[64,512]{1,0:T(8,128)(2,1)S(1)}, u32[]{:S(2)}, u32[]{:S(2)}) %collective-permute-start) | collective-permute-done | bytes 65568 | tf_op jit(solution)/shard_map/ppermute | solution.py:374
  6.9 0.2 rotate_last.1
  7.2 1.8 %collective-permute-start.3 = (f32[4,512]{1,0:T(4,128)S(1)}, f32[4,512]{1,0:T(4,128)S(1)}, u32[]{:S(2)}, u32[]{:S(2)}) collective-permute-start(f32[4,512]{1,0:T(4,128)S(1)} %get-tuple-element.23.refs_0_), channel_id=1, source_target_pairs={{0,4},{4,0},{8,12},{12,8},{16,20},{20,16},{24,28},{28,24},{1,5},{5... | collective-permute-start | bytes 24584 | tf_op jit(solution)/shard_map/ppermute | solution.py:446
  9.0 1.6 %collective-permute-start.4 = (f32[4,512]{1,0:T(4,128)S(1)}, f32[4,512]{1,0:T(4,128)S(1)}, u32[]{:S(2)}, u32[]{:S(2)}) collective-permute-start(f32[4,512]{1,0:T(4,128)S(1)} %get-tuple-element.23.refs_0_), channel_id=1, source_target_pairs={{0,8},{4,12},{8,0},{12,4},{16,24},{20,28},{24,16},{28,20},{1,9},{5... | collective-permute-start | bytes 24584 | tf_op jit(solution)/shard_map/ppermute | solution.py:446
  10.5 0.2 collective-permute-start.5
  10.7 0.2 collective-permute-done.3.refs_1_
  10.9 1.7 %collective-permute-done.4.refs_2_ = f32[4,512]{1,0:T(4,128)S(1)} collective-permute-done((f32[4,512]{1,0:T(4,128)S(1)}, f32[4,512]{1,0:T(4,128)S(1)}, u32[]{:S(2)}, u32[]{:S(2)}) %collective-permute-start.4) | collective-permute-done | bytes 8224 | tf_op jit(solution)/shard_map/ppermute | solution.py:446
  12.6 2.5 %collective-permute-done.5.refs_3_ = f32[4,512]{1,0:T(4,128)S(1)} collective-permute-done((f32[4,512]{1,0:T(4,128)S(1)}, f32[4,512]{1,0:T(4,128)S(1)}, u32[]{:S(2)}, u32[]{:S(2)}) %collective-permute-start.5) | collective-permute-done | bytes 8224 | tf_op jit(solution)/shard_map/ppermute | solution.py:446
  15.1 0.1 merge.1
  15.2 2.7 %collective-permute-start.6 = (f32[4,512]{1,0:T(4,128)S(1)}, f32[4,512]{1,0:T(4,128)S(1)}, u32[]{:S(2)}, u32[]{:S(2)}) collective-permute-start(f32[4,512]{1,0:T(4,128)S(1)} %merge.1), channel_id=1, source_target_pairs={{0,16},{4,20},{8,24},{12,28},{16,0},{20,4},{24,8},{28,12},{1,17},{... | collective-permute-start | bytes 24584 | tf_op jit(solution)/shard_map/ppermute | solution.py:457
  17.8 0.3 %local.1.r_ref = f32[64,512]{1,0:T(8,128)S(1)} custom-call(f32[64,512]{1,0:T(8,128)S(1)} %get-tuple-element.20.z_ref, f32[20,8,512]{2,1,0:T(8,128)S(1)} %get-tuple-element.21.const_ref), custom_call_target="tpu_custom_call" | custom-call | flops 10000000 | bytes 1000000 | tf_op jit(solution)/shard_map/local/pallas_call | solution.py:458
  18.1 1.7 %collective-permute-done.6.refs_4_ = f32[4,512]{1,0:T(4,128)S(1)} collective-permute-done((f32[4,512]{1,0:T(4,128)S(1)}, f32[4,512]{1,0:T(4,128)S(1)}, u32[]{:S(2)}, u32[]{:S(2)}) %collective-permute-start.6) | collective-permute-done | bytes 8224 | tf_op jit(solution)/shard_map/ppermute | solution.py:457
  19.8 0.6 %finish.1 = (bf16[64,512]{1,0:T(8,128)(2,1)S(1)}, bf16[64,512]{1,0:T(8,128)(2,1)S(1)}, bf16[64,512]{1,0:T(8,128)(2,1)S(1)}, bf16[64,512]{1,0:T(8,128)(2,1)S(1)}) custom-call(s32[1]{0:T(128)} %bitcast.place_ref, f32[64,512]{1,0:T(8,128)S(1)} %local.1.r_ref, f32[4,64,512]{2,1,0:T(8,128)S(1)} %get-tuple-element.19.refs_3_.w_ref, ...), custom_call_target="tpu_custom_call" | custom-call | tf_op jit(solution)/shard_map/finish/pallas_call | solution.py:470
  20.4 1.6 %collective-permute-start.7 = (bf16[64,512]{1,0:T(8,128)(2,1)S(1)}, bf16[64,512]{1,0:T(8,128)(2,1)S(1)}, u32[]{:S(2)}, u32[]{:S(2)}) collective-permute-start(bf16[64,512]{1,0:T(8,128)(2,1)S(1)} %get-tuple-element.26), channel_id=1, source_target_pairs={{0,2},{1,3},{2,0},{3,1},{4,6},{5,7},{6,4},{7,5},{8,10},{9,11},{10,... | collective-permute-start | bytes 196616 | tf_op jit(solution)/shard_map/ppermute | solution.py:480
  22.0 0.0 collective-permute-start.8
  22.0 0.6 %collective-permute-start.9 = (bf16[64,512]{1,0:T(8,128)(2,1)S(1)}, bf16[64,512]{1,0:T(8,128)(2,1)S(1)}, u32[]{:S(2)}, u32[]{:S(2)}) collective-permute-start(bf16[64,512]{1,0:T(8,128)(2,1)S(1)} %get-tuple-element.28), channel_id=1, source_target_pairs={{0,1},{1,0},{2,3},{3,2},{4,5},{5,4},{6,7},{7,6},{8,9},{9,8},{10,11... | collective-permute-start | bytes 196616 | tf_op jit(solution)/shard_map/ppermute | solution.py:480
  22.6 0.3 %rest.1 = f32[64,512]{1,0:T(8,128)S(1)} custom-call(s32[1]{0:T(128)} %bitcast.place_ref, bf16[64,512]{1,0:T(8,128)(2,1)S(1)} %get-tuple-element.25.residual_ref, bf16[2048,512]{1,0:T(8,128)(2,1)S(1)} %get-tuple-element.17.refs_3_.refs_1_.basis_ref), custom_call_target="tpu_custom_call" | custom-call | flops 80000000 | bytes 1500000 | tf_op jit(solution)/shard_map/rest/pallas_call | solution.py:483
  22.9 1.8 %collective-permute-done.7 = bf16[64,512]{1,0:T(8,128)(2,1)S(1)} collective-permute-done((bf16[64,512]{1,0:T(8,128)(2,1)S(1)}, bf16[64,512]{1,0:T(8,128)(2,1)S(1)}, u32[]{:S(2)}, u32[]{:S(2)}) %collective-permute-start.7) | collective-permute-done | bytes 65568 | tf_op jit(solution)/shard_map/ppermute | solution.py:480
  24.7 1.4 %collective-permute-done.8 = bf16[64,512]{1,0:T(8,128)(2,1)S(1)} collective-permute-done((bf16[64,512]{1,0:T(8,128)(2,1)S(1)}, bf16[64,512]{1,0:T(8,128)(2,1)S(1)}, u32[]{:S(2)}, u32[]{:S(2)}) %collective-permute-start.8) | collective-permute-done | bytes 65568 | tf_op jit(solution)/shard_map/ppermute | solution.py:480
  26.1 0.0 collective-permute-done.9
  26.1 0.7 %convert_add_fusion = f32[64,512]{1,0:T(8,128)} fusion(bf16[64,512]{1,0:T(8,128)(2,1)S(1)} %collective-permute-done.9, bf16[64,512]{1,0:T(8,128)(2,1)S(1)} %collective-permute-done.8, f32[64,512]{1,0:T(8,128)S(1)} %rest.1, bf16[64,512]{1,0:T(8,128)(2,1)S(1)} %collective-permute-done.7), kind=kLoop, calls=%fused_computation | loop fusion | flops 196608 | bytes 458752 | tf_op jit(solution)/shard_map/add | solution.py:493
Async XLA Ops:
  0.0 6.2 %collective-permute-start.1 = (bf16[64,512]{1,0:T(8,128)(2,1)}, bf16[64,512]{1,0:T(8,128)(2,1)S(1)}, u32[]{:S(2)}, u32[]{:S(2)}) collective-permute-start(bf16[64,512]{1,0:T(8,128)(2,1)} %refs_2_.1), channel_id=1, source_target_pairs={{0,2},{1,3},{2,0},{3,1},{4,6},{5,7},{6,4},{7,5},{8,10},{9,11},{10,... | collective-permute-start | bytes 196616 | tf_op jit(solution)/shard_map/ppermute | solution.py:374
  3.0 3.3 %collective-permute-start.2 = (bf16[64,512]{1,0:T(8,128)(2,1)}, bf16[64,512]{1,0:T(8,128)(2,1)S(1)}, u32[]{:S(2)}, u32[]{:S(2)}) collective-permute-start(bf16[64,512]{1,0:T(8,128)(2,1)} %refs_2_.1), channel_id=1, source_target_pairs={{0,1},{1,0},{2,3},{3,2},{4,5},{5,4},{6,7},{7,6},{8,9},{9,8},{10,11... | collective-permute-start | bytes 196616 | tf_op jit(solution)/shard_map/ppermute | solution.py:374
  3.0 4.0 %collective-permute-start = (bf16[64,512]{1,0:T(8,128)(2,1)}, bf16[64,512]{1,0:T(8,128)(2,1)S(1)}, u32[]{:S(2)}, u32[]{:S(2)}) collective-permute-start(bf16[64,512]{1,0:T(8,128)(2,1)} %refs_2_.1), channel_id=1, source_target_pairs={{0,3},{1,2},{2,1},{3,0},{4,7},{5,6},{6,5},{7,4},{8,11},{9,10},{10,... | collective-permute-start | bytes 196616 | tf_op jit(solution)/shard_map/ppermute | solution.py:374
  7.2 3.7 %collective-permute-start.3 = (f32[4,512]{1,0:T(4,128)S(1)}, f32[4,512]{1,0:T(4,128)S(1)}, u32[]{:S(2)}, u32[]{:S(2)}) collective-permute-start(f32[4,512]{1,0:T(4,128)S(1)} %get-tuple-element.23.refs_0_), channel_id=1, source_target_pairs={{0,4},{4,0},{8,12},{12,8},{16,20},{20,16},{24,28},{28,24},{1,5},{5... | collective-permute-start | bytes 24584 | tf_op jit(solution)/shard_map/ppermute | solution.py:446
  9.0 3.7 %collective-permute-start.4 = (f32[4,512]{1,0:T(4,128)S(1)}, f32[4,512]{1,0:T(4,128)S(1)}, u32[]{:S(2)}, u32[]{:S(2)}) collective-permute-start(f32[4,512]{1,0:T(4,128)S(1)} %get-tuple-element.23.refs_0_), channel_id=1, source_target_pairs={{0,8},{4,12},{8,0},{12,4},{16,24},{20,28},{24,16},{28,20},{1,9},{5... | collective-permute-start | bytes 24584 | tf_op jit(solution)/shard_map/ppermute | solution.py:446
  10.5 4.5 %collective-permute-start.5 = (f32[4,512]{1,0:T(4,128)S(1)}, f32[4,512]{1,0:T(4,128)S(1)}, u32[]{:S(2)}, u32[]{:S(2)}) collective-permute-start(f32[4,512]{1,0:T(4,128)S(1)} %get-tuple-element.23.refs_0_), channel_id=1, source_target_pairs={{0,12},{4,8},{8,4},{12,0},{16,28},{20,24},{24,20},{28,16},{1,13},{... | collective-permute-start | bytes 24584 | tf_op jit(solution)/shard_map/ppermute | solution.py:446
  15.2 4.6 %collective-permute-start.6 = (f32[4,512]{1,0:T(4,128)S(1)}, f32[4,512]{1,0:T(4,128)S(1)}, u32[]{:S(2)}, u32[]{:S(2)}) collective-permute-start(f32[4,512]{1,0:T(4,128)S(1)} %merge.1), channel_id=1, source_target_pairs={{0,16},{4,20},{8,24},{12,28},{16,0},{20,4},{24,8},{28,12},{1,17},{... | collective-permute-start | bytes 24584 | tf_op jit(solution)/shard_map/ppermute | solution.py:457
  20.4 4.3 %collective-permute-start.7 = (bf16[64,512]{1,0:T(8,128)(2,1)S(1)}, bf16[64,512]{1,0:T(8,128)(2,1)S(1)}, u32[]{:S(2)}, u32[]{:S(2)}) collective-permute-start(bf16[64,512]{1,0:T(8,128)(2,1)S(1)} %get-tuple-element.26), channel_id=1, source_target_pairs={{0,2},{1,3},{2,0},{3,1},{4,6},{5,7},{6,4},{7,5},{8,10},{9,11},{10,... | collective-permute-start | bytes 196616 | tf_op jit(solution)/shard_map/ppermute | solution.py:480
  22.0 4.2 %collective-permute-start.8 = (bf16[64,512]{1,0:T(8,128)(2,1)S(1)}, bf16[64,512]{1,0:T(8,128)(2,1)S(1)}, u32[]{:S(2)}, u32[]{:S(2)}) collective-permute-start(bf16[64,512]{1,0:T(8,128)(2,1)S(1)} %get-tuple-element.27), channel_id=1, source_target_pairs={{0,3},{1,2},{2,1},{3,0},{4,7},{5,6},{6,5},{7,4},{8,11},{9,10},{10,... | collective-permute-start | bytes 196616 | tf_op jit(solution)/shard_map/ppermute | solution.py:480
  22.0 4.2 %collective-permute-start.9 = (bf16[64,512]{1,0:T(8,128)(2,1)S(1)}, bf16[64,512]{1,0:T(8,128)(2,1)S(1)}, u32[]{:S(2)}, u32[]{:S(2)}) collective-permute-start(bf16[64,512]{1,0:T(8,128)(2,1)S(1)} %get-tuple-element.28), channel_id=1, source_target_pairs={{0,1},{1,0},{2,3},{3,2},{4,5},{5,4},{6,7},{7,6},{8,9},{9,8},{10,11... | collective-permute-start | bytes 196616 | tf_op jit(solution)/shard_map/ppermute | solution.py:480
where the time goes:
time: 27 us; the launch traced here: 26.8 us
  starting transfers between devices  11.5 us (43%)
  waiting for transfers between devices  9.57 us (35%)
  Pallas kernels  4.33 us (16%)
  between operations  0.71 us (3%)
  other arithmetic  0.69 us (3%)
    ppermute x4, starting transfers between devices, shards(): lax.ppermute(summary, 'tm', [(a, a ^ step) for a in range(blocks)])  6.22 us
    ppermute x4, waiting for transfers between devices, shards(): lax.ppermute(summary, 'tm', [(a, a ^ step) for a in range(blocks)])  6.02 us
    ppermute x3, waiting for transfers between devices, shards(): lax.ppermute(part, 'mode', [(a, a ^ piece) for a in range(pieces)])  3.25 us
    ppermute x3, starting transfers between devices, exchange(): out.append(lax.ppermute(value, axis, [(a, a ^ step) for a in range(count)]))  3.08 us
    pallas_call x1, Pallas kernels, shards(): pl.pallas_call(functools.partial(coefficients_kernel, blocks), out_shape=...  2.48 us
    ppermute x3, starting transfers between devices, shards(): lax.ppermute(part, 'mode', [(a, a ^ piece) for a in range(pieces)])  2.21 us
    add x1, other arithmetic, shards(): grad_obs = grad_obs + part.astype(F32)  0.69 us
    pallas_call x1, Pallas kernels, shards(): pl.pallas_call(functools.partial(finish_kernel, far), out_shape=(shape(st...  0.6 us
  transfers between devices with their start and end apart: 10, of which 7 were waited for; matrix products, arithmetic and copies ran while one was open for 0% of the time, Pallas kernels for 13%

commit v1 on v0

--- a/solution.py
+++ b/solution.py
@@ -117,17 +117,13 @@
     return closed, gain0, gain1, inverse, (rho - p00, -p01, rho - p11)
 
 
-def coefficients_kernel(blocks, me_ref, noise_ref, *refs):
-    arguments, (const_ref, w_ref, g_ref, merge_ref, basis_ref, obs_ref) = (
-        refs[:4],
-        refs[4:10],
-    )
-    scale_ref, length_ref, sems = refs[10:]
+def coefficients_kernel(blocks, noise_ref, *refs):
+    arguments, (const_ref, w_ref, merge_ref, basis_ref, obs_ref) = refs[:4], refs[4:9]
+    scale_ref, length_ref, sems = refs[9:]
+    targets = (scale_ref, length_ref, obs_ref, basis_ref)
     copies = [
         pltpu.make_async_copy(source, target, sems.at[k])
-        for k, (source, target) in enumerate(
-            zip(arguments, (scale_ref, length_ref, obs_ref, basis_ref))
-        )
+        for k, (source, target) in enumerate(zip(arguments, targets))
     ]
     for copy in copies:
         copy.start()
@@ -136,7 +132,6 @@
     steps = w_ref.shape[1]
     width = scale_ref.shape[1]
     tile = (SUB, width)
-    me = me_ref[0]
     scale2 = jnp.broadcast_to(scale_ref[...], tile)
     length = jnp.broadcast_to(length_ref[...], tile)
     noise_var = jnp.full(tile, noise_ref[0], F32)
@@ -154,9 +149,11 @@
     for place, value in enumerate(consts):
         const_ref[place] = value
     const_ref[len(consts)] = -1.0 / noise_var
-    for level in range(blocks.bit_length() - 1):
-        for place, value in enumerate(squares[local + level] + grams[local + level]):
-            merge_ref[7 * level + place : 7 * level + place + 1, :] = value[0:1, :]
+    rounds = blocks.bit_length() - 1
+    groups = squares[local:-1] + [()], grams[local:], [()] * rounds + [excess]
+    values = [value for group in zip(*groups) for part in group for value in part]
+    for place, value in enumerate(values):
+        merge_ref[place : place + 1, :] = value[0:1, :]
 
     row = lax.broadcasted_iota(jnp.int32, tile, 0)
     small, gram_small = squares[:3], grams[:3]
@@ -184,7 +181,80 @@
         if part < parts - 1:
             ahead = mat_mul(ahead, eight)
 
-    s = grams[-1]
+    for copy in copies[2:]:
+        copy.wait()
+
+
+def rotate_kernel(first, place_ref, *refs):
+    pieces, others = first
+    obs_refs, (basis_ref, *refs) = refs[: len(pieces)], refs[len(pieces) :]
+    depth = obs_refs[0].shape[1]
+    z = None if others is None else refs[0][...]
+    for piece, obs_ref in zip(pieces, obs_refs):
+        begin = pl.multiple_of((place_ref[0] ^ piece) * depth, depth)
+        term = jnp.dot(
+            obs_ref[...], basis_ref[pl.ds(begin, depth), :], preferred_element_type=F32
+        )
+        z = term if z is None else z + term
+    if others is None:
+        refs[0][...] = z
+        return
+    _, w_ref, z_ref, sum_ref = refs
+    z_ref[...] = z
+    for line in range(4):
+        sum_ref[line : line + 1, :] = jnp.sum(w_ref[line] * z, axis=0, keepdims=True)
+
+
+def merge(level, me, own, other, merge_ref):
+    lower = jnp.full(own.shape, (me >> level) & 1, jnp.int32) == 0
+    left, right = jnp.where(lower, own, other), jnp.where(lower, other, own)
+    f00, f01, f10, f11, s00, s01, s11 = (
+        merge_ref[7 * level + k : 7 * level + k + 1, :] for k in range(7)
+    )
+    b0, b1 = left[0:1, :], left[1:2, :]
+    a0 = right[2:3, :] - s00 * b0 - s01 * b1
+    a1 = right[3:4, :] - s01 * b0 - s11 * b1
+    return jnp.concatenate(
+        (
+            right[0:1, :] + f00 * b0 + f01 * b1,
+            right[1:2, :] + f10 * b0 + f11 * b1,
+            left[2:3, :] + f00 * a0 + f10 * a1,
+            left[3:4, :] + f01 * a0 + f11 * a1,
+        ),
+        axis=0,
+    )
+
+
+def merge_kernel(level, me_ref, merge_ref, *refs):
+    *parts, out_ref = refs
+    me = me_ref[0]
+    parts = [ref[...] for ref in parts]
+    if level:
+        out_ref[...] = merge(level, me, parts[0], parts[1], merge_ref)
+    else:
+        near = merge(0, me, parts[0], parts[1], merge_ref)
+        far = merge(0, me, parts[2], parts[3], merge_ref)
+        out_ref[...] = merge(1, me, near, far, merge_ref)
+
+
+def shift(value, by):
+    rows = value.shape[0]
+    row = lax.broadcasted_iota(jnp.int32, value.shape, 0)
+    keep = row >= by if by > 0 else row < rows + by
+    return jnp.where(keep, pltpu.roll(value, by % rows, 0), 0.0)
+
+
+def reach(blocks, me, merge_ref, g_ref):
+    tile = (SUB, merge_ref.shape[1])
+    rounds = blocks.bit_length() - 1
+    values = [
+        jnp.broadcast_to(merge_ref[k : k + 1, :], tile) for k in range(7 * rounds + 6)
+    ]
+    block_squares = [tuple(values[7 * k : 7 * k + 4]) for k in range(rounds)]
+    block_grams = [tuple(values[7 * k + 4 : 7 * k + 7]) for k in range(rounds)]
+    s, excess = values[-6:-3], values[-3:]
+    zero = jnp.zeros(tile, F32)
+    row = lax.broadcasted_iota(jnp.int32, tile, 0)
     left = (
         1.0 + excess[0] * s[0] + excess[1] * s[1],
         excess[0] * s[1] + excess[1] * s[2],
@@ -194,7 +264,6 @@
     determ = 1.0 / (left[0] * left[3] - left[1] * left[2])
     start = mat_mul((left[3], -left[1], -left[2], left[0]), full(excess))
     start = tuple(x * determ for x in start)
-    block_squares, block_grams = squares[local:-1], grams[local:-1]
     mine = jnp.full(tile, me, jnp.int32)
     to_me = power(block_squares, mine, zero)
     rest = full(gramian(block_squares, block_grams, blocks - 1 - mine, zero))
@@ -234,70 +303,10 @@
                 jnp.where(kind == 0, from_b[0], from_b[1]),
                 jnp.where(kind == 2, from_l[0], from_l[1]),
             )
-    for copy in copies[2:]:
-        copy.wait()
-
-
-def rotate_kernel(first, place_ref, *refs):
-    pieces, others = first
-    obs_refs, (basis_ref, *refs) = refs[: len(pieces)], refs[len(pieces) :]
-    depth = obs_refs[0].shape[1]
-    z = None if others is None else refs[0][...]
-    for piece, obs_ref in zip(pieces, obs_refs):
-        begin = pl.multiple_of((place_ref[0] ^ piece) * depth, depth)
-        term = jnp.dot(
-            obs_ref[...], basis_ref[pl.ds(begin, depth), :], preferred_element_type=F32
-        )
-        z = term if z is None else z + term
-    if others is None:
-        refs[0][...] = z
-        return
-    _, w_ref, z_ref, sum_ref = refs
-    z_ref[...] = z
-    for line in range(4):
-        sum_ref[line : line + 1, :] = jnp.sum(w_ref[line] * z, axis=0, keepdims=True)
-
-
-def merge(level, me, own, other, merge_ref):
-    lower = jnp.full(own.shape, (me >> level) & 1, jnp.int32) == 0
-    left, right = jnp.where(lower, own, other), jnp.where(lower, other, own)
-    f00, f01, f10, f11, s00, s01, s11 = (
-        merge_ref[7 * level + k : 7 * level + k + 1, :] for k in range(7)
-    )
-    b0, b1 = left[0:1, :], left[1:2, :]
-    a0 = right[2:3, :] - s00 * b0 - s01 * b1
-    a1 = right[3:4, :] - s01 * b0 - s11 * b1
-    return jnp.concatenate(
-        (
-            right[0:1, :] + f00 * b0 + f01 * b1,
-            right[1:2, :] + f10 * b0 + f11 * b1,
-            left[2:3, :] + f00 * a0 + f10 * a1,
-            left[3:4, :] + f01 * a0 + f11 * a1,
-        ),
-        axis=0,
-    )
-
-
-def merge_kernel(level, me_ref, merge_ref, *refs):
-    *parts, out_ref = refs
-    me = me_ref[0]
-    parts = [ref[...] for ref in parts]
-    if level:
-        out_ref[...] = merge(level, me, parts[0], parts[1], merge_ref)
-    else:
-        near = merge(0, me, parts[0], parts[1], merge_ref)
-        far = merge(0, me, parts[2], parts[3], merge_ref)
-        out_ref[...] = merge(1, me, near, far, merge_ref)
-
-
-def shift(value, by):
-    rows = value.shape[0]
-    row = lax.broadcasted_iota(jnp.int32, value.shape, 0)
-    keep = row >= by if by > 0 else row < rows + by
-    return jnp.where(keep, pltpu.roll(value, by % rows, 0), 0.0)
-
-
-def local_kernel(z_ref, const_ref, r_ref, scratch):
+
+
+def local_kernel(blocks, me_ref, z_ref, const_ref, merge_ref, r_ref, g_ref, scratch):
+    reach(blocks, me_ref[0], merge_ref, g_ref)
     steps, width = z_ref.shape
     span = steps // SUB
     lanes = 128
@@ -390,18 +399,17 @@
         return jax.ShapeDtypeStruct(dims, dtype)
 
     obs = exchange(observations, "mode", pieces)
-    const, w, g, merges, basis, obs[0] = pl.pallas_call(
+    const, w, merges, basis, obs[0] = pl.pallas_call(
         functools.partial(coefficients_kernel, blocks),
         out_shape=(
             shape(20, SUB, width),
             shape(4, steps, width),
-            shape(4, -(-4 * (rounds + 2) // SUB) * SUB, width),
-            shape(-(-7 * rounds // SUB) * SUB, width),
+            shape(-(-(7 * rounds + 6) // SUB) * SUB, width),
             shape(*basis.shape, dtype=basis.dtype),
             shape(steps, depth, dtype=observations.dtype),
         ),
-        in_specs=[smem] * 2 + [pl.BlockSpec(memory_space=pltpu.HBM)] * 4,
-        out_specs=(vmem,) * 6,
+        in_specs=[smem] + [pl.BlockSpec(memory_space=pltpu.HBM)] * 4,
+        out_specs=(vmem,) * 5,
         scratch_shapes=[
             pltpu.VMEM((1, width), F32),
             pltpu.VMEM((1, width), F32),
@@ -411,7 +419,6 @@
         cost_estimate=pl.CostEstimate(flops=20000000, bytes_accessed=2000000, transcendentals=0),
         name="coefficients",
     )(
-        me,
         noise,
         *(
             pltpu.with_memory_space_constraint(x, pltpu.HBM)
@@ -424,7 +431,7 @@
         ),
     )
     last = pieces - 1
-    early = [0, *range(2, last), 1]
+    early = list(range(last))
     z = pl.pallas_call(
         functools.partial(rotate_kernel, (early, None)),
         out_shape=shape(steps, width),
@@ -455,16 +462,16 @@
         )(me, merges, *(sums if level == 2 else (summary, sums[-1])))
         step = 1 << level
         sums.append(lax.ppermute(summary, "tm", [(a, a ^ step) for a in range(blocks)]))
-    local = pl.pallas_call(
-        local_kernel,
-        out_shape=shape(steps, width),
-        in_specs=[vmem] * 2,
-        out_specs=vmem,
+    local, g = pl.pallas_call(
+        functools.partial(local_kernel, blocks),
+        out_shape=(shape(steps, width), shape(4, -(-4 * (rounds + 2) // SUB) * SUB, width)),
+        in_specs=[smem] + [vmem] * 3,
+        out_specs=(vmem,) * 2,
         scratch_shapes=[pltpu.VMEM((width // 128, steps, 128), F32)],
         compiler_params=params,
         cost_estimate=pl.CostEstimate(flops=10000000, bytes_accessed=1000000, transcendentals=0),
         name="local",
-    )(z, const)
+    )(me, z, const, merges)
     far = list(range(2, pieces)) + [1]
     near = [0]
     residual, *parts = pl.pallas_call(

time: 27 us -> 25.7 us (0.952)
  waiting for transfers between devices: 9.57 us -> 8.17 us
    ppermute x4, waiting for transfers between devices: 6.02 us -> 3.82 us  [shards(): lax.ppermute(summary, 'tm', [(a, a ^ step) for a in range(blocks)])]
    pallas_call x1, Pallas kernels: 0.28 us -> 1.25 us  [shards(): pl.pallas_call(functools.partial(local_kernel, blocks), out_shape=(shape(...]
    ppermute x3, waiting for transfers between devices: 0.3 us -> 1.1 us  [exchange(): out.append(lax.ppermute(value, axis, [(a, a ^ step) for a in range(count)]))]
    pallas_call x1, Pallas kernels: 2.48 us -> 1.7 us  [shards(): pl.pallas_call(functools.partial(coefficients_kernel, blocks), out_shape=...]
  transfers between devices with their start and end apart: 10 -> 10, of which waited for: 7 -> 8; matrix products, arithmetic and copies ran while one was open for 0% -> 0% of each run, Pallas kernels for 13% -> 14%
where the time goes in v1:
time: 25.7 us; the launch traced here: 25.6 us
  starting transfers between devices  11.5 us (45%)
  waiting for transfers between devices  8.17 us (32%)
  Pallas kernels  4.53 us (18%)
  other arithmetic  0.69 us (3%)
  between operations  0.69 us (3%)
    ppermute x4, starting transfers between devices, shards(): lax.ppermute(summary, 'tm', [(a, a ^ step) for a in range(blocks)])  6.21 us
    ppermute x4, waiting for transfers between devices, shards(): lax.ppermute(summary, 'tm', [(a, a ^ step) for a in range(blocks)])  3.82 us
    ppermute x3, waiting for transfers between devices, shards(): lax.ppermute(part, 'mode', [(a, a ^ piece) for a in range(pieces)])  3.25 us
    ppermute x3, starting transfers between devices, exchange(): out.append(lax.ppermute(value, axis, [(a, a ^ step) for a in range(count)]))  3.08 us
    ppermute x3, starting transfers between devices, shards(): lax.ppermute(part, 'mode', [(a, a ^ piece) for a in range(pieces)])  2.21 us
    pallas_call x1, Pallas kernels, shards(): pl.pallas_call(functools.partial(coefficients_kernel, blocks), out_shape=...  1.7 us
    pallas_call x1, Pallas kernels, shards(): pl.pallas_call(functools.partial(local_kernel, blocks), out_shape=(shape(...  1.25 us
    ppermute x3, waiting for transfers between devices, exchange(): out.append(lax.ppermute(value, axis, [(a, a ^ step) for a in range(count)]))  1.1 us
  transfers between devices with their start and end apart: 10, of which 8 were waited for; matrix products, arithmetic and copies ran while one was open for 0% of the time, Pallas kernels for 14%

profile of v1, /device:TPU:0, one launch (start us, length us, event | category | flops | bytes accessed | tf_op | source)
XLA Modules:
  0.0 25.6 jit_solution(15607417334343326361)
XLA Ops:
  0.0 3.0 %collective-permute-start.2 = (bf16[64,512]{1,0:T(8,128)(2,1)}, bf16[64,512]{1,0:T(8,128)(2,1)S(1)}, u32[]{:S(2)}, u32[]{:S(2)}) collective-permute-start(bf16[64,512]{1,0:T(8,128)(2,1)} %refs_2_.1), channel_id=1, source_target_pairs={{0,2},{1,3},{2,0},{3,1},{4,6},{5,7},{6,4},{7,5},{8,10},{9,11},{10,... | collective-permute-start | bytes 196616 | tf_op jit(solution)/shard_map/ppermute | solution.py:383
  3.0 0.0 collective-permute-start.1
  3.0 0.1 collective-permute-start
  3.7 1.7 %coefficients.1 = (f32[20,8,512]{2,1,0:T(8,128)S(1)}, f32[4,64,512]{2,1,0:T(8,128)S(1)}, f32[32,512]{1,0:T(8,128)S(1)}, bf16[2048,512]{1,0:T(8,128)(2,1)S(1)}, bf16[64,512]{1,0:T(8,128)(2,1)S(1)}) custom-call(f32[1]{0:T(128)S(6)} %copy.6.noise_ref, f32[1,512]{1,0:T(1,128)} %bitcast.4, f32[1,512]{1,0:T(1,128)} %bitcast.5, bf16[64,512]{1,0:T(8,128)(2,1)} %refs_2_.1, ...), custom_call_target="tpu_custom_call" | custom-call | flops 20000000 | bytes 2000000 | tf_op jit(solution)/shard_map/coefficients/pallas_call | solution.py:402
  5.4 0.1 collective-permute-done.2.refs_2_
  5.6 0.0 collective-permute-done.1.refs_1_
  5.6 0.4 %rotate_early.1.refs_2_ = f32[64,512]{1,0:T(8,128)S(1)} custom-call(s32[1]{0:T(128)} %bitcast.place_ref, bf16[64,512]{1,0:T(8,128)(2,1)S(1)} %get-tuple-element.19.refs_0_, bf16[64,512]{1,0:T(8,128)(2,1)S(1)} %collective-permute-done.1.refs_1_, bf16[64,512]{1,0:T(8,128)(2,1)S(1)} %collective-permute-done.2.refs_2_, ...), custom_call_target="tpu_custom_call" | custom-call | tf_op jit(solution)/shard_map/rotate_early/pallas_call | solution.py:435
  6.0 0.9 %collective-permute-done.refs_0_ = bf16[64,512]{1,0:T(8,128)(2,1)S(1)} collective-permute-done((bf16[64,512]{1,0:T(8,128)(2,1)}, bf16[64,512]{1,0:T(8,128)(2,1)S(1)}, u32[]{:S(2)}, u32[]{:S(2)}) %collective-permute-start) | collective-permute-done | bytes 65568 | tf_op jit(solution)/shard_map/ppermute | solution.py:383
  6.9 0.3 rotate_last.1
  7.2 2.6 %collective-permute-start.5 = (f32[4,512]{1,0:T(4,128)S(1)}, f32[4,512]{1,0:T(4,128)S(1)}, u32[]{:S(2)}, u32[]{:S(2)}) collective-permute-start(f32[4,512]{1,0:T(4,128)S(1)} %get-tuple-element.26.refs_0_), channel_id=1, source_target_pairs={{0,12},{4,8},{8,4},{12,0},{16,28},{20,24},{24,20},{28,16},{1,13},{... | collective-permute-start | bytes 24584 | tf_op jit(solution)/shard_map/ppermute | solution.py:453
  9.8 0.4 %collective-permute-start.4 = (f32[4,512]{1,0:T(4,128)S(1)}, f32[4,512]{1,0:T(4,128)S(1)}, u32[]{:S(2)}, u32[]{:S(2)}) collective-permute-start(f32[4,512]{1,0:T(4,128)S(1)} %get-tuple-element.26.refs_0_), channel_id=1, source_target_pairs={{0,8},{4,12},{8,0},{12,4},{16,24},{20,28},{24,16},{28,20},{1,9},{5... | collective-permute-start | bytes 24584 | tf_op jit(solution)/shard_map/ppermute | solution.py:453
  10.2 0.5 %collective-permute-start.3 = (f32[4,512]{1,0:T(4,128)S(1)}, f32[4,512]{1,0:T(4,128)S(1)}, u32[]{:S(2)}, u32[]{:S(2)}) collective-permute-start(f32[4,512]{1,0:T(4,128)S(1)} %get-tuple-element.26.refs_0_), channel_id=1, source_target_pairs={{0,4},{4,0},{8,12},{12,8},{16,20},{20,16},{24,28},{28,24},{1,5},{5... | collective-permute-start | bytes 24584 | tf_op jit(solution)/shard_map/ppermute | solution.py:453
  10.7 1.1 %collective-permute-done.5.refs_3_ = f32[4,512]{1,0:T(4,128)S(1)} collective-permute-done((f32[4,512]{1,0:T(4,128)S(1)}, f32[4,512]{1,0:T(4,128)S(1)}, u32[]{:S(2)}, u32[]{:S(2)}) %collective-permute-start.5) | collective-permute-done | bytes 8224 | tf_op jit(solution)/shard_map/ppermute | solution.py:453
  11.8 1.6 %collective-permute-done.4.refs_2_ = f32[4,512]{1,0:T(4,128)S(1)} collective-permute-done((f32[4,512]{1,0:T(4,128)S(1)}, f32[4,512]{1,0:T(4,128)S(1)}, u32[]{:S(2)}, u32[]{:S(2)}) %collective-permute-start.4) | collective-permute-done | bytes 8224 | tf_op jit(solution)/shard_map/ppermute | solution.py:453
  13.4 0.4 %collective-permute-done.3.refs_1_ = f32[4,512]{1,0:T(4,128)S(1)} collective-permute-done((f32[4,512]{1,0:T(4,128)S(1)}, f32[4,512]{1,0:T(4,128)S(1)}, u32[]{:S(2)}, u32[]{:S(2)}) %collective-permute-start.3) | collective-permute-done | bytes 8224 | tf_op jit(solution)/shard_map/ppermute | solution.py:453
  13.9 0.1 merge.1
  13.9 2.7 %collective-permute-start.6 = (f32[4,512]{1,0:T(4,128)S(1)}, f32[4,512]{1,0:T(4,128)S(1)}, u32[]{:S(2)}, u32[]{:S(2)}) collective-permute-start(f32[4,512]{1,0:T(4,128)S(1)} %merge.1), channel_id=1, source_target_pairs={{0,16},{4,20},{8,24},{12,28},{16,0},{20,4},{24,8},{28,12},{1,17},{... | collective-permute-start | bytes 24584 | tf_op jit(solution)/shard_map/ppermute | solution.py:464
  16.6 1.3 %local.1 = (f32[64,512]{1,0:T(8,128)S(1)}, f32[4,24,512]{2,1,0:T(8,128)S(1)}) custom-call(s32[1]{0:T(128)} %bitcast.1.me_ref, f32[64,512]{1,0:T(8,128)S(1)} %get-tuple-element.21.z_ref, f32[20,8,512]{2,1,0:T(8,128)S(1)} %get-tuple-element.22.const_ref, f32[32,512]{1,0:T(8,128)S(1)} %get-tuple-element.23.merge_ref), custom_call_target="tpu_custom_call" | custom-call | flops 10000000 | bytes 1000000 | tf_op jit(solution)/shard_map/local/pallas_call | solution.py:465
  17.8 0.7 %collective-permute-done.6.refs_4_ = f32[4,512]{1,0:T(4,128)S(1)} collective-permute-done((f32[4,512]{1,0:T(4,128)S(1)}, f32[4,512]{1,0:T(4,128)S(1)}, u32[]{:S(2)}, u32[]{:S(2)}) %collective-permute-start.6) | collective-permute-done | bytes 8224 | tf_op jit(solution)/shard_map/ppermute | solution.py:464
  18.5 0.6 %finish.1 = (bf16[64,512]{1,0:T(8,128)(2,1)S(1)}, bf16[64,512]{1,0:T(8,128)(2,1)S(1)}, bf16[64,512]{1,0:T(8,128)(2,1)S(1)}, bf16[64,512]{1,0:T(8,128)(2,1)S(1)}) custom-call(s32[1]{0:T(128)} %bitcast.place_ref, f32[64,512]{1,0:T(8,128)S(1)} %get-tuple-element.24.r_ref, f32[4,64,512]{2,1,0:T(8,128)S(1)} %get-tuple-element.20.refs_3_.w_ref, ...), custom_call_target="tpu_custom_call" | custom-call | tf_op jit(solution)/shard_map/finish/pallas_call | solution.py:477
  19.1 1.6 %collective-permute-start.7 = (bf16[64,512]{1,0:T(8,128)(2,1)S(1)}, bf16[64,512]{1,0:T(8,128)(2,1)S(1)}, u32[]{:S(2)}, u32[]{:S(2)}) collective-permute-start(bf16[64,512]{1,0:T(8,128)(2,1)S(1)} %get-tuple-element.28), channel_id=1, source_target_pairs={{0,2},{1,3},{2,0},{3,1},{4,6},{5,7},{6,4},{7,5},{8,10},{9,11},{10,... | collective-permute-start | bytes 196616 | tf_op jit(solution)/shard_map/ppermute | solution.py:487
  20.8 0.0 collective-permute-start.8
  20.8 0.6 %collective-permute-start.9 = (bf16[64,512]{1,0:T(8,128)(2,1)S(1)}, bf16[64,512]{1,0:T(8,128)(2,1)S(1)}, u32[]{:S(2)}, u32[]{:S(2)}) collective-permute-start(bf16[64,512]{1,0:T(8,128)(2,1)S(1)} %get-tuple-element.30), channel_id=1, source_target_pairs={{0,1},{1,0},{2,3},{3,2},{4,5},{5,4},{6,7},{7,6},{8,9},{9,8},{10,11... | collective-permute-start | bytes 196616 | tf_op jit(solution)/shard_map/ppermute | solution.py:487
  21.4 0.3 %rest.1 = f32[64,512]{1,0:T(8,128)S(1)} custom-call(s32[1]{0:T(128)} %bitcast.place_ref, bf16[64,512]{1,0:T(8,128)(2,1)S(1)} %get-tuple-element.27.residual_ref, bf16[2048,512]{1,0:T(8,128)(2,1)S(1)} %get-tuple-element.18.refs_3_.refs_1_.basis_ref), custom_call_target="tpu_custom_call" | custom-call | flops 80000000 | bytes 1500000 | tf_op jit(solution)/shard_map/rest/pallas_call | solution.py:490
  21.6 1.8 %collective-permute-done.7 = bf16[64,512]{1,0:T(8,128)(2,1)S(1)} collective-permute-done((bf16[64,512]{1,0:T(8,128)(2,1)S(1)}, bf16[64,512]{1,0:T(8,128)(2,1)S(1)}, u32[]{:S(2)}, u32[]{:S(2)}) %collective-permute-start.7) | collective-permute-done | bytes 65568 | tf_op jit(solution)/shard_map/ppermute | solution.py:487
  23.5 1.4 %collective-permute-done.8 = bf16[64,512]{1,0:T(8,128)(2,1)S(1)} collective-permute-done((bf16[64,512]{1,0:T(8,128)(2,1)S(1)}, bf16[64,512]{1,0:T(8,128)(2,1)S(1)}, u32[]{:S(2)}, u32[]{:S(2)}) %collective-permute-start.8) | collective-permute-done | bytes 65568 | tf_op jit(solution)/shard_map/ppermute | solution.py:487
  24.9 0.0 collective-permute-done.9
  24.9 0.7 %convert_add_fusion = f32[64,512]{1,0:T(8,128)} fusion(bf16[64,512]{1,0:T(8,128)(2,1)S(1)} %collective-permute-done.9, bf16[64,512]{1,0:T(8,128)(2,1)S(1)} %collective-permute-done.8, f32[64,512]{1,0:T(8,128)S(1)} %rest.1, bf16[64,512]{1,0:T(8,128)(2,1)S(1)} %collective-permute-done.7), kind=kLoop, calls=%fused_computation | loop fusion | flops 196608 | bytes 458752 | tf_op jit(solution)/shard_map/add | solution.py:500
Async XLA Ops:
  0.0 5.6 %collective-permute-start.2 = (bf16[64,512]{1,0:T(8,128)(2,1)}, bf16[64,512]{1,0:T(8,128)(2,1)S(1)}, u32[]{:S(2)}, u32[]{:S(2)}) collective-permute-start(bf16[64,512]{1,0:T(8,128)(2,1)} %refs_2_.1), channel_id=1, source_target_pairs={{0,2},{1,3},{2,0},{3,1},{4,6},{5,7},{6,4},{7,5},{8,10},{9,11},{10,... | collective-permute-start | bytes 196616 | tf_op jit(solution)/shard_map/ppermute | solution.py:383
  3.0 2.6 %collective-permute-start.1 = (bf16[64,512]{1,0:T(8,128)(2,1)}, bf16[64,512]{1,0:T(8,128)(2,1)S(1)}, u32[]{:S(2)}, u32[]{:S(2)}) collective-permute-start(bf16[64,512]{1,0:T(8,128)(2,1)} %refs_2_.1), channel_id=1, source_target_pairs={{0,1},{1,0},{2,3},{3,2},{4,5},{5,4},{6,7},{7,6},{8,9},{9,8},{10,11... | collective-permute-start | bytes 196616 | tf_op jit(solution)/shard_map/ppermute | solution.py:383
  3.0 4.0 %collective-permute-start = (bf16[64,512]{1,0:T(8,128)(2,1)}, bf16[64,512]{1,0:T(8,128)(2,1)S(1)}, u32[]{:S(2)}, u32[]{:S(2)}) collective-permute-start(bf16[64,512]{1,0:T(8,128)(2,1)} %refs_2_.1), channel_id=1, source_target_pairs={{0,3},{1,2},{2,1},{3,0},{4,7},{5,6},{6,5},{7,4},{8,11},{9,10},{10,... | collective-permute-start | bytes 196616 | tf_op jit(solution)/shard_map/ppermute | solution.py:383
  7.2 4.6 %collective-permute-start.5 = (f32[4,512]{1,0:T(4,128)S(1)}, f32[4,512]{1,0:T(4,128)S(1)}, u32[]{:S(2)}, u32[]{:S(2)}) collective-permute-start(f32[4,512]{1,0:T(4,128)S(1)} %get-tuple-element.26.refs_0_), channel_id=1, source_target_pairs={{0,12},{4,8},{8,4},{12,0},{16,28},{20,24},{24,20},{28,16},{1,13},{... | collective-permute-start | bytes 24584 | tf_op jit(solution)/shard_map/ppermute | solution.py:453
  9.8 3.7 %collective-permute-start.4 = (f32[4,512]{1,0:T(4,128)S(1)}, f32[4,512]{1,0:T(4,128)S(1)}, u32[]{:S(2)}, u32[]{:S(2)}) collective-permute-start(f32[4,512]{1,0:T(4,128)S(1)} %get-tuple-element.26.refs_0_), channel_id=1, source_target_pairs={{0,8},{4,12},{8,0},{12,4},{16,24},{20,28},{24,16},{28,20},{1,9},{5... | collective-permute-start | bytes 24584 | tf_op jit(solution)/shard_map/ppermute | solution.py:453
  10.2 3.7 %collective-permute-start.3 = (f32[4,512]{1,0:T(4,128)S(1)}, f32[4,512]{1,0:T(4,128)S(1)}, u32[]{:S(2)}, u32[]{:S(2)}) collective-permute-start(f32[4,512]{1,0:T(4,128)S(1)} %get-tuple-element.26.refs_0_), channel_id=1, source_target_pairs={{0,4},{4,0},{8,12},{12,8},{16,20},{20,16},{24,28},{28,24},{1,5},{5... | collective-permute-start | bytes 24584 | tf_op jit(solution)/shard_map/ppermute | solution.py:453
  13.9 4.6 %collective-permute-start.6 = (f32[4,512]{1,0:T(4,128)S(1)}, f32[4,512]{1,0:T(4,128)S(1)}, u32[]{:S(2)}, u32[]{:S(2)}) collective-permute-start(f32[4,512]{1,0:T(4,128)S(1)} %merge.1), channel_id=1, source_target_pairs={{0,16},{4,20},{8,24},{12,28},{16,0},{20,4},{24,8},{28,12},{1,17},{... | collective-permute-start | bytes 24584 | tf_op jit(solution)/shard_map/ppermute | solution.py:464
  19.1 4.3 %collective-permute-start.7 = (bf16[64,512]{1,0:T(8,128)(2,1)S(1)}, bf16[64,512]{1,0:T(8,128)(2,1)S(1)}, u32[]{:S(2)}, u32[]{:S(2)}) collective-permute-start(bf16[64,512]{1,0:T(8,128)(2,1)S(1)} %get-tuple-element.28), channel_id=1, source_target_pairs={{0,2},{1,3},{2,0},{3,1},{4,6},{5,7},{6,4},{7,5},{8,10},{9,11},{10,... | collective-permute-start | bytes 196616 | tf_op jit(solution)/shard_map/ppermute | solution.py:487
  20.8 4.1 %collective-permute-start.8 = (bf16[64,512]{1,0:T(8,128)(2,1)S(1)}, bf16[64,512]{1,0:T(8,128)(2,1)S(1)}, u32[]{:S(2)}, u32[]{:S(2)}) collective-permute-start(bf16[64,512]{1,0:T(8,128)(2,1)S(1)} %get-tuple-element.29), channel_id=1, source_target_pairs={{0,3},{1,2},{2,1},{3,0},{4,7},{5,6},{6,5},{7,4},{8,11},{9,10},{10,... | collective-permute-start | bytes 196616 | tf_op jit(solution)/shard_map/ppermute | solution.py:487
  20.8 4.1 %collective-permute-start.9 = (bf16[64,512]{1,0:T(8,128)(2,1)S(1)}, bf16[64,512]{1,0:T(8,128)(2,1)S(1)}, u32[]{:S(2)}, u32[]{:S(2)}) collective-permute-start(bf16[64,512]{1,0:T(8,128)(2,1)S(1)} %get-tuple-element.30), channel_id=1, source_target_pairs={{0,1},{1,0},{2,3},{3,2},{4,5},{5,4},{6,7},{7,6},{8,9},{9,8},{10,11... | collective-permute-start | bytes 196616 | tf_op jit(solution)/shard_map/ppermute | solution.py:487

commit v2 on v1

--- a/solution.py
+++ b/solution.py
@@ -186,18 +186,18 @@
 
 
 def rotate_kernel(first, place_ref, *refs):
-    pieces, others = first
+    pieces, stage = first
     obs_refs, (basis_ref, *refs) = refs[: len(pieces)], refs[len(pieces) :]
     depth = obs_refs[0].shape[1]
-    z = None if others is None else refs[0][...]
+    z = refs[0][...] if stage else None
     for piece, obs_ref in zip(pieces, obs_refs):
         begin = pl.multiple_of((place_ref[0] ^ piece) * depth, depth)
         term = jnp.dot(
             obs_ref[...], basis_ref[pl.ds(begin, depth), :], preferred_element_type=F32
         )
         z = term if z is None else z + term
-    if others is None:
-        refs[0][...] = z
+    if stage < 2:
+        refs[-1][...] = z
         return
     _, w_ref, z_ref, sum_ref = refs
     z_ref[...] = z
@@ -430,24 +430,26 @@
             )
         ),
     )
-    last = pieces - 1
-    early = list(range(last))
-    z = pl.pallas_call(
-        functools.partial(rotate_kernel, (early, None)),
-        out_shape=shape(steps, width),
-        in_specs=[smem] + [vmem] * pieces,
-        out_specs=vmem,
-        compiler_params=params,
-        name="rotate_early",
-    )(place, *(obs[piece] for piece in early), basis)
+    *early, last = [[0, 1], *([piece] for piece in range(2, pieces))] if pieces > 2 else [[0], [1]]
+    z = ()
+    for group in early:
+        z = pl.pallas_call(
+            functools.partial(rotate_kernel, (group, len(z))),
+            out_shape=shape(steps, width),
+            in_specs=[smem] + [vmem] * (len(group) + 1 + len(z)),
+            out_specs=vmem,
+            compiler_params=params,
+            name="rotate_early",
+        )(place, *(obs[piece] for piece in group), basis, *z)
+        z = (z,)
     z, summary = pl.pallas_call(
-        functools.partial(rotate_kernel, ([last], early)),
+        functools.partial(rotate_kernel, (last, 2)),
         out_shape=(shape(steps, width), shape(4, width)),
         in_specs=[smem] + [vmem] * 4,
         out_specs=(vmem,) * 2,
         compiler_params=params,
         name="rotate_last",
-    )(place, obs[last], basis, z, w)
+    )(place, obs[last[0]], basis, *z, w)
     sums = [summary]
     for step in range(1, 4):
         sums.append(lax.ppermute(summary, "tm", [(a, a ^ step) for a in range(blocks)]))
@@ -472,7 +474,7 @@
         cost_estimate=pl.CostEstimate(flops=10000000, bytes_accessed=1000000, transcendentals=0),
         name="local",
     )(me, z, const, merges)
-    far = list(range(2, pieces)) + [1]
+    far = list(range(pieces - 1, 0, -1))
     near = [0]
     residual, *parts = pl.pallas_call(
         functools.partial(finish_kernel, far),

time: 25.7 us -> 26.2 us (1.019)
  waiting for transfers between devices: 8.17 us -> 8.73 us
  starting transfers between devices: 11.5 us -> 11.2 us
    ppermute x3, waiting for transfers between devices: 3.25 us -> 3.66 us  [shards(): lax.ppermute(part, 'mode', [(a, a ^ piece) for a in range(pieces)])]
    ppermute x3, starting transfers between devices: 2.21 us -> 1.92 us  [shards(): lax.ppermute(part, 'mode', [(a, a ^ piece) for a in range(pieces)])]
    pallas_call x2 -> x3, Pallas kernels: 0.63 us -> 0.75 us  [the longest x2 0.5 us: shards(): pl.pallas_call(functools.partial(rotate_kernel, (group, len(z))), out_sha...]
where the time goes in v2:
time: 26.2 us; the launch traced here: 26 us
  starting transfers between devices  11.2 us (43%)
  waiting for transfers between devices  8.73 us (33%)
  Pallas kernels  4.65 us (18%)
  between operations  0.71 us (3%)
  other arithmetic  0.69 us (3%)
    ppermute x4, starting transfers between devices, shards(): lax.ppermute(summary, 'tm', [(a, a ^ step) for a in range(blocks)])  6.21 us
    ppermute x4, waiting for transfers between devices, shards(): lax.ppermute(summary, 'tm', [(a, a ^ step) for a in range(blocks)])  3.82 us
    ppermute x3, waiting for transfers between devices, shards(): lax.ppermute(part, 'mode', [(a, a ^ piece) for a in range(pieces)])  3.66 us
    ppermute x3, starting transfers between devices, exchange(): out.append(lax.ppermute(value, axis, [(a, a ^ step) for a in range(count)]))  3.11 us
    ppermute x3, starting transfers between devices, shards(): lax.ppermute(part, 'mode', [(a, a ^ piece) for a in range(pieces)])  1.92 us
    pallas_call x1, Pallas kernels, shards(): pl.pallas_call(functools.partial(coefficients_kernel, blocks), out_shape=...  1.7 us
    pallas_call x1, Pallas kernels, shards(): pl.pallas_call(functools.partial(local_kernel, blocks), out_shape=(shape(...  1.25 us
    ppermute x3, waiting for transfers between devices, exchange(): out.append(lax.ppermute(value, axis, [(a, a ^ step) for a in range(count)]))  1.25 us
  transfers between devices with their start and end apart: 10, of which 8 were waited for; matrix products, arithmetic and copies ran while one was open for 0% of the time, Pallas kernels for 14%

profile of v2, /device:TPU:0, one launch (start us, length us, event | category | flops | bytes accessed | tf_op | source)
XLA Modules:
  0.0 26.0 jit_solution(4601104168192412821)
XLA Ops:
  0.0 0.5 %collective-permute-start.2 = (bf16[64,512]{1,0:T(8,128)(2,1)}, bf16[64,512]{1,0:T(8,128)(2,1)S(1)}, u32[]{:S(2)}, u32[]{:S(2)}) collective-permute-start(bf16[64,512]{1,0:T(8,128)(2,1)} %refs_2_.1), channel_id=1, source_target_pairs={{0,1},{1,0},{2,3},{3,2},{4,5},{5,4},{6,7},{7,6},{8,9},{9,8},{10,11... | collective-permute-start | bytes 196616 | tf_op jit(solution)/shard_map/ppermute | solution.py:383
  0.5 2.5 %collective-permute-start.1 = (bf16[64,512]{1,0:T(8,128)(2,1)}, bf16[64,512]{1,0:T(8,128)(2,1)S(1)}, u32[]{:S(2)}, u32[]{:S(2)}) collective-permute-start(bf16[64,512]{1,0:T(8,128)(2,1)} %refs_2_.1), channel_id=1, source_target_pairs={{0,2},{1,3},{2,0},{3,1},{4,6},{5,7},{6,4},{7,5},{8,10},{9,11},{10,... | collective-permute-start | bytes 196616 | tf_op jit(solution)/shard_map/ppermute | solution.py:383
  3.0 0.1 collective-permute-start
  3.8 1.7 %coefficients.1 = (f32[20,8,512]{2,1,0:T(8,128)S(1)}, f32[4,64,512]{2,1,0:T(8,128)S(1)}, f32[32,512]{1,0:T(8,128)S(1)}, bf16[2048,512]{1,0:T(8,128)(2,1)S(1)}, bf16[64,512]{1,0:T(8,128)(2,1)S(1)}) custom-call(f32[1]{0:T(128)S(6)} %copy.6.noise_ref, f32[1,512]{1,0:T(1,128)} %bitcast.4, f32[1,512]{1,0:T(1,128)} %bitcast.5, bf16[64,512]{1,0:T(8,128)(2,1)} %refs_2_.1, ...), custom_call_target="tpu_custom_call" | custom-call | flops 20000000 | bytes 2000000 | tf_op jit(solution)/shard_map/coefficients/pallas_call | solution.py:402
  5.5 0.0 collective-permute-done.2.refs_1_
  5.5 0.3 %rotate_early.2.refs_2_ = f32[64,512]{1,0:T(8,128)S(1)} custom-call(s32[1]{0:T(128)} %bitcast.place_ref, bf16[64,512]{1,0:T(8,128)(2,1)S(1)} %get-tuple-element.19.refs_0_, bf16[64,512]{1,0:T(8,128)(2,1)S(1)} %collective-permute-done.2.refs_1_, bf16[2048,512]{1,0:T(8,128)(2,1)S(1)} %get-tuple-element.18.refs_2_.refs_1_.basis_ref), custom_call_target="tpu_custom_call" | custom-call | tf_op jit(solution)/shard_map/rotate_early/pallas_call | solution.py:436
  5.8 0.2 collective-permute-done.1.refs_0_
  5.9 0.2 rotate_early.3.refs_2_
  6.2 1.1 %collective-permute-done.refs_0_ = bf16[64,512]{1,0:T(8,128)(2,1)S(1)} collective-permute-done((bf16[64,512]{1,0:T(8,128)(2,1)}, bf16[64,512]{1,0:T(8,128)(2,1)S(1)}, u32[]{:S(2)}, u32[]{:S(2)}) %collective-permute-start) | collective-permute-done | bytes 65568 | tf_op jit(solution)/shard_map/ppermute | solution.py:383
  7.3 0.3 rotate_last.1
  7.5 2.6 %collective-permute-start.5 = (f32[4,512]{1,0:T(4,128)S(1)}, f32[4,512]{1,0:T(4,128)S(1)}, u32[]{:S(2)}, u32[]{:S(2)}) collective-permute-start(f32[4,512]{1,0:T(4,128)S(1)} %get-tuple-element.26.refs_0_), channel_id=1, source_target_pairs={{0,12},{4,8},{8,4},{12,0},{16,28},{20,24},{24,20},{28,16},{1,13},{... | collective-permute-start | bytes 24584 | tf_op jit(solution)/shard_map/ppermute | solution.py:455
  10.1 0.4 %collective-permute-start.4 = (f32[4,512]{1,0:T(4,128)S(1)}, f32[4,512]{1,0:T(4,128)S(1)}, u32[]{:S(2)}, u32[]{:S(2)}) collective-permute-start(f32[4,512]{1,0:T(4,128)S(1)} %get-tuple-element.26.refs_0_), channel_id=1, source_target_pairs={{0,8},{4,12},{8,0},{12,4},{16,24},{20,28},{24,16},{28,20},{1,9},{5... | collective-permute-start | bytes 24584 | tf_op jit(solution)/shard_map/ppermute | solution.py:455
  10.5 0.5 %collective-permute-start.3 = (f32[4,512]{1,0:T(4,128)S(1)}, f32[4,512]{1,0:T(4,128)S(1)}, u32[]{:S(2)}, u32[]{:S(2)}) collective-permute-start(f32[4,512]{1,0:T(4,128)S(1)} %get-tuple-element.26.refs_0_), channel_id=1, source_target_pairs={{0,4},{4,0},{8,12},{12,8},{16,20},{20,16},{24,28},{28,24},{1,5},{5... | collective-permute-start | bytes 24584 | tf_op jit(solution)/shard_map/ppermute | solution.py:455
  11.1 1.1 %collective-permute-done.5.refs_3_ = f32[4,512]{1,0:T(4,128)S(1)} collective-permute-done((f32[4,512]{1,0:T(4,128)S(1)}, f32[4,512]{1,0:T(4,128)S(1)}, u32[]{:S(2)}, u32[]{:S(2)}) %collective-permute-start.5) | collective-permute-done | bytes 8224 | tf_op jit(solution)/shard_map/ppermute | solution.py:455
  12.1 1.6 %collective-permute-done.4.refs_2_ = f32[4,512]{1,0:T(4,128)S(1)} collective-permute-done((f32[4,512]{1,0:T(4,128)S(1)}, f32[4,512]{1,0:T(4,128)S(1)}, u32[]{:S(2)}, u32[]{:S(2)}) %collective-permute-start.4) | collective-permute-done | bytes 8224 | tf_op jit(solution)/shard_map/ppermute | solution.py:455
  13.7 0.4 %collective-permute-done.3.refs_1_ = f32[4,512]{1,0:T(4,128)S(1)} collective-permute-done((f32[4,512]{1,0:T(4,128)S(1)}, f32[4,512]{1,0:T(4,128)S(1)}, u32[]{:S(2)}, u32[]{:S(2)}) %collective-permute-start.3) | collective-permute-done | bytes 8224 | tf_op jit(solution)/shard_map/ppermute | solution.py:455
  14.2 0.1 merge.1
  14.2 2.7 %collective-permute-start.6 = (f32[4,512]{1,0:T(4,128)S(1)}, f32[4,512]{1,0:T(4,128)S(1)}, u32[]{:S(2)}, u32[]{:S(2)}) collective-permute-start(f32[4,512]{1,0:T(4,128)S(1)} %merge.1), channel_id=1, source_target_pairs={{0,16},{4,20},{8,24},{12,28},{16,0},{20,4},{24,8},{28,12},{1,17},{... | collective-permute-start | bytes 24584 | tf_op jit(solution)/shard_map/ppermute | solution.py:466
  16.9 1.3 %local.1 = (f32[64,512]{1,0:T(8,128)S(1)}, f32[4,24,512]{2,1,0:T(8,128)S(1)}) custom-call(s32[1]{0:T(128)} %bitcast.1.me_ref, f32[64,512]{1,0:T(8,128)S(1)} %get-tuple-element.21.z_ref, f32[20,8,512]{2,1,0:T(8,128)S(1)} %get-tuple-element.22.const_ref, f32[32,512]{1,0:T(8,128)S(1)} %get-tuple-element.23.merge_ref), custom_call_target="tpu_custom_call" | custom-call | flops 10000000 | bytes 1000000 | tf_op jit(solution)/shard_map/local/pallas_call | solution.py:467
  18.2 0.7 %collective-permute-done.6.refs_4_ = f32[4,512]{1,0:T(4,128)S(1)} collective-permute-done((f32[4,512]{1,0:T(4,128)S(1)}, f32[4,512]{1,0:T(4,128)S(1)}, u32[]{:S(2)}, u32[]{:S(2)}) %collective-permute-start.6) | collective-permute-done | bytes 8224 | tf_op jit(solution)/shard_map/ppermute | solution.py:466
  18.9 0.6 %finish.1 = (bf16[64,512]{1,0:T(8,128)(2,1)S(1)}, bf16[64,512]{1,0:T(8,128)(2,1)S(1)}, bf16[64,512]{1,0:T(8,128)(2,1)S(1)}, bf16[64,512]{1,0:T(8,128)(2,1)S(1)}) custom-call(s32[1]{0:T(128)} %bitcast.place_ref, f32[64,512]{1,0:T(8,128)S(1)} %get-tuple-element.24.r_ref, f32[4,64,512]{2,1,0:T(8,128)S(1)} %get-tuple-element.20.refs_3_.w_ref, ...), custom_call_target="tpu_custom_call" | custom-call | tf_op jit(solution)/shard_map/finish/pallas_call | solution.py:479
  19.5 0.1 collective-permute-start.7
  19.5 1.5 %collective-permute-start.8 = (bf16[64,512]{1,0:T(8,128)(2,1)S(1)}, bf16[64,512]{1,0:T(8,128)(2,1)S(1)}, u32[]{:S(2)}, u32[]{:S(2)}) collective-permute-start(bf16[64,512]{1,0:T(8,128)(2,1)S(1)} %get-tuple-element.29), channel_id=1, source_target_pairs={{0,2},{1,3},{2,0},{3,1},{4,6},{5,7},{6,4},{7,5},{8,10},{9,11},{10,... | collective-permute-start | bytes 196616 | tf_op jit(solution)/shard_map/ppermute | solution.py:489
  21.1 0.3 %collective-permute-start.9 = (bf16[64,512]{1,0:T(8,128)(2,1)S(1)}, bf16[64,512]{1,0:T(8,128)(2,1)S(1)}, u32[]{:S(2)}, u32[]{:S(2)}) collective-permute-start(bf16[64,512]{1,0:T(8,128)(2,1)S(1)} %get-tuple-element.30), channel_id=1, source_target_pairs={{0,1},{1,0},{2,3},{3,2},{4,5},{5,4},{6,7},{7,6},{8,9},{9,8},{10,11... | collective-permute-start | bytes 196616 | tf_op jit(solution)/shard_map/ppermute | solution.py:489
  21.4 0.3 %rest.1 = f32[64,512]{1,0:T(8,128)S(1)} custom-call(s32[1]{0:T(128)} %bitcast.place_ref, bf16[64,512]{1,0:T(8,128)(2,1)S(1)} %get-tuple-element.27.residual_ref, bf16[2048,512]{1,0:T(8,128)(2,1)S(1)} %get-tuple-element.18.refs_2_.refs_1_.basis_ref), custom_call_target="tpu_custom_call" | custom-call | flops 80000000 | bytes 1500000 | tf_op jit(solution)/shard_map/rest/pallas_call | solution.py:492
  21.7 2.2 %collective-permute-done.7 = bf16[64,512]{1,0:T(8,128)(2,1)S(1)} collective-permute-done((bf16[64,512]{1,0:T(8,128)(2,1)S(1)}, bf16[64,512]{1,0:T(8,128)(2,1)S(1)}, u32[]{:S(2)}, u32[]{:S(2)}) %collective-permute-start.7) | collective-permute-done | bytes 65568 | tf_op jit(solution)/shard_map/ppermute | solution.py:489
  23.9 1.4 %collective-permute-done.8 = bf16[64,512]{1,0:T(8,128)(2,1)S(1)} collective-permute-done((bf16[64,512]{1,0:T(8,128)(2,1)S(1)}, bf16[64,512]{1,0:T(8,128)(2,1)S(1)}, u32[]{:S(2)}, u32[]{:S(2)}) %collective-permute-start.8) | collective-permute-done | bytes 65568 | tf_op jit(solution)/shard_map/ppermute | solution.py:489
  25.3 0.0 collective-permute-done.9
  25.3 0.7 %convert_add_fusion = f32[64,512]{1,0:T(8,128)} fusion(bf16[64,512]{1,0:T(8,128)(2,1)S(1)} %collective-permute-done.9, bf16[64,512]{1,0:T(8,128)(2,1)S(1)} %collective-permute-done.8, f32[64,512]{1,0:T(8,128)S(1)} %rest.1, bf16[64,512]{1,0:T(8,128)(2,1)S(1)} %collective-permute-done.7), kind=kLoop, calls=%fused_computation | loop fusion | flops 196608 | bytes 458752 | tf_op jit(solution)/shard_map/add | solution.py:502
Async XLA Ops:
  0.0 5.5 %collective-permute-start.2 = (bf16[64,512]{1,0:T(8,128)(2,1)}, bf16[64,512]{1,0:T(8,128)(2,1)S(1)}, u32[]{:S(2)}, u32[]{:S(2)}) collective-permute-start(bf16[64,512]{1,0:T(8,128)(2,1)} %refs_2_.1), channel_id=1, source_target_pairs={{0,1},{1,0},{2,3},{3,2},{4,5},{5,4},{6,7},{7,6},{8,9},{9,8},{10,11... | collective-permute-start | bytes 196616 | tf_op jit(solution)/shard_map/ppermute | solution.py:383
  0.5 5.5 %collective-permute-start.1 = (bf16[64,512]{1,0:T(8,128)(2,1)}, bf16[64,512]{1,0:T(8,128)(2,1)S(1)}, u32[]{:S(2)}, u32[]{:S(2)}) collective-permute-start(bf16[64,512]{1,0:T(8,128)(2,1)} %refs_2_.1), channel_id=1, source_target_pairs={{0,2},{1,3},{2,0},{3,1},{4,6},{5,7},{6,4},{7,5},{8,10},{9,11},{10,... | collective-permute-start | bytes 196616 | tf_op jit(solution)/shard_map/ppermute | solution.py:383
  3.0 4.3 %collective-permute-start = (bf16[64,512]{1,0:T(8,128)(2,1)}, bf16[64,512]{1,0:T(8,128)(2,1)S(1)}, u32[]{:S(2)}, u32[]{:S(2)}) collective-permute-start(bf16[64,512]{1,0:T(8,128)(2,1)} %refs_2_.1), channel_id=1, source_target_pairs={{0,3},{1,2},{2,1},{3,0},{4,7},{5,6},{6,5},{7,4},{8,11},{9,10},{10,... | collective-permute-start | bytes 196616 | tf_op jit(solution)/shard_map/ppermute | solution.py:383
  7.5 4.6 %collective-permute-start.5 = (f32[4,512]{1,0:T(4,128)S(1)}, f32[4,512]{1,0:T(4,128)S(1)}, u32[]{:S(2)}, u32[]{:S(2)}) collective-permute-start(f32[4,512]{1,0:T(4,128)S(1)} %get-tuple-element.26.refs_0_), channel_id=1, source_target_pairs={{0,12},{4,8},{8,4},{12,0},{16,28},{20,24},{24,20},{28,16},{1,13},{... | collective-permute-start | bytes 24584 | tf_op jit(solution)/shard_map/ppermute | solution.py:455
  10.1 3.7 %collective-permute-start.4 = (f32[4,512]{1,0:T(4,128)S(1)}, f32[4,512]{1,0:T(4,128)S(1)}, u32[]{:S(2)}, u32[]{:S(2)}) collective-permute-start(f32[4,512]{1,0:T(4,128)S(1)} %get-tuple-element.26.refs_0_), channel_id=1, source_target_pairs={{0,8},{4,12},{8,0},{12,4},{16,24},{20,28},{24,16},{28,20},{1,9},{5... | collective-permute-start | bytes 24584 | tf_op jit(solution)/shard_map/ppermute | solution.py:455
  10.5 3.7 %collective-permute-start.3 = (f32[4,512]{1,0:T(4,128)S(1)}, f32[4,512]{1,0:T(4,128)S(1)}, u32[]{:S(2)}, u32[]{:S(2)}) collective-permute-start(f32[4,512]{1,0:T(4,128)S(1)} %get-tuple-element.26.refs_0_), channel_id=1, source_target_pairs={{0,4},{4,0},{8,12},{12,8},{16,20},{20,16},{24,28},{28,24},{1,5},{5... | collective-permute-start | bytes 24584 | tf_op jit(solution)/shard_map/ppermute | solution.py:455
  14.2 4.6 %collective-permute-start.6 = (f32[4,512]{1,0:T(4,128)S(1)}, f32[4,512]{1,0:T(4,128)S(1)}, u32[]{:S(2)}, u32[]{:S(2)}) collective-permute-start(f32[4,512]{1,0:T(4,128)S(1)} %merge.1), channel_id=1, source_target_pairs={{0,16},{4,20},{8,24},{12,28},{16,0},{20,4},{24,8},{28,12},{1,17},{... | collective-permute-start | bytes 24584 | tf_op jit(solution)/shard_map/ppermute | solution.py:466
  19.5 4.5 %collective-permute-start.7 = (bf16[64,512]{1,0:T(8,128)(2,1)S(1)}, bf16[64,512]{1,0:T(8,128)(2,1)S(1)}, u32[]{:S(2)}, u32[]{:S(2)}) collective-permute-start(bf16[64,512]{1,0:T(8,128)(2,1)S(1)} %get-tuple-element.28), channel_id=1, source_target_pairs={{0,3},{1,2},{2,1},{3,0},{4,7},{5,6},{6,5},{7,4},{8,11},{9,10},{10,... | collective-permute-start | bytes 196616 | tf_op jit(solution)/shard_map/ppermute | solution.py:489
  19.5 5.8 %collective-permute-start.8 = (bf16[64,512]{1,0:T(8,128)(2,1)S(1)}, bf16[64,512]{1,0:T(8,128)(2,1)S(1)}, u32[]{:S(2)}, u32[]{:S(2)}) collective-permute-start(bf16[64,512]{1,0:T(8,128)(2,1)S(1)} %get-tuple-element.29), channel_id=1, source_target_pairs={{0,2},{1,3},{2,0},{3,1},{4,6},{5,7},{6,4},{7,5},{8,10},{9,11},{10,... | collective-permute-start | bytes 196616 | tf_op jit(solution)/shard_map/ppermute | solution.py:489
  21.1 4.3 %collective-permute-start.9 = (bf16[64,512]{1,0:T(8,128)(2,1)S(1)}, bf16[64,512]{1,0:T(8,128)(2,1)S(1)}, u32[]{:S(2)}, u32[]{:S(2)}) collective-permute-start(bf16[64,512]{1,0:T(8,128)(2,1)S(1)} %get-tuple-element.30), channel_id=1, source_target_pairs={{0,1},{1,0},{2,3},{3,2},{4,5},{5,4},{6,7},{7,6},{8,9},{9,8},{10,11... | collective-permute-start | bytes 196616 | tf_op jit(solution)/shard_map/ppermute | solution.py:489

commit v3 on v1

--- a/solution.py
+++ b/solution.py
@@ -377,6 +377,23 @@
     rotate_back(residual_ref[...], pieces, place_ref, basis_ref, outs)
 
 
+def add_kernel(own_ref, *refs):
+    *parts, out_ref, total_ref, sems = refs
+    quarter = own_ref.shape[0] // 4
+    copies = []
+    for k in range(4):
+        rows = pl.ds(k * quarter, quarter)
+        total = own_ref[rows, :]
+        for part in parts:
+            total = total + part[rows, :].astype(F32)
+        total_ref[rows, :] = total
+        copy = pltpu.make_async_copy(total_ref.at[rows, :], out_ref.at[rows, :], sems.at[k])
+        copy.start()
+        copies.append(copy)
+    for copy in copies:
+        copy.wait()
+
+
 def exchange(value, axis, count):
     out = [value]
     for step in range(1, count):
@@ -496,9 +513,15 @@
         cost_estimate=pl.CostEstimate(flops=80000000, bytes_accessed=1500000, transcendentals=0),
         name="rest",
     )(place, residual, basis)
-    for part in arrived:
-        grad_obs = grad_obs + part.astype(F32)
-    return grad_obs
+    return pl.pallas_call(
+        add_kernel,
+        out_shape=shape(steps, depth),
+        in_specs=[vmem] * pieces,
+        out_specs=pl.BlockSpec(memory_space=pltpu.HBM),
+        scratch_shapes=[pltpu.VMEM((steps, depth), F32), pltpu.SemaphoreType.DMA((4,))],
+        compiler_params=params,
+        name="add",
+    )(grad_obs, *arrived)
 
 
 def solution(mesh):

time: 25.7 us -> 25.8 us (level)
  other arithmetic: 0.69 us -> 0 us
  Pallas kernels: 4.53 us -> 5.22 us
    pallas_call x0 -> x1, Pallas kernels: none -> 0.69 us  [shards(): pl.pallas_call(add_kernel, out_shape=shape(steps, depth), in_specs=[vmem]...]
    add x1 -> x0, other arithmetic: 0.69 us -> none  [shards(): grad_obs = grad_obs + part.astype(F32)]
where the time goes in v3:
time: 25.8 us; the launch traced here: 25.6 us
  starting transfers between devices  11.5 us (45%)
  waiting for transfers between devices  8.17 us (32%)
  Pallas kernels  5.22 us (20%)
  between operations  0.69 us (3%)
    ppermute x4, starting transfers between devices, shards(): lax.ppermute(summary, 'tm', [(a, a ^ step) for a in range(blocks)])  6.21 us
    ppermute x4, waiting for transfers between devices, shards(): lax.ppermute(summary, 'tm', [(a, a ^ step) for a in range(blocks)])  3.82 us
    ppermute x3, waiting for transfers between devices, shards(): lax.ppermute(part, 'mode', [(a, a ^ piece) for a in range(pieces)])  3.25 us
    ppermute x3, starting transfers between devices, exchange(): out.append(lax.ppermute(value, axis, [(a, a ^ step) for a in range(count)]))  3.08 us
    ppermute x3, starting transfers between devices, shards(): lax.ppermute(part, 'mode', [(a, a ^ piece) for a in range(pieces)])  2.21 us
    pallas_call x1, Pallas kernels, shards(): pl.pallas_call(functools.partial(coefficients_kernel, blocks), out_shape=...  1.7 us
    pallas_call x1, Pallas kernels, shards(): pl.pallas_call(functools.partial(local_kernel, blocks), out_shape=(shape(...  1.25 us
    ppermute x3, waiting for transfers between devices, exchange(): out.append(lax.ppermute(value, axis, [(a, a ^ step) for a in range(count)]))  1.1 us
  transfers between devices with their start and end apart: 10, of which 8 were waited for; matrix products, arithmetic and copies ran while one was open for 0% of the time, Pallas kernels for 14%

profile of v3, /device:TPU:0, one launch (start us, length us, event | category | flops | bytes accessed | tf_op | source)
XLA Modules:
  0.0 25.6 jit_solution(16427149380439392317)
XLA Ops:
  0.0 3.0 %collective-permute-start.2 = (bf16[64,512]{1,0:T(8,128)(2,1)}, bf16[64,512]{1,0:T(8,128)(2,1)S(1)}, u32[]{:S(2)}, u32[]{:S(2)}) collective-permute-start(bf16[64,512]{1,0:T(8,128)(2,1)} %refs_2_.1), channel_id=1, source_target_pairs={{0,2},{1,3},{2,0},{3,1},{4,6},{5,7},{6,4},{7,5},{8,10},{9,11},{10,... | collective-permute-start | bytes 196616 | tf_op jit(solution)/shard_map/ppermute | solution.py:400
  3.0 0.0 collective-permute-start.1
  3.0 0.1 collective-permute-start
  3.7 1.7 %coefficients.1 = (f32[20,8,512]{2,1,0:T(8,128)S(1)}, f32[4,64,512]{2,1,0:T(8,128)S(1)}, f32[32,512]{1,0:T(8,128)S(1)}, bf16[2048,512]{1,0:T(8,128)(2,1)S(1)}, bf16[64,512]{1,0:T(8,128)(2,1)S(1)}) custom-call(f32[1]{0:T(128)S(6)} %copy.6.noise_ref, f32[1,512]{1,0:T(1,128)} %bitcast.4, f32[1,512]{1,0:T(1,128)} %bitcast.5, bf16[64,512]{1,0:T(8,128)(2,1)} %refs_2_.1, ...), custom_call_target="tpu_custom_call" | custom-call | flops 20000000 | bytes 2000000 | tf_op jit(solution)/shard_map/coefficients/pallas_call | solution.py:419
  5.4 0.1 collective-permute-done.2.refs_2_
  5.6 0.0 collective-permute-done.1.refs_1_
  5.6 0.4 %rotate_early.1.refs_2_ = f32[64,512]{1,0:T(8,128)S(1)} custom-call(s32[1]{0:T(128)} %bitcast.place_ref, bf16[64,512]{1,0:T(8,128)(2,1)S(1)} %get-tuple-element.19.refs_0_, bf16[64,512]{1,0:T(8,128)(2,1)S(1)} %collective-permute-done.1.refs_1_, bf16[64,512]{1,0:T(8,128)(2,1)S(1)} %collective-permute-done.2.refs_2_, ...), custom_call_target="tpu_custom_call" | custom-call | tf_op jit(solution)/shard_map/rotate_early/pallas_call | solution.py:452
  6.0 0.9 %collective-permute-done.refs_0_ = bf16[64,512]{1,0:T(8,128)(2,1)S(1)} collective-permute-done((bf16[64,512]{1,0:T(8,128)(2,1)}, bf16[64,512]{1,0:T(8,128)(2,1)S(1)}, u32[]{:S(2)}, u32[]{:S(2)}) %collective-permute-start) | collective-permute-done | bytes 65568 | tf_op jit(solution)/shard_map/ppermute | solution.py:400
  6.9 0.3 rotate_last.1
  7.2 2.6 %collective-permute-start.5 = (f32[4,512]{1,0:T(4,128)S(1)}, f32[4,512]{1,0:T(4,128)S(1)}, u32[]{:S(2)}, u32[]{:S(2)}) collective-permute-start(f32[4,512]{1,0:T(4,128)S(1)} %get-tuple-element.26.refs_0_), channel_id=1, source_target_pairs={{0,12},{4,8},{8,4},{12,0},{16,28},{20,24},{24,20},{28,16},{1,13},{... | collective-permute-start | bytes 24584 | tf_op jit(solution)/shard_map/ppermute | solution.py:470
  9.8 0.4 %collective-permute-start.4 = (f32[4,512]{1,0:T(4,128)S(1)}, f32[4,512]{1,0:T(4,128)S(1)}, u32[]{:S(2)}, u32[]{:S(2)}) collective-permute-start(f32[4,512]{1,0:T(4,128)S(1)} %get-tuple-element.26.refs_0_), channel_id=1, source_target_pairs={{0,8},{4,12},{8,0},{12,4},{16,24},{20,28},{24,16},{28,20},{1,9},{5... | collective-permute-start | bytes 24584 | tf_op jit(solution)/shard_map/ppermute | solution.py:470
  10.2 0.5 %collective-permute-start.3 = (f32[4,512]{1,0:T(4,128)S(1)}, f32[4,512]{1,0:T(4,128)S(1)}, u32[]{:S(2)}, u32[]{:S(2)}) collective-permute-start(f32[4,512]{1,0:T(4,128)S(1)} %get-tuple-element.26.refs_0_), channel_id=1, source_target_pairs={{0,4},{4,0},{8,12},{12,8},{16,20},{20,16},{24,28},{28,24},{1,5},{5... | collective-permute-start | bytes 24584 | tf_op jit(solution)/shard_map/ppermute | solution.py:470
  10.7 1.1 %collective-permute-done.5.refs_3_ = f32[4,512]{1,0:T(4,128)S(1)} collective-permute-done((f32[4,512]{1,0:T(4,128)S(1)}, f32[4,512]{1,0:T(4,128)S(1)}, u32[]{:S(2)}, u32[]{:S(2)}) %collective-permute-start.5) | collective-permute-done | bytes 8224 | tf_op jit(solution)/shard_map/ppermute | solution.py:470
  11.8 1.6 %collective-permute-done.4.refs_2_ = f32[4,512]{1,0:T(4,128)S(1)} collective-permute-done((f32[4,512]{1,0:T(4,128)S(1)}, f32[4,512]{1,0:T(4,128)S(1)}, u32[]{:S(2)}, u32[]{:S(2)}) %collective-permute-start.4) | collective-permute-done | bytes 8224 | tf_op jit(solution)/shard_map/ppermute | solution.py:470
  13.4 0.4 %collective-permute-done.3.refs_1_ = f32[4,512]{1,0:T(4,128)S(1)} collective-permute-done((f32[4,512]{1,0:T(4,128)S(1)}, f32[4,512]{1,0:T(4,128)S(1)}, u32[]{:S(2)}, u32[]{:S(2)}) %collective-permute-start.3) | collective-permute-done | bytes 8224 | tf_op jit(solution)/shard_map/ppermute | solution.py:470
  13.9 0.1 merge.1
  13.9 2.7 %collective-permute-start.6 = (f32[4,512]{1,0:T(4,128)S(1)}, f32[4,512]{1,0:T(4,128)S(1)}, u32[]{:S(2)}, u32[]{:S(2)}) collective-permute-start(f32[4,512]{1,0:T(4,128)S(1)} %merge.1), channel_id=1, source_target_pairs={{0,16},{4,20},{8,24},{12,28},{16,0},{20,4},{24,8},{28,12},{1,17},{... | collective-permute-start | bytes 24584 | tf_op jit(solution)/shard_map/ppermute | solution.py:481
  16.6 1.3 %local.1 = (f32[64,512]{1,0:T(8,128)S(1)}, f32[4,24,512]{2,1,0:T(8,128)S(1)}) custom-call(s32[1]{0:T(128)} %bitcast.1.me_ref, f32[64,512]{1,0:T(8,128)S(1)} %get-tuple-element.21.z_ref, f32[20,8,512]{2,1,0:T(8,128)S(1)} %get-tuple-element.22.const_ref, f32[32,512]{1,0:T(8,128)S(1)} %get-tuple-element.23.merge_ref), custom_call_target="tpu_custom_call" | custom-call | flops 10000000 | bytes 1000000 | tf_op jit(solution)/shard_map/local/pallas_call | solution.py:482
  17.8 0.7 %collective-permute-done.6.refs_4_ = f32[4,512]{1,0:T(4,128)S(1)} collective-permute-done((f32[4,512]{1,0:T(4,128)S(1)}, f32[4,512]{1,0:T(4,128)S(1)}, u32[]{:S(2)}, u32[]{:S(2)}) %collective-permute-start.6) | collective-permute-done | bytes 8224 | tf_op jit(solution)/shard_map/ppermute | solution.py:481
  18.5 0.6 %finish.1 = (bf16[64,512]{1,0:T(8,128)(2,1)S(1)}, bf16[64,512]{1,0:T(8,128)(2,1)S(1)}, bf16[64,512]{1,0:T(8,128)(2,1)S(1)}, bf16[64,512]{1,0:T(8,128)(2,1)S(1)}) custom-call(s32[1]{0:T(128)} %bitcast.place_ref, f32[64,512]{1,0:T(8,128)S(1)} %get-tuple-element.24.r_ref, f32[4,64,512]{2,1,0:T(8,128)S(1)} %get-tuple-element.20.refs_3_.w_ref, ...), custom_call_target="tpu_custom_call" | custom-call | tf_op jit(solution)/shard_map/finish/pallas_call | solution.py:494
  19.1 1.6 %collective-permute-start.7 = (bf16[64,512]{1,0:T(8,128)(2,1)S(1)}, bf16[64,512]{1,0:T(8,128)(2,1)S(1)}, u32[]{:S(2)}, u32[]{:S(2)}) collective-permute-start(bf16[64,512]{1,0:T(8,128)(2,1)S(1)} %get-tuple-element.28), channel_id=1, source_target_pairs={{0,2},{1,3},{2,0},{3,1},{4,6},{5,7},{6,4},{7,5},{8,10},{9,11},{10,... | collective-permute-start | bytes 196616 | tf_op jit(solution)/shard_map/ppermute | solution.py:504
  20.8 0.0 collective-permute-start.8
  20.8 0.6 %collective-permute-start.9 = (bf16[64,512]{1,0:T(8,128)(2,1)S(1)}, bf16[64,512]{1,0:T(8,128)(2,1)S(1)}, u32[]{:S(2)}, u32[]{:S(2)}) collective-permute-start(bf16[64,512]{1,0:T(8,128)(2,1)S(1)} %get-tuple-element.30), channel_id=1, source_target_pairs={{0,1},{1,0},{2,3},{3,2},{4,5},{5,4},{6,7},{7,6},{8,9},{9,8},{10,11... | collective-permute-start | bytes 196616 | tf_op jit(solution)/shard_map/ppermute | solution.py:504
  21.4 0.3 %rest.1.own_ref = f32[64,512]{1,0:T(8,128)S(1)} custom-call(s32[1]{0:T(128)} %bitcast.place_ref, bf16[64,512]{1,0:T(8,128)(2,1)S(1)} %get-tuple-element.27.residual_ref, bf16[2048,512]{1,0:T(8,128)(2,1)S(1)} %get-tuple-element.18.refs_3_.refs_1_.basis_ref), custom_call_target="tpu_custom_call" | custom-call | flops 80000000 | bytes 1500000 | tf_op jit(solution)/shard_map/rest/pallas_call | solution.py:507
  21.6 1.8 %collective-permute-done.7.refs_0_ = bf16[64,512]{1,0:T(8,128)(2,1)S(1)} collective-permute-done((bf16[64,512]{1,0:T(8,128)(2,1)S(1)}, bf16[64,512]{1,0:T(8,128)(2,1)S(1)}, u32[]{:S(2)}, u32[]{:S(2)}) %collective-permute-start.7) | collective-permute-done | bytes 65568 | tf_op jit(solution)/shard_map/ppermute | solution.py:504
  23.5 1.4 %collective-permute-done.8.refs_1_ = bf16[64,512]{1,0:T(8,128)(2,1)S(1)} collective-permute-done((bf16[64,512]{1,0:T(8,128)(2,1)S(1)}, bf16[64,512]{1,0:T(8,128)(2,1)S(1)}, u32[]{:S(2)}, u32[]{:S(2)}) %collective-permute-start.8) | collective-permute-done | bytes 65568 | tf_op jit(solution)/shard_map/ppermute | solution.py:504
  24.9 0.0 collective-permute-done.9.refs_2_
  24.9 0.7 %add.1 = f32[64,512]{1,0:T(8,128)} custom-call(f32[64,512]{1,0:T(8,128)S(1)} %rest.1.own_ref, bf16[64,512]{1,0:T(8,128)(2,1)S(1)} %collective-permute-done.7.refs_0_, bf16[64,512]{1,0:T(8,128)(2,1)S(1)} %collective-permute-done.8.refs_1_, bf16[64,512]{1,0:T(8,128)(2,1)S(1)} %collective-permute-done.9.refs_2_), custom_call_target="tpu_custom_call" | custom-call | tf_op jit(solution)/shard_map/add/pallas_call | solution.py:516
Async XLA Ops:
  0.0 5.6 %collective-permute-start.2 = (bf16[64,512]{1,0:T(8,128)(2,1)}, bf16[64,512]{1,0:T(8,128)(2,1)S(1)}, u32[]{:S(2)}, u32[]{:S(2)}) collective-permute-start(bf16[64,512]{1,0:T(8,128)(2,1)} %refs_2_.1), channel_id=1, source_target_pairs={{0,2},{1,3},{2,0},{3,1},{4,6},{5,7},{6,4},{7,5},{8,10},{9,11},{10,... | collective-permute-start | bytes 196616 | tf_op jit(solution)/shard_map/ppermute | solution.py:400
  3.0 2.6 %collective-permute-start.1 = (bf16[64,512]{1,0:T(8,128)(2,1)}, bf16[64,512]{1,0:T(8,128)(2,1)S(1)}, u32[]{:S(2)}, u32[]{:S(2)}) collective-permute-start(bf16[64,512]{1,0:T(8,128)(2,1)} %refs_2_.1), channel_id=1, source_target_pairs={{0,1},{1,0},{2,3},{3,2},{4,5},{5,4},{6,7},{7,6},{8,9},{9,8},{10,11... | collective-permute-start | bytes 196616 | tf_op jit(solution)/shard_map/ppermute | solution.py:400
  3.0 4.0 %collective-permute-start = (bf16[64,512]{1,0:T(8,128)(2,1)}, bf16[64,512]{1,0:T(8,128)(2,1)S(1)}, u32[]{:S(2)}, u32[]{:S(2)}) collective-permute-start(bf16[64,512]{1,0:T(8,128)(2,1)} %refs_2_.1), channel_id=1, source_target_pairs={{0,3},{1,2},{2,1},{3,0},{4,7},{5,6},{6,5},{7,4},{8,11},{9,10},{10,... | collective-permute-start | bytes 196616 | tf_op jit(solution)/shard_map/ppermute | solution.py:400
  7.2 4.6 %collective-permute-start.5 = (f32[4,512]{1,0:T(4,128)S(1)}, f32[4,512]{1,0:T(4,128)S(1)}, u32[]{:S(2)}, u32[]{:S(2)}) collective-permute-start(f32[4,512]{1,0:T(4,128)S(1)} %get-tuple-element.26.refs_0_), channel_id=1, source_target_pairs={{0,12},{4,8},{8,4},{12,0},{16,28},{20,24},{24,20},{28,16},{1,13},{... | collective-permute-start | bytes 24584 | tf_op jit(solution)/shard_map/ppermute | solution.py:470
  9.8 3.7 %collective-permute-start.4 = (f32[4,512]{1,0:T(4,128)S(1)}, f32[4,512]{1,0:T(4,128)S(1)}, u32[]{:S(2)}, u32[]{:S(2)}) collective-permute-start(f32[4,512]{1,0:T(4,128)S(1)} %get-tuple-element.26.refs_0_), channel_id=1, source_target_pairs={{0,8},{4,12},{8,0},{12,4},{16,24},{20,28},{24,16},{28,20},{1,9},{5... | collective-permute-start | bytes 24584 | tf_op jit(solution)/shard_map/ppermute | solution.py:470
  10.2 3.7 %collective-permute-start.3 = (f32[4,512]{1,0:T(4,128)S(1)}, f32[4,512]{1,0:T(4,128)S(1)}, u32[]{:S(2)}, u32[]{:S(2)}) collective-permute-start(f32[4,512]{1,0:T(4,128)S(1)} %get-tuple-element.26.refs_0_), channel_id=1, source_target_pairs={{0,4},{4,0},{8,12},{12,8},{16,20},{20,16},{24,28},{28,24},{1,5},{5... | collective-permute-start | bytes 24584 | tf_op jit(solution)/shard_map/ppermute | solution.py:470
  13.9 4.6 %collective-permute-start.6 = (f32[4,512]{1,0:T(4,128)S(1)}, f32[4,512]{1,0:T(4,128)S(1)}, u32[]{:S(2)}, u32[]{:S(2)}) collective-permute-start(f32[4,512]{1,0:T(4,128)S(1)} %merge.1), channel_id=1, source_target_pairs={{0,16},{4,20},{8,24},{12,28},{16,0},{20,4},{24,8},{28,12},{1,17},{... | collective-permute-start | bytes 24584 | tf_op jit(solution)/shard_map/ppermute | solution.py:481
  19.1 4.3 %collective-permute-start.7 = (bf16[64,512]{1,0:T(8,128)(2,1)S(1)}, bf16[64,512]{1,0:T(8,128)(2,1)S(1)}, u32[]{:S(2)}, u32[]{:S(2)}) collective-permute-start(bf16[64,512]{1,0:T(8,128)(2,1)S(1)} %get-tuple-element.28), channel_id=1, source_target_pairs={{0,2},{1,3},{2,0},{3,1},{4,6},{5,7},{6,4},{7,5},{8,10},{9,11},{10,... | collective-permute-start | bytes 196616 | tf_op jit(solution)/shard_map/ppermute | solution.py:504
  20.8 4.1 %collective-permute-start.8 = (bf16[64,512]{1,0:T(8,128)(2,1)S(1)}, bf16[64,512]{1,0:T(8,128)(2,1)S(1)}, u32[]{:S(2)}, u32[]{:S(2)}) collective-permute-start(bf16[64,512]{1,0:T(8,128)(2,1)S(1)} %get-tuple-element.29), channel_id=1, source_target_pairs={{0,3},{1,2},{2,1},{3,0},{4,7},{5,6},{6,5},{7,4},{8,11},{9,10},{10,... | collective-permute-start | bytes 196616 | tf_op jit(solution)/shard_map/ppermute | solution.py:504
  20.8 4.1 %collective-permute-start.9 = (bf16[64,512]{1,0:T(8,128)(2,1)S(1)}, bf16[64,512]{1,0:T(8,128)(2,1)S(1)}, u32[]{:S(2)}, u32[]{:S(2)}) collective-permute-start(bf16[64,512]{1,0:T(8,128)(2,1)S(1)} %get-tuple-element.30), channel_id=1, source_target_pairs={{0,1},{1,0},{2,3},{3,2},{4,5},{5,4},{6,7},{7,6},{8,9},{9,8},{10,11... | collective-permute-start | bytes 196616 | tf_op jit(solution)/shard_map/ppermute | solution.py:504

commit v4 on v1

--- a/solution.py
+++ b/solution.py
@@ -10,6 +10,7 @@
 
 F32 = jnp.float32
 SUB = 8
+NEAR = (2, 1, 3)
 VMEM_LIMIT = 24 * 1024 * 1024
 
 
@@ -232,8 +233,8 @@
     if level:
         out_ref[...] = merge(level, me, parts[0], parts[1], merge_ref)
     else:
-        near = merge(0, me, parts[0], parts[1], merge_ref)
-        far = merge(0, me, parts[2], parts[3], merge_ref)
+        near = merge(0, me, parts[0], parts[1 + NEAR.index(1)], merge_ref)
+        far = merge(0, me, parts[1 + NEAR.index(2)], parts[1 + NEAR.index(3)], merge_ref)
         out_ref[...] = merge(1, me, near, far, merge_ref)
 
 
@@ -273,8 +274,9 @@
         rows = row + group * SUB
         kind = rows & 3
         line = rows >> 2
+        step = jnp.where(line == 1, NEAR[0], jnp.where(line == 2, NEAR[1], jnp.where(line == 3, NEAR[2], 0)))
         span = jnp.where(line < 4, 1, jnp.left_shift(1, jnp.maximum(line - 2, 0)))
-        near_me = mine ^ jnp.where(line < 4, line, span)
+        near_me = mine ^ jnp.where(line < 4, step, span)
         front = jnp.minimum((near_me // span) * span, blocks - 1)
         back = jnp.minimum(front + span - 1, blocks - 1)
         before, after = back < me, front > me
@@ -449,7 +451,7 @@
         name="rotate_last",
     )(place, obs[last], basis, z, w)
     sums = [summary]
-    for step in range(1, 4):
+    for step in NEAR:
         sums.append(lax.ppermute(summary, "tm", [(a, a ^ step) for a in range(blocks)]))
     for level in range(2, rounds):
         summary = pl.pallas_call(

time: 25.7 us -> 25.8 us (level)
  no operation moved by 1% of the time
where the time goes in v4:
time: 25.8 us; the launch traced here: 25.7 us
  starting transfers between devices  11.5 us (45%)
  waiting for transfers between devices  8.25 us (32%)
  Pallas kernels  4.53 us (18%)
  other arithmetic  0.69 us (3%)
  between operations  0.69 us (3%)
    ppermute x4, starting transfers between devices, shards(): lax.ppermute(summary, 'tm', [(a, a ^ step) for a in range(blocks)])  6.21 us
    ppermute x4, waiting for transfers between devices, shards(): lax.ppermute(summary, 'tm', [(a, a ^ step) for a in range(blocks)])  3.9 us
    ppermute x3, waiting for transfers between devices, shards(): lax.ppermute(part, 'mode', [(a, a ^ piece) for a in range(pieces)])  3.25 us
    ppermute x3, starting transfers between devices, exchange(): out.append(lax.ppermute(value, axis, [(a, a ^ step) for a in range(count)]))  3.08 us
    ppermute x3, starting transfers between devices, shards(): lax.ppermute(part, 'mode', [(a, a ^ piece) for a in range(pieces)])  2.21 us
    pallas_call x1, Pallas kernels, shards(): pl.pallas_call(functools.partial(coefficients_kernel, blocks), out_shape=...  1.7 us
    pallas_call x1, Pallas kernels, shards(): pl.pallas_call(functools.partial(local_kernel, blocks), out_shape=(shape(...  1.26 us
    ppermute x3, waiting for transfers between devices, exchange(): out.append(lax.ppermute(value, axis, [(a, a ^ step) for a in range(count)]))  1.1 us
  transfers between devices with their start and end apart: 10, of which 8 were waited for; matrix products, arithmetic and copies ran while one was open for 0% of the time, Pallas kernels for 14%

profile of v4, /device:TPU:0, one launch (start us, length us, event | category | flops | bytes accessed | tf_op | source)
XLA Modules:
  0.0 25.7 jit_solution(15594290939502939443)
XLA Ops:
  0.0 3.0 %collective-permute-start.2 = (bf16[64,512]{1,0:T(8,128)(2,1)}, bf16[64,512]{1,0:T(8,128)(2,1)S(1)}, u32[]{:S(2)}, u32[]{:S(2)}) collective-permute-start(bf16[64,512]{1,0:T(8,128)(2,1)} %refs_2_.1), channel_id=1, source_target_pairs={{0,2},{1,3},{2,0},{3,1},{4,6},{5,7},{6,4},{7,5},{8,10},{9,11},{10,... | collective-permute-start | bytes 196616 | tf_op jit(solution)/shard_map/ppermute | solution.py:385
  3.0 0.0 collective-permute-start.1
  3.0 0.1 collective-permute-start
  3.7 1.7 %coefficients.1 = (f32[20,8,512]{2,1,0:T(8,128)S(1)}, f32[4,64,512]{2,1,0:T(8,128)S(1)}, f32[32,512]{1,0:T(8,128)S(1)}, bf16[2048,512]{1,0:T(8,128)(2,1)S(1)}, bf16[64,512]{1,0:T(8,128)(2,1)S(1)}) custom-call(f32[1]{0:T(128)S(6)} %copy.6.noise_ref, f32[1,512]{1,0:T(1,128)} %bitcast.4, f32[1,512]{1,0:T(1,128)} %bitcast.5, bf16[64,512]{1,0:T(8,128)(2,1)} %refs_2_.1, ...), custom_call_target="tpu_custom_call" | custom-call | flops 20000000 | bytes 2000000 | tf_op jit(solution)/shard_map/coefficients/pallas_call | solution.py:404
  5.4 0.1 collective-permute-done.2.refs_2_
  5.6 0.0 collective-permute-done.1.refs_1_
  5.6 0.4 %rotate_early.1.refs_2_ = f32[64,512]{1,0:T(8,128)S(1)} custom-call(s32[1]{0:T(128)} %bitcast.place_ref, bf16[64,512]{1,0:T(8,128)(2,1)S(1)} %get-tuple-element.19.refs_0_, bf16[64,512]{1,0:T(8,128)(2,1)S(1)} %collective-permute-done.1.refs_1_, bf16[64,512]{1,0:T(8,128)(2,1)S(1)} %collective-permute-done.2.refs_2_, ...), custom_call_target="tpu_custom_call" | custom-call | tf_op jit(solution)/shard_map/rotate_early/pallas_call | solution.py:437
  6.0 0.9 %collective-permute-done.refs_0_ = bf16[64,512]{1,0:T(8,128)(2,1)S(1)} collective-permute-done((bf16[64,512]{1,0:T(8,128)(2,1)}, bf16[64,512]{1,0:T(8,128)(2,1)S(1)}, u32[]{:S(2)}, u32[]{:S(2)}) %collective-permute-start) | collective-permute-done | bytes 65568 | tf_op jit(solution)/shard_map/ppermute | solution.py:385
  6.9 0.3 rotate_last.1
  7.2 2.6 %collective-permute-start.5 = (f32[4,512]{1,0:T(4,128)S(1)}, f32[4,512]{1,0:T(4,128)S(1)}, u32[]{:S(2)}, u32[]{:S(2)}) collective-permute-start(f32[4,512]{1,0:T(4,128)S(1)} %get-tuple-element.26.refs_0_), channel_id=1, source_target_pairs={{0,12},{4,8},{8,4},{12,0},{16,28},{20,24},{24,20},{28,16},{1,13},{... | collective-permute-start | bytes 24584 | tf_op jit(solution)/shard_map/ppermute | solution.py:455
  9.8 0.5 %collective-permute-start.4 = (f32[4,512]{1,0:T(4,128)S(1)}, f32[4,512]{1,0:T(4,128)S(1)}, u32[]{:S(2)}, u32[]{:S(2)}) collective-permute-start(f32[4,512]{1,0:T(4,128)S(1)} %get-tuple-element.26.refs_0_), channel_id=1, source_target_pairs={{0,4},{4,0},{8,12},{12,8},{16,20},{20,16},{24,28},{28,24},{1,5},{5... | collective-permute-start | bytes 24584 | tf_op jit(solution)/shard_map/ppermute | solution.py:455
  10.3 0.4 %collective-permute-start.3 = (f32[4,512]{1,0:T(4,128)S(1)}, f32[4,512]{1,0:T(4,128)S(1)}, u32[]{:S(2)}, u32[]{:S(2)}) collective-permute-start(f32[4,512]{1,0:T(4,128)S(1)} %get-tuple-element.26.refs_0_), channel_id=1, source_target_pairs={{0,8},{4,12},{8,0},{12,4},{16,24},{20,28},{24,16},{28,20},{1,9},{5... | collective-permute-start | bytes 24584 | tf_op jit(solution)/shard_map/ppermute | solution.py:455
  10.7 1.1 %collective-permute-done.5.refs_3_ = f32[4,512]{1,0:T(4,128)S(1)} collective-permute-done((f32[4,512]{1,0:T(4,128)S(1)}, f32[4,512]{1,0:T(4,128)S(1)}, u32[]{:S(2)}, u32[]{:S(2)}) %collective-permute-start.5) | collective-permute-done | bytes 8224 | tf_op jit(solution)/shard_map/ppermute | solution.py:455
  11.8 1.6 %collective-permute-done.4.refs_2_ = f32[4,512]{1,0:T(4,128)S(1)} collective-permute-done((f32[4,512]{1,0:T(4,128)S(1)}, f32[4,512]{1,0:T(4,128)S(1)}, u32[]{:S(2)}, u32[]{:S(2)}) %collective-permute-start.4) | collective-permute-done | bytes 8224 | tf_op jit(solution)/shard_map/ppermute | solution.py:455
  13.4 0.5 %collective-permute-done.3.refs_1_ = f32[4,512]{1,0:T(4,128)S(1)} collective-permute-done((f32[4,512]{1,0:T(4,128)S(1)}, f32[4,512]{1,0:T(4,128)S(1)}, u32[]{:S(2)}, u32[]{:S(2)}) %collective-permute-start.3) | collective-permute-done | bytes 8224 | tf_op jit(solution)/shard_map/ppermute | solution.py:455
  13.9 0.1 merge.1
  14.0 2.7 %collective-permute-start.6 = (f32[4,512]{1,0:T(4,128)S(1)}, f32[4,512]{1,0:T(4,128)S(1)}, u32[]{:S(2)}, u32[]{:S(2)}) collective-permute-start(f32[4,512]{1,0:T(4,128)S(1)} %merge.1), channel_id=1, source_target_pairs={{0,16},{4,20},{8,24},{12,28},{16,0},{20,4},{24,8},{28,12},{1,17},{... | collective-permute-start | bytes 24584 | tf_op jit(solution)/shard_map/ppermute | solution.py:466
  16.7 1.3 %local.1 = (f32[64,512]{1,0:T(8,128)S(1)}, f32[4,24,512]{2,1,0:T(8,128)S(1)}) custom-call(s32[1]{0:T(128)} %bitcast.1.me_ref, f32[64,512]{1,0:T(8,128)S(1)} %get-tuple-element.21.z_ref, f32[20,8,512]{2,1,0:T(8,128)S(1)} %get-tuple-element.22.const_ref, f32[32,512]{1,0:T(8,128)S(1)} %get-tuple-element.23.merge_ref), custom_call_target="tpu_custom_call" | custom-call | flops 10000000 | bytes 1000000 | tf_op jit(solution)/shard_map/local/pallas_call | solution.py:467
  17.9 0.7 %collective-permute-done.6.refs_4_ = f32[4,512]{1,0:T(4,128)S(1)} collective-permute-done((f32[4,512]{1,0:T(4,128)S(1)}, f32[4,512]{1,0:T(4,128)S(1)}, u32[]{:S(2)}, u32[]{:S(2)}) %collective-permute-start.6) | collective-permute-done | bytes 8224 | tf_op jit(solution)/shard_map/ppermute | solution.py:466
  18.6 0.6 %finish.1 = (bf16[64,512]{1,0:T(8,128)(2,1)S(1)}, bf16[64,512]{1,0:T(8,128)(2,1)S(1)}, bf16[64,512]{1,0:T(8,128)(2,1)S(1)}, bf16[64,512]{1,0:T(8,128)(2,1)S(1)}) custom-call(s32[1]{0:T(128)} %bitcast.place_ref, f32[64,512]{1,0:T(8,128)S(1)} %get-tuple-element.24.r_ref, f32[4,64,512]{2,1,0:T(8,128)S(1)} %get-tuple-element.20.refs_3_.w_ref, ...), custom_call_target="tpu_custom_call" | custom-call | tf_op jit(solution)/shard_map/finish/pallas_call | solution.py:479
  19.2 1.6 %collective-permute-start.7 = (bf16[64,512]{1,0:T(8,128)(2,1)S(1)}, bf16[64,512]{1,0:T(8,128)(2,1)S(1)}, u32[]{:S(2)}, u32[]{:S(2)}) collective-permute-start(bf16[64,512]{1,0:T(8,128)(2,1)S(1)} %get-tuple-element.28), channel_id=1, source_target_pairs={{0,2},{1,3},{2,0},{3,1},{4,6},{5,7},{6,4},{7,5},{8,10},{9,11},{10,... | collective-permute-start | bytes 196616 | tf_op jit(solution)/shard_map/ppermute | solution.py:489
  20.9 0.0 collective-permute-start.8
  20.9 0.6 %collective-permute-start.9 = (bf16[64,512]{1,0:T(8,128)(2,1)S(1)}, bf16[64,512]{1,0:T(8,128)(2,1)S(1)}, u32[]{:S(2)}, u32[]{:S(2)}) collective-permute-start(bf16[64,512]{1,0:T(8,128)(2,1)S(1)} %get-tuple-element.30), channel_id=1, source_target_pairs={{0,1},{1,0},{2,3},{3,2},{4,5},{5,4},{6,7},{7,6},{8,9},{9,8},{10,11... | collective-permute-start | bytes 196616 | tf_op jit(solution)/shard_map/ppermute | solution.py:489
  21.4 0.3 %rest.1 = f32[64,512]{1,0:T(8,128)S(1)} custom-call(s32[1]{0:T(128)} %bitcast.place_ref, bf16[64,512]{1,0:T(8,128)(2,1)S(1)} %get-tuple-element.27.residual_ref, bf16[2048,512]{1,0:T(8,128)(2,1)S(1)} %get-tuple-element.18.refs_3_.refs_1_.basis_ref), custom_call_target="tpu_custom_call" | custom-call | flops 80000000 | bytes 1500000 | tf_op jit(solution)/shard_map/rest/pallas_call | solution.py:492
  21.7 1.8 %collective-permute-done.7 = bf16[64,512]{1,0:T(8,128)(2,1)S(1)} collective-permute-done((bf16[64,512]{1,0:T(8,128)(2,1)S(1)}, bf16[64,512]{1,0:T(8,128)(2,1)S(1)}, u32[]{:S(2)}, u32[]{:S(2)}) %collective-permute-start.7) | collective-permute-done | bytes 65568 | tf_op jit(solution)/shard_map/ppermute | solution.py:489
  23.6 1.4 %collective-permute-done.8 = bf16[64,512]{1,0:T(8,128)(2,1)S(1)} collective-permute-done((bf16[64,512]{1,0:T(8,128)(2,1)S(1)}, bf16[64,512]{1,0:T(8,128)(2,1)S(1)}, u32[]{:S(2)}, u32[]{:S(2)}) %collective-permute-start.8) | collective-permute-done | bytes 65568 | tf_op jit(solution)/shard_map/ppermute | solution.py:489
  25.0 0.0 collective-permute-done.9
  25.0 0.7 %convert_add_fusion = f32[64,512]{1,0:T(8,128)} fusion(bf16[64,512]{1,0:T(8,128)(2,1)S(1)} %collective-permute-done.9, bf16[64,512]{1,0:T(8,128)(2,1)S(1)} %collective-permute-done.8, f32[64,512]{1,0:T(8,128)S(1)} %rest.1, bf16[64,512]{1,0:T(8,128)(2,1)S(1)} %collective-permute-done.7), kind=kLoop, calls=%fused_computation | loop fusion | flops 196608 | bytes 458752 | tf_op jit(solution)/shard_map/add | solution.py:502
Async XLA Ops:
  0.0 5.6 %collective-permute-start.2 = (bf16[64,512]{1,0:T(8,128)(2,1)}, bf16[64,512]{1,0:T(8,128)(2,1)S(1)}, u32[]{:S(2)}, u32[]{:S(2)}) collective-permute-start(bf16[64,512]{1,0:T(8,128)(2,1)} %refs_2_.1), channel_id=1, source_target_pairs={{0,2},{1,3},{2,0},{3,1},{4,6},{5,7},{6,4},{7,5},{8,10},{9,11},{10,... | collective-permute-start | bytes 196616 | tf_op jit(solution)/shard_map/ppermute | solution.py:385
  3.0 2.6 %collective-permute-start.1 = (bf16[64,512]{1,0:T(8,128)(2,1)}, bf16[64,512]{1,0:T(8,128)(2,1)S(1)}, u32[]{:S(2)}, u32[]{:S(2)}) collective-permute-start(bf16[64,512]{1,0:T(8,128)(2,1)} %refs_2_.1), channel_id=1, source_target_pairs={{0,1},{1,0},{2,3},{3,2},{4,5},{5,4},{6,7},{7,6},{8,9},{9,8},{10,11... | collective-permute-start | bytes 196616 | tf_op jit(solution)/shard_map/ppermute | solution.py:385
  3.0 4.0 %collective-permute-start = (bf16[64,512]{1,0:T(8,128)(2,1)}, bf16[64,512]{1,0:T(8,128)(2,1)S(1)}, u32[]{:S(2)}, u32[]{:S(2)}) collective-permute-start(bf16[64,512]{1,0:T(8,128)(2,1)} %refs_2_.1), channel_id=1, source_target_pairs={{0,3},{1,2},{2,1},{3,0},{4,7},{5,6},{6,5},{7,4},{8,11},{9,10},{10,... | collective-permute-start | bytes 196616 | tf_op jit(solution)/shard_map/ppermute | solution.py:385
  7.2 4.6 %collective-permute-start.5 = (f32[4,512]{1,0:T(4,128)S(1)}, f32[4,512]{1,0:T(4,128)S(1)}, u32[]{:S(2)}, u32[]{:S(2)}) collective-permute-start(f32[4,512]{1,0:T(4,128)S(1)} %get-tuple-element.26.refs_0_), channel_id=1, source_target_pairs={{0,12},{4,8},{8,4},{12,0},{16,28},{20,24},{24,20},{28,16},{1,13},{... | collective-permute-start | bytes 24584 | tf_op jit(solution)/shard_map/ppermute | solution.py:455
  9.8 3.7 %collective-permute-start.4 = (f32[4,512]{1,0:T(4,128)S(1)}, f32[4,512]{1,0:T(4,128)S(1)}, u32[]{:S(2)}, u32[]{:S(2)}) collective-permute-start(f32[4,512]{1,0:T(4,128)S(1)} %get-tuple-element.26.refs_0_), channel_id=1, source_target_pairs={{0,4},{4,0},{8,12},{12,8},{16,20},{20,16},{24,28},{28,24},{1,5},{5... | collective-permute-start | bytes 24584 | tf_op jit(solution)/shard_map/ppermute | solution.py:455
  10.3 3.7 %collective-permute-start.3 = (f32[4,512]{1,0:T(4,128)S(1)}, f32[4,512]{1,0:T(4,128)S(1)}, u32[]{:S(2)}, u32[]{:S(2)}) collective-permute-start(f32[4,512]{1,0:T(4,128)S(1)} %get-tuple-element.26.refs_0_), channel_id=1, source_target_pairs={{0,8},{4,12},{8,0},{12,4},{16,24},{20,28},{24,16},{28,20},{1,9},{5... | collective-permute-start | bytes 24584 | tf_op jit(solution)/shard_map/ppermute | solution.py:455
  14.0 4.6 %collective-permute-start.6 = (f32[4,512]{1,0:T(4,128)S(1)}, f32[4,512]{1,0:T(4,128)S(1)}, u32[]{:S(2)}, u32[]{:S(2)}) collective-permute-start(f32[4,512]{1,0:T(4,128)S(1)} %merge.1), channel_id=1, source_target_pairs={{0,16},{4,20},{8,24},{12,28},{16,0},{20,4},{24,8},{28,12},{1,17},{... | collective-permute-start | bytes 24584 | tf_op jit(solution)/shard_map/ppermute | solution.py:466
  19.2 4.3 %collective-permute-start.7 = (bf16[64,512]{1,0:T(8,128)(2,1)S(1)}, bf16[64,512]{1,0:T(8,128)(2,1)S(1)}, u32[]{:S(2)}, u32[]{:S(2)}) collective-permute-start(bf16[64,512]{1,0:T(8,128)(2,1)S(1)} %get-tuple-element.28), channel_id=1, source_target_pairs={{0,2},{1,3},{2,0},{3,1},{4,6},{5,7},{6,4},{7,5},{8,10},{9,11},{10,... | collective-permute-start | bytes 196616 | tf_op jit(solution)/shard_map/ppermute | solution.py:489
  20.9 4.1 %collective-permute-start.8 = (bf16[64,512]{1,0:T(8,128)(2,1)S(1)}, bf16[64,512]{1,0:T(8,128)(2,1)S(1)}, u32[]{:S(2)}, u32[]{:S(2)}) collective-permute-start(bf16[64,512]{1,0:T(8,128)(2,1)S(1)} %get-tuple-element.29), channel_id=1, source_target_pairs={{0,3},{1,2},{2,1},{3,0},{4,7},{5,6},{6,5},{7,4},{8,11},{9,10},{10,... | collective-permute-start | bytes 196616 | tf_op jit(solution)/shard_map/ppermute | solution.py:489
  20.9 4.1 %collective-permute-start.9 = (bf16[64,512]{1,0:T(8,128)(2,1)S(1)}, bf16[64,512]{1,0:T(8,128)(2,1)S(1)}, u32[]{:S(2)}, u32[]{:S(2)}) collective-permute-start(bf16[64,512]{1,0:T(8,128)(2,1)S(1)} %get-tuple-element.30), channel_id=1, source_target_pairs={{0,1},{1,0},{2,3},{3,2},{4,5},{5,4},{6,7},{7,6},{8,9},{9,8},{10,11... | collective-permute-start | bytes 196616 | tf_op jit(solution)/shard_map/ppermute | solution.py:489

commit v5 on v4

--- a/solution.py
+++ b/solution.py
@@ -10,7 +10,8 @@
 
 F32 = jnp.float32
 SUB = 8
-NEAR = (2, 1, 3)
+MIRROR, NEAR = 6, (2, 1, 3)
+GROUP = (0, MIRROR) + tuple(step ^ other for step in NEAR for other in (0, MIRROR))
 VMEM_LIMIT = 24 * 1024 * 1024
 
 
@@ -226,16 +227,26 @@
     )
 
 
+def pair_kernel(own_ref, other_ref, out_ref):
+    out_ref[0:4, :] = own_ref[...]
+    out_ref[4:8, :] = other_ref[...]
+
+
 def merge_kernel(level, me_ref, merge_ref, *refs):
-    *parts, out_ref = refs
+    *refs, out_ref = refs
     me = me_ref[0]
-    parts = [ref[...] for ref in parts]
-    if level:
-        out_ref[...] = merge(level, me, parts[0], parts[1], merge_ref)
-    else:
-        near = merge(0, me, parts[0], parts[1 + NEAR.index(1)], merge_ref)
-        far = merge(0, me, parts[1 + NEAR.index(2)], parts[1 + NEAR.index(3)], merge_ref)
-        out_ref[...] = merge(1, me, near, far, merge_ref)
+    if level > 2:
+        out_ref[...] = merge(level, me, refs[0][...], refs[1][...], merge_ref)
+        return
+    parts = {}
+    for place, step in enumerate(GROUP):
+        parts[step] = refs[place // 2][4 * (place % 2) : 4 * (place % 2) + 4, :]
+    for level, stride in enumerate((1, 2, 4)):
+        parts = {
+            step: merge(level, me ^ step, parts[step], parts[step ^ stride], merge_ref)
+            for step in range(0, 8, 2 * stride)
+        }
+    out_ref[...] = parts[0]
 
 
 def shift(value, by):
@@ -274,9 +285,11 @@
         rows = row + group * SUB
         kind = rows & 3
         line = rows >> 2
-        step = jnp.where(line == 1, NEAR[0], jnp.where(line == 2, NEAR[1], jnp.where(line == 3, NEAR[2], 0)))
-        span = jnp.where(line < 4, 1, jnp.left_shift(1, jnp.maximum(line - 2, 0)))
-        near_me = mine ^ jnp.where(line < 4, step, span)
+        step = jnp.zeros_like(line)
+        for place, offset in enumerate(GROUP):
+            step = jnp.where(line == place, offset, step)
+        span = jnp.where(line < 8, 1, jnp.left_shift(1, jnp.maximum(line - 5, 0)))
+        near_me = mine ^ jnp.where(line < 8, step, span)
         front = jnp.minimum((near_me // span) * span, blocks - 1)
         back = jnp.minimum(front + span - 1, blocks - 1)
         before, after = back < me, front > me
@@ -364,11 +377,15 @@
     *sums, residual_ref = refs[: -len(pieces)]
     value = r_ref[...]
     for line in range(4):
-        total = None
-        for place, sum_ref in enumerate(sums):
-            term = g_ref[line, pl.ds(4 * place, 4), :] * sum_ref[...]
-            total = term if total is None else total + term
-        value = value - w_ref[line] * jnp.sum(total, axis=0, keepdims=True)
+        total, place = 0.0, 0
+        for sum_ref in sums:
+            count = sum_ref.shape[0]
+            term = g_ref[line, pl.ds(place, count), :] * sum_ref[...]
+            total = total + jnp.sum(term, axis=0, keepdims=True) if count < SUB else total + term
+            place += count
+            if place == 4 * len(GROUP):
+                total = jnp.sum(total, axis=0, keepdims=True)
+        value = value - w_ref[line] * total
     scale = const_ref[19, 0:1, :]
     residual = (value * scale).astype(jnp.bfloat16)
     residual_ref[...] = residual
@@ -450,23 +467,31 @@
         compiler_params=params,
         name="rotate_last",
     )(place, obs[last], basis, z, w)
-    sums = [summary]
+    pair = pl.pallas_call(
+        pair_kernel,
+        out_shape=shape(8, width),
+        in_specs=[vmem] * 2,
+        out_specs=vmem,
+        compiler_params=params,
+        name="pair",
+    )(summary, lax.ppermute(summary, "tm", [(a, a ^ MIRROR) for a in range(blocks)]))
+    sums = [pair]
     for step in NEAR:
-        sums.append(lax.ppermute(summary, "tm", [(a, a ^ step) for a in range(blocks)]))
-    for level in range(2, rounds):
+        sums.append(lax.ppermute(pair, "tm", [(a, a ^ step) for a in range(blocks)]))
+    for level in range(3, rounds):
         summary = pl.pallas_call(
-            functools.partial(merge_kernel, 0 if level == 2 else level - 1),
+            functools.partial(merge_kernel, level - 1),
             out_shape=shape(4, width),
-            in_specs=[smem] + [vmem] * (5 if level == 2 else 3),
+            in_specs=[smem] + [vmem] * (5 if level == 3 else 3),
             out_specs=vmem,
             compiler_params=params,
             name="merge",
-        )(me, merges, *(sums if level == 2 else (summary, sums[-1])))
+        )(me, merges, *(sums if level == 3 else (summary, sums[-1])))
         step = 1 << level
         sums.append(lax.ppermute(summary, "tm", [(a, a ^ step) for a in range(blocks)]))
     local, g = pl.pallas_call(
         functools.partial(local_kernel, blocks),
-        out_shape=(shape(steps, width), shape(4, -(-4 * (rounds + 2) // SUB) * SUB, width)),
+        out_shape=(shape(steps, width), shape(4, -(-4 * (rounds + 5) // SUB) * SUB, width)),
         in_specs=[smem] + [vmem] * 3,
         out_specs=(vmem,) * 2,
         scratch_shapes=[pltpu.VMEM((width // 128, steps, 128), F32)],

time: 25.8 us -> 25.2 us (0.977)
  waiting for transfers between devices: 8.25 us -> 6.36 us
  starting transfers between devices: 11.5 us -> 12.4 us
  Pallas kernels: 4.53 us -> 4.79 us
    ppermute x4, waiting for transfers between devices: 3.9 us -> 2.01 us  [the longest x1 1.85 us: shards(): lax.ppermute(summary, 'tm', [(a, a ^ MIRROR) for a in range(blocks)])]
    ppermute x4, starting transfers between devices: 6.21 us -> 7.16 us  [the longest x1 3.67 us: shards(): lax.ppermute(summary, 'tm', [(a, a ^ MIRROR) for a in range(blocks)])]
    pallas_call x1, Pallas kernels: 1.26 us -> 1.57 us  [shards(): pl.pallas_call(functools.partial(local_kernel, blocks), out_shape=(shape(...]
  transfers between devices with their start and end apart: 10 -> 10, of which waited for: 8 -> 6; matrix products, arithmetic and copies ran while one was open for 0% -> 0% of each run, Pallas kernels for 14% -> 16%
where the time goes in v5:
time: 25.2 us; the launch traced here: 25 us
  starting transfers between devices  12.4 us (49%)
  waiting for transfers between devices  6.36 us (25%)
  Pallas kernels  4.79 us (19%)
  between operations  0.7 us (3%)
  other arithmetic  0.69 us (3%)
    ppermute x1, starting transfers between devices, shards(): lax.ppermute(summary, 'tm', [(a, a ^ MIRROR) for a in range(blocks)])  3.67 us
    ppermute x3, starting transfers between devices, shards(): lax.ppermute(pair, 'tm', [(a, a ^ step) for a in range(blocks)])  3.49 us
    ppermute x3, waiting for transfers between devices, shards(): lax.ppermute(part, 'mode', [(a, a ^ piece) for a in range(pieces)])  3.25 us
    ppermute x3, starting transfers between devices, exchange(): out.append(lax.ppermute(value, axis, [(a, a ^ step) for a in range(count)]))  3.08 us
    ppermute x3, starting transfers between devices, shards(): lax.ppermute(part, 'mode', [(a, a ^ piece) for a in range(pieces)])  2.2 us
    ppermute x1, waiting for transfers between devices, shards(): lax.ppermute(summary, 'tm', [(a, a ^ MIRROR) for a in range(blocks)])  1.85 us
    pallas_call x1, Pallas kernels, shards(): pl.pallas_call(functools.partial(coefficients_kernel, blocks), out_shape=...  1.7 us
    pallas_call x1, Pallas kernels, shards(): pl.pallas_call(functools.partial(local_kernel, blocks), out_shape=(shape(...  1.57 us
  transfers between devices with their start and end apart: 10, of which 6 were waited for; matrix products, arithmetic and copies ran while one was open for 0% of the time, Pallas kernels for 16%

profile of v5, /device:TPU:0, one launch (start us, length us, event | category | flops | bytes accessed | tf_op | source)
XLA Modules:
  0.0 25.0 jit_solution(1371036258895936351)
XLA Ops:
  0.0 3.0 %collective-permute-start.2 = (bf16[64,512]{1,0:T(8,128)(2,1)}, bf16[64,512]{1,0:T(8,128)(2,1)S(1)}, u32[]{:S(2)}, u32[]{:S(2)}) collective-permute-start(bf16[64,512]{1,0:T(8,128)(2,1)} %refs_2_.1), channel_id=1, source_target_pairs={{0,2},{1,3},{2,0},{3,1},{4,6},{5,7},{6,4},{7,5},{8,10},{9,11},{10,... | collective-permute-start | bytes 196616 | tf_op jit(solution)/shard_map/ppermute | solution.py:402
  3.0 0.0 collective-permute-start.1
  3.0 0.1 collective-permute-start
  3.7 1.7 %coefficients.1 = (f32[20,8,512]{2,1,0:T(8,128)S(1)}, f32[4,64,512]{2,1,0:T(8,128)S(1)}, f32[32,512]{1,0:T(8,128)S(1)}, bf16[2048,512]{1,0:T(8,128)(2,1)S(1)}, bf16[64,512]{1,0:T(8,128)(2,1)S(1)}) custom-call(f32[1]{0:T(128)S(6)} %copy.6.noise_ref, f32[1,512]{1,0:T(1,128)} %bitcast.4, f32[1,512]{1,0:T(1,128)} %bitcast.5, bf16[64,512]{1,0:T(8,128)(2,1)} %refs_2_.1, ...), custom_call_target="tpu_custom_call" | custom-call | flops 20000000 | bytes 2000000 | tf_op jit(solution)/shard_map/coefficients/pallas_call | solution.py:421
  5.4 0.1 collective-permute-done.2.refs_2_
  5.6 0.0 collective-permute-done.1.refs_1_
  5.6 0.4 %rotate_early.1.refs_2_ = f32[64,512]{1,0:T(8,128)S(1)} custom-call(s32[1]{0:T(128)} %bitcast.place_ref, bf16[64,512]{1,0:T(8,128)(2,1)S(1)} %get-tuple-element.19.refs_0_, bf16[64,512]{1,0:T(8,128)(2,1)S(1)} %collective-permute-done.1.refs_1_, bf16[64,512]{1,0:T(8,128)(2,1)S(1)} %collective-permute-done.2.refs_2_, ...), custom_call_target="tpu_custom_call" | custom-call | tf_op jit(solution)/shard_map/rotate_early/pallas_call | solution.py:454
  6.0 0.9 %collective-permute-done.refs_0_ = bf16[64,512]{1,0:T(8,128)(2,1)S(1)} collective-permute-done((bf16[64,512]{1,0:T(8,128)(2,1)}, bf16[64,512]{1,0:T(8,128)(2,1)S(1)}, u32[]{:S(2)}, u32[]{:S(2)}) %collective-permute-start) | collective-permute-done | bytes 65568 | tf_op jit(solution)/shard_map/ppermute | solution.py:402
  6.9 0.3 %rotate_last.1 = (f32[64,512]{1,0:T(8,128)S(1)}, f32[4,512]{1,0:T(4,128)S(1)}) custom-call(s32[1]{0:T(128)} %bitcast.place_ref, bf16[64,512]{1,0:T(8,128)(2,1)S(1)} %collective-permute-done.refs_0_, bf16[2048,512]{1,0:T(8,128)(2,1)S(1)} %get-tuple-element.18.refs_3_.refs_1_.basis_ref, f32[64,512]{1,0:T(8,128)S(1)} %rotate_early.1.refs_2_, ...), custom_call_target="tpu_custom_call" | custom-call | tf_op jit(solution)/shard_map/rotate_last/pallas_call | solution.py:462
  7.2 3.7 %collective-permute-start.3 = (f32[4,512]{1,0:T(4,128)S(1)}, f32[4,512]{1,0:T(4,128)S(1)}, u32[]{:S(2)}, u32[]{:S(2)}) collective-permute-start(f32[4,512]{1,0:T(4,128)S(1)} %get-tuple-element.26.own_ref), channel_id=1, source_target_pairs={{0,24},{4,28},{8,16},{12,20},{16,8},{20,12},{24,0},{28,4},{1,25},{... | collective-permute-start | bytes 24584 | tf_op jit(solution)/shard_map/ppermute | solution.py:477
  10.9 1.8 %collective-permute-done.3.other_ref = f32[4,512]{1,0:T(4,128)S(1)} collective-permute-done((f32[4,512]{1,0:T(4,128)S(1)}, f32[4,512]{1,0:T(4,128)S(1)}, u32[]{:S(2)}, u32[]{:S(2)}) %collective-permute-start.3) | collective-permute-done | bytes 8224 | tf_op jit(solution)/shard_map/ppermute | solution.py:477
  12.7 0.7 %collective-permute-start.6 = (f32[8,512]{1,0:T(8,128)S(1)}, f32[8,512]{1,0:T(8,128)S(1)}, u32[]{:S(2)}, u32[]{:S(2)}) collective-permute-start(f32[8,512]{1,0:T(8,128)S(1)} %pair.1.refs_0_), channel_id=1, source_target_pairs={{0,12},{4,8},{8,4},{12,0},{16,28},{20,24},{24,20},{28,16},{1,13},{... | collective-permute-start | bytes 49160 | tf_op jit(solution)/shard_map/ppermute | solution.py:480
  13.4 0.8 %collective-permute-start.5 = (f32[8,512]{1,0:T(8,128)S(1)}, f32[8,512]{1,0:T(8,128)S(1)}, u32[]{:S(2)}, u32[]{:S(2)}) collective-permute-start(f32[8,512]{1,0:T(8,128)S(1)} %pair.1.refs_0_), channel_id=1, source_target_pairs={{0,4},{4,0},{8,12},{12,8},{16,20},{20,16},{24,28},{28,24},{1,5},{5... | collective-permute-start | bytes 49160 | tf_op jit(solution)/shard_map/ppermute | solution.py:480
  14.2 2.0 %collective-permute-start.4 = (f32[8,512]{1,0:T(8,128)S(1)}, f32[8,512]{1,0:T(8,128)S(1)}, u32[]{:S(2)}, u32[]{:S(2)}) collective-permute-start(f32[8,512]{1,0:T(8,128)S(1)} %pair.1.refs_0_), channel_id=1, source_target_pairs={{0,8},{4,12},{8,0},{12,4},{16,24},{20,28},{24,16},{28,20},{1,9},{5... | collective-permute-start | bytes 49160 | tf_op jit(solution)/shard_map/ppermute | solution.py:480
  16.2 1.6 %local.1 = (f32[64,512]{1,0:T(8,128)S(1)}, f32[4,32,512]{2,1,0:T(8,128)S(1)}) custom-call(s32[1]{0:T(128)} %bitcast.1.me_ref, f32[64,512]{1,0:T(8,128)S(1)} %get-tuple-element.21.z_ref, f32[20,8,512]{2,1,0:T(8,128)S(1)} %get-tuple-element.22.const_ref, f32[32,512]{1,0:T(8,128)S(1)} %get-tuple-element.23.merge_ref), custom_call_target="tpu_custom_call" | custom-call | flops 10000000 | bytes 1000000 | tf_op jit(solution)/shard_map/local/pallas_call | solution.py:492
  17.8 0.0 collective-permute-done.6.refs_3_
  17.8 0.0 collective-permute-done.5.refs_2_
  17.8 0.2 collective-permute-done.4.refs_1_
  17.9 0.6 %finish.1 = (bf16[64,512]{1,0:T(8,128)(2,1)S(1)}, bf16[64,512]{1,0:T(8,128)(2,1)S(1)}, bf16[64,512]{1,0:T(8,128)(2,1)S(1)}, bf16[64,512]{1,0:T(8,128)(2,1)S(1)}) custom-call(s32[1]{0:T(128)} %bitcast.place_ref, f32[64,512]{1,0:T(8,128)S(1)} %get-tuple-element.24.r_ref, f32[4,64,512]{2,1,0:T(8,128)S(1)} %get-tuple-element.20.refs_3_.w_ref, ...), custom_call_target="tpu_custom_call" | custom-call | tf_op jit(solution)/shard_map/finish/pallas_call | solution.py:504
  18.5 1.6 %collective-permute-start.7 = (bf16[64,512]{1,0:T(8,128)(2,1)S(1)}, bf16[64,512]{1,0:T(8,128)(2,1)S(1)}, u32[]{:S(2)}, u32[]{:S(2)}) collective-permute-start(bf16[64,512]{1,0:T(8,128)(2,1)S(1)} %get-tuple-element.28), channel_id=1, source_target_pairs={{0,2},{1,3},{2,0},{3,1},{4,6},{5,7},{6,4},{7,5},{8,10},{9,11},{10,... | collective-permute-start | bytes 196616 | tf_op jit(solution)/shard_map/ppermute | solution.py:514
  20.2 0.0 collective-permute-start.8
  20.2 0.6 %collective-permute-start.9 = (bf16[64,512]{1,0:T(8,128)(2,1)S(1)}, bf16[64,512]{1,0:T(8,128)(2,1)S(1)}, u32[]{:S(2)}, u32[]{:S(2)}) collective-permute-start(bf16[64,512]{1,0:T(8,128)(2,1)S(1)} %get-tuple-element.30), channel_id=1, source_target_pairs={{0,1},{1,0},{2,3},{3,2},{4,5},{5,4},{6,7},{7,6},{8,9},{9,8},{10,11... | collective-permute-start | bytes 196616 | tf_op jit(solution)/shard_map/ppermute | solution.py:514
  20.8 0.3 %rest.1 = f32[64,512]{1,0:T(8,128)S(1)} custom-call(s32[1]{0:T(128)} %bitcast.place_ref, bf16[64,512]{1,0:T(8,128)(2,1)S(1)} %get-tuple-element.27.residual_ref, bf16[2048,512]{1,0:T(8,128)(2,1)S(1)} %get-tuple-element.18.refs_3_.refs_1_.basis_ref), custom_call_target="tpu_custom_call" | custom-call | flops 80000000 | bytes 1500000 | tf_op jit(solution)/shard_map/rest/pallas_call | solution.py:517
  21.0 1.8 %collective-permute-done.7 = bf16[64,512]{1,0:T(8,128)(2,1)S(1)} collective-permute-done((bf16[64,512]{1,0:T(8,128)(2,1)S(1)}, bf16[64,512]{1,0:T(8,128)(2,1)S(1)}, u32[]{:S(2)}, u32[]{:S(2)}) %collective-permute-start.7) | collective-permute-done | bytes 65568 | tf_op jit(solution)/shard_map/ppermute | solution.py:514
  22.9 1.4 %collective-permute-done.8 = bf16[64,512]{1,0:T(8,128)(2,1)S(1)} collective-permute-done((bf16[64,512]{1,0:T(8,128)(2,1)S(1)}, bf16[64,512]{1,0:T(8,128)(2,1)S(1)}, u32[]{:S(2)}, u32[]{:S(2)}) %collective-permute-start.8) | collective-permute-done | bytes 65568 | tf_op jit(solution)/shard_map/ppermute | solution.py:514
  24.3 0.0 collective-permute-done.9
  24.3 0.7 %convert_add_fusion = f32[64,512]{1,0:T(8,128)} fusion(bf16[64,512]{1,0:T(8,128)(2,1)S(1)} %collective-permute-done.9, bf16[64,512]{1,0:T(8,128)(2,1)S(1)} %collective-permute-done.8, f32[64,512]{1,0:T(8,128)S(1)} %rest.1, bf16[64,512]{1,0:T(8,128)(2,1)S(1)} %collective-permute-done.7), kind=kLoop, calls=%fused_computation | loop fusion | flops 196608 | bytes 458752 | tf_op jit(solution)/shard_map/add | solution.py:527
  (1 shorter events, 0.0 us)
Async XLA Ops:
  0.0 5.6 %collective-permute-start.2 = (bf16[64,512]{1,0:T(8,128)(2,1)}, bf16[64,512]{1,0:T(8,128)(2,1)S(1)}, u32[]{:S(2)}, u32[]{:S(2)}) collective-permute-start(bf16[64,512]{1,0:T(8,128)(2,1)} %refs_2_.1), channel_id=1, source_target_pairs={{0,2},{1,3},{2,0},{3,1},{4,6},{5,7},{6,4},{7,5},{8,10},{9,11},{10,... | collective-permute-start | bytes 196616 | tf_op jit(solution)/shard_map/ppermute | solution.py:402
  3.0 2.6 %collective-permute-start.1 = (bf16[64,512]{1,0:T(8,128)(2,1)}, bf16[64,512]{1,0:T(8,128)(2,1)S(1)}, u32[]{:S(2)}, u32[]{:S(2)}) collective-permute-start(bf16[64,512]{1,0:T(8,128)(2,1)} %refs_2_.1), channel_id=1, source_target_pairs={{0,1},{1,0},{2,3},{3,2},{4,5},{5,4},{6,7},{7,6},{8,9},{9,8},{10,11... | collective-permute-start | bytes 196616 | tf_op jit(solution)/shard_map/ppermute | solution.py:402
  3.0 4.0 %collective-permute-start = (bf16[64,512]{1,0:T(8,128)(2,1)}, bf16[64,512]{1,0:T(8,128)(2,1)S(1)}, u32[]{:S(2)}, u32[]{:S(2)}) collective-permute-start(bf16[64,512]{1,0:T(8,128)(2,1)} %refs_2_.1), channel_id=1, source_target_pairs={{0,3},{1,2},{2,1},{3,0},{4,7},{5,6},{6,5},{7,4},{8,11},{9,10},{10,... | collective-permute-start | bytes 196616 | tf_op jit(solution)/shard_map/ppermute | solution.py:402
  7.2 5.5 %collective-permute-start.3 = (f32[4,512]{1,0:T(4,128)S(1)}, f32[4,512]{1,0:T(4,128)S(1)}, u32[]{:S(2)}, u32[]{:S(2)}) collective-permute-start(f32[4,512]{1,0:T(4,128)S(1)} %get-tuple-element.26.own_ref), channel_id=1, source_target_pairs={{0,24},{4,28},{8,16},{12,20},{16,8},{20,12},{24,0},{28,4},{1,25},{... | collective-permute-start | bytes 24584 | tf_op jit(solution)/shard_map/ppermute | solution.py:477
  12.7 5.1 %collective-permute-start.6 = (f32[8,512]{1,0:T(8,128)S(1)}, f32[8,512]{1,0:T(8,128)S(1)}, u32[]{:S(2)}, u32[]{:S(2)}) collective-permute-start(f32[8,512]{1,0:T(8,128)S(1)} %pair.1.refs_0_), channel_id=1, source_target_pairs={{0,12},{4,8},{8,4},{12,0},{16,28},{20,24},{24,20},{28,16},{1,13},{... | collective-permute-start | bytes 49160 | tf_op jit(solution)/shard_map/ppermute | solution.py:480
  13.4 4.4 %collective-permute-start.5 = (f32[8,512]{1,0:T(8,128)S(1)}, f32[8,512]{1,0:T(8,128)S(1)}, u32[]{:S(2)}, u32[]{:S(2)}) collective-permute-start(f32[8,512]{1,0:T(8,128)S(1)} %pair.1.refs_0_), channel_id=1, source_target_pairs={{0,4},{4,0},{8,12},{12,8},{16,20},{20,16},{24,28},{28,24},{1,5},{5... | collective-permute-start | bytes 49160 | tf_op jit(solution)/shard_map/ppermute | solution.py:480
  14.2 3.7 %collective-permute-start.4 = (f32[8,512]{1,0:T(8,128)S(1)}, f32[8,512]{1,0:T(8,128)S(1)}, u32[]{:S(2)}, u32[]{:S(2)}) collective-permute-start(f32[8,512]{1,0:T(8,128)S(1)} %pair.1.refs_0_), channel_id=1, source_target_pairs={{0,8},{4,12},{8,0},{12,4},{16,24},{20,28},{24,16},{28,20},{1,9},{5... | collective-permute-start | bytes 49160 | tf_op jit(solution)/shard_map/ppermute | solution.py:480
  18.5 4.3 %collective-permute-start.7 = (bf16[64,512]{1,0:T(8,128)(2,1)S(1)}, bf16[64,512]{1,0:T(8,128)(2,1)S(1)}, u32[]{:S(2)}, u32[]{:S(2)}) collective-permute-start(bf16[64,512]{1,0:T(8,128)(2,1)S(1)} %get-tuple-element.28), channel_id=1, source_target_pairs={{0,2},{1,3},{2,0},{3,1},{4,6},{5,7},{6,4},{7,5},{8,10},{9,11},{10,... | collective-permute-start | bytes 196616 | tf_op jit(solution)/shard_map/ppermute | solution.py:514
  20.2 4.1 %collective-permute-start.8 = (bf16[64,512]{1,0:T(8,128)(2,1)S(1)}, bf16[64,512]{1,0:T(8,128)(2,1)S(1)}, u32[]{:S(2)}, u32[]{:S(2)}) collective-permute-start(bf16[64,512]{1,0:T(8,128)(2,1)S(1)} %get-tuple-element.29), channel_id=1, source_target_pairs={{0,3},{1,2},{2,1},{3,0},{4,7},{5,6},{6,5},{7,4},{8,11},{9,10},{10,... | collective-permute-start | bytes 196616 | tf_op jit(solution)/shard_map/ppermute | solution.py:514
  20.2 4.1 %collective-permute-start.9 = (bf16[64,512]{1,0:T(8,128)(2,1)S(1)}, bf16[64,512]{1,0:T(8,128)(2,1)S(1)}, u32[]{:S(2)}, u32[]{:S(2)}) collective-permute-start(bf16[64,512]{1,0:T(8,128)(2,1)S(1)} %get-tuple-element.30), channel_id=1, source_target_pairs={{0,1},{1,0},{2,3},{3,2},{4,5},{5,4},{6,7},{7,6},{8,9},{9,8},{10,11... | collective-permute-start | bytes 196616 | tf_op jit(solution)/shard_map/ppermute | solution.py:514

commit v6 on v5

--- a/solution.py
+++ b/solution.py
@@ -10,7 +10,7 @@
 
 F32 = jnp.float32
 SUB = 8
-MIRROR, NEAR = 6, (2, 1, 3)
+MIRROR, NEAR = 6, (3, 1, 2)
 GROUP = (0, MIRROR) + tuple(step ^ other for step in NEAR for other in (0, MIRROR))
 VMEM_LIMIT = 24 * 1024 * 1024
 
@@ -188,18 +188,18 @@
 
 
 def rotate_kernel(first, place_ref, *refs):
-    pieces, others = first
+    pieces, stage = first
     obs_refs, (basis_ref, *refs) = refs[: len(pieces)], refs[len(pieces) :]
     depth = obs_refs[0].shape[1]
-    z = None if others is None else refs[0][...]
+    z = refs[0][...] if stage else None
     for piece, obs_ref in zip(pieces, obs_refs):
         begin = pl.multiple_of((place_ref[0] ^ piece) * depth, depth)
         term = jnp.dot(
             obs_ref[...], basis_ref[pl.ds(begin, depth), :], preferred_element_type=F32
         )
         z = term if z is None else z + term
-    if others is None:
-        refs[0][...] = z
+    if stage < 2:
+        refs[-1][...] = z
         return
     _, w_ref, z_ref, sum_ref = refs
     z_ref[...] = z
@@ -450,23 +450,25 @@
         ),
     )
     last = pieces - 1
-    early = list(range(last))
-    z = pl.pallas_call(
-        functools.partial(rotate_kernel, (early, None)),
-        out_shape=shape(steps, width),
-        in_specs=[smem] + [vmem] * pieces,
-        out_specs=vmem,
-        compiler_params=params,
-        name="rotate_early",
-    )(place, *(obs[piece] for piece in early), basis)
+    z = ()
+    for stage, group in enumerate(([0], list(range(last - 1, 0, -1)))):
+        z = pl.pallas_call(
+            functools.partial(rotate_kernel, (group, stage)),
+            out_shape=shape(steps, width),
+            in_specs=[smem] + [vmem] * (len(group) + 1 + len(z)),
+            out_specs=vmem,
+            compiler_params=params,
+            name="rotate_early",
+        )(place, *(obs[piece] for piece in group), basis, *z)
+        z = (z,)
     z, summary = pl.pallas_call(
-        functools.partial(rotate_kernel, ([last], early)),
+        functools.partial(rotate_kernel, ([last], 2)),
         out_shape=(shape(steps, width), shape(4, width)),
         in_specs=[smem] + [vmem] * 4,
         out_specs=(vmem,) * 2,
         compiler_params=params,
         name="rotate_last",
-    )(place, obs[last], basis, z, w)
+    )(place, obs[last], basis, *z, w)
     pair = pl.pallas_call(
         pair_kernel,
         out_shape=shape(8, width),
@@ -499,33 +501,30 @@
         cost_estimate=pl.CostEstimate(flops=10000000, bytes_accessed=1000000, transcendentals=0),
         name="local",
     )(me, z, const, merges)
-    far = list(range(2, pieces)) + [1]
-    near = [0]
-    residual, *parts = pl.pallas_call(
-        functools.partial(finish_kernel, far),
+    residual, part_y, part_d = pl.pallas_call(
+        functools.partial(finish_kernel, [2, 3]),
         out_shape=(shape(steps, width, dtype=jnp.bfloat16),)
-        + (shape(steps, depth, dtype=jnp.bfloat16),) * len(far),
+        + (shape(steps, depth, dtype=jnp.bfloat16),) * 2,
         in_specs=[smem] + [vmem] * (5 + len(sums)),
-        out_specs=(vmem,) * (1 + len(far)),
+        out_specs=(vmem,) * 3,
         compiler_params=params,
         name="finish",
     )(place, local, w, g, const, basis, *sums)
-    arrived = [
+    from_y, from_d = (
         lax.ppermute(part, "mode", [(a, a ^ piece) for a in range(pieces)])
-        for piece, part in zip(far, parts)
-    ]
-    grad_obs = pl.pallas_call(
-        functools.partial(rest_kernel, near),
-        out_shape=shape(steps, depth),
+        for piece, part in ((2, part_y), (3, part_d))
+    )
+    own, part_m = pl.pallas_call(
+        functools.partial(rest_kernel, [0, 1]),
+        out_shape=(shape(steps, depth), shape(steps, depth, dtype=jnp.bfloat16)),
         in_specs=[smem] + [vmem] * 2,
-        out_specs=vmem,
+        out_specs=(vmem,) * 2,
         compiler_params=params,
-        cost_estimate=pl.CostEstimate(flops=80000000, bytes_accessed=1500000, transcendentals=0),
         name="rest",
     )(place, residual, basis)
-    for part in arrived:
-        grad_obs = grad_obs + part.astype(F32)
-    return grad_obs
+    from_m = lax.ppermute(part_m, "mode", [(a, a ^ 1) for a in range(pieces)])
+    own, from_y, from_d, from_m = (v.astype(F32) for v in (own, from_y, from_d, from_m))
+    return (own + from_m) + (from_d + from_y)
 
 
 def solution(mesh):

time: 25.2 us -> 25.2 us (level)
  waiting for transfers between devices: 6.36 us -> 5.98 us
    ppermute x0 -> x1, starting transfers between devices: none -> 0.72 us  [shards(): from_m = lax.ppermute(part_m, 'mode', [(a, a ^ 1) for a in range(pieces)])]
    ppermute x3 -> x2, starting transfers between devices: 2.2 us -> 1.55 us  [shards(): lax.ppermute(part, 'mode', [(a, a ^ piece) for a in range(pieces)])]
    ppermute x3 -> x2, waiting for transfers between devices: 3.25 us -> 3.02 us  [shards(): lax.ppermute(part, 'mode', [(a, a ^ piece) for a in range(pieces)])]
    pallas_call x4 -> x5, Pallas kernels: 1.51 us -> 1.64 us  [the longest x2 0.5 us: shards(): pl.pallas_call(functools.partial(rotate_kernel, (group, stage)), out_shap...]
  transfers between devices with their start and end apart: 10 -> 10, of which waited for: 6 -> 5; matrix products, arithmetic and copies ran while one was open for 0% -> 0% of each run, Pallas kernels for 16% -> 17%
where the time goes in v6:
time: 25.2 us; the launch traced here: 24.8 us
  starting transfers between devices  12.5 us (50%)
  waiting for transfers between devices  5.98 us (24%)
  Pallas kernels  4.92 us (20%)
  between operations  0.72 us (3%)
  other arithmetic  0.68 us (3%)
    ppermute x1, starting transfers between devices, shards(): lax.ppermute(summary, 'tm', [(a, a ^ MIRROR) for a in range(blocks)])  3.67 us
    ppermute x3, starting transfers between devices, shards(): lax.ppermute(pair, 'tm', [(a, a ^ step) for a in range(blocks)])  3.49 us
    ppermute x3, starting transfers between devices, exchange(): out.append(lax.ppermute(value, axis, [(a, a ^ step) for a in range(count)]))  3.08 us
    ppermute x2, waiting for transfers between devices, shards(): lax.ppermute(part, 'mode', [(a, a ^ piece) for a in range(pieces)])  3.02 us
    ppermute x1, waiting for transfers between devices, shards(): lax.ppermute(summary, 'tm', [(a, a ^ MIRROR) for a in range(blocks)])  1.85 us
    pallas_call x1, Pallas kernels, shards(): pl.pallas_call(functools.partial(coefficients_kernel, blocks), out_shape=...  1.7 us
    pallas_call x1, Pallas kernels, shards(): pl.pallas_call(functools.partial(local_kernel, blocks), out_shape=(shape(...  1.57 us
    ppermute x2, starting transfers between devices, shards(): lax.ppermute(part, 'mode', [(a, a ^ piece) for a in range(pieces)])  1.55 us
  transfers between devices with their start and end apart: 10, of which 5 were waited for; matrix products, arithmetic and copies ran while one was open for 0% of the time, Pallas kernels for 17%

profile of v6, /device:TPU:0, one launch (start us, length us, event | category | flops | bytes accessed | tf_op | source)
XLA Modules:
  0.0 24.8 jit_solution(10100724550962364150)
XLA Ops:
  0.0 3.0 %collective-permute-start.1 = (bf16[64,512]{1,0:T(8,128)(2,1)}, bf16[64,512]{1,0:T(8,128)(2,1)S(1)}, u32[]{:S(2)}, u32[]{:S(2)}) collective-permute-start(bf16[64,512]{1,0:T(8,128)(2,1)} %refs_2_.1), channel_id=1, source_target_pairs={{0,2},{1,3},{2,0},{3,1},{4,6},{5,7},{6,4},{7,5},{8,10},{9,11},{10,... | collective-permute-start | bytes 196616 | tf_op jit(solution)/shard_map/ppermute | solution.py:402
  3.0 0.0 collective-permute-start.2
  3.0 0.1 collective-permute-start
  3.7 1.7 %coefficients.1 = (f32[20,8,512]{2,1,0:T(8,128)S(1)}, f32[4,64,512]{2,1,0:T(8,128)S(1)}, f32[32,512]{1,0:T(8,128)S(1)}, bf16[2048,512]{1,0:T(8,128)(2,1)S(1)}, bf16[64,512]{1,0:T(8,128)(2,1)S(1)}) custom-call(f32[1]{0:T(128)S(6)} %copy.6.noise_ref, f32[1,512]{1,0:T(1,128)} %bitcast.4, f32[1,512]{1,0:T(1,128)} %bitcast.5, bf16[64,512]{1,0:T(8,128)(2,1)} %refs_2_.1, ...), custom_call_target="tpu_custom_call" | custom-call | flops 20000000 | bytes 2000000 | tf_op jit(solution)/shard_map/coefficients/pallas_call | solution.py:421
  5.4 0.2 rotate_early.2.refs_3_
  5.7 0.0 collective-permute-done.1.refs_0_
  5.7 0.0 collective-permute-done.2.refs_1_
  5.7 0.3 %rotate_early.3.refs_2_ = f32[64,512]{1,0:T(8,128)S(1)} custom-call(s32[1]{0:T(128)} %bitcast.place_ref, bf16[64,512]{1,0:T(8,128)(2,1)S(1)} %collective-permute-done.1.refs_0_, bf16[64,512]{1,0:T(8,128)(2,1)S(1)} %collective-permute-done.2.refs_1_, bf16[2048,512]{1,0:T(8,128)(2,1)S(1)} %get-tuple-element.19.refs_1_.refs_2_.basis_ref, ...), custom_call_target="tpu_custom_call" | custom-call | tf_op jit(solution)/shard_map/rotate_early/pallas_call | solution.py:455
  6.0 0.9 %collective-permute-done.refs_0_ = bf16[64,512]{1,0:T(8,128)(2,1)S(1)} collective-permute-done((bf16[64,512]{1,0:T(8,128)(2,1)}, bf16[64,512]{1,0:T(8,128)(2,1)S(1)}, u32[]{:S(2)}, u32[]{:S(2)}) %collective-permute-start) | collective-permute-done | bytes 65568 | tf_op jit(solution)/shard_map/ppermute | solution.py:402
  6.9 0.3 %rotate_last.1 = (f32[64,512]{1,0:T(8,128)S(1)}, f32[4,512]{1,0:T(4,128)S(1)}) custom-call(s32[1]{0:T(128)} %bitcast.place_ref, bf16[64,512]{1,0:T(8,128)(2,1)S(1)} %collective-permute-done.refs_0_, bf16[2048,512]{1,0:T(8,128)(2,1)S(1)} %get-tuple-element.19.refs_1_.refs_2_.basis_ref, f32[64,512]{1,0:T(8,128)S(1)} %rotate_early.3.refs_2_, ...), custom_call_target="tpu_custom_call" | custom-call | tf_op jit(solution)/shard_map/rotate_last/pallas_call | solution.py:464
  7.2 3.7 %collective-permute-start.3 = (f32[4,512]{1,0:T(4,128)S(1)}, f32[4,512]{1,0:T(4,128)S(1)}, u32[]{:S(2)}, u32[]{:S(2)}) collective-permute-start(f32[4,512]{1,0:T(4,128)S(1)} %get-tuple-element.27.own_ref), channel_id=1, source_target_pairs={{0,24},{4,28},{8,16},{12,20},{16,8},{20,12},{24,0},{28,4},{1,25},{... | collective-permute-start | bytes 24584 | tf_op jit(solution)/shard_map/ppermute | solution.py:479
  10.9 1.8 %collective-permute-done.3.other_ref = f32[4,512]{1,0:T(4,128)S(1)} collective-permute-done((f32[4,512]{1,0:T(4,128)S(1)}, f32[4,512]{1,0:T(4,128)S(1)}, u32[]{:S(2)}, u32[]{:S(2)}) %collective-permute-start.3) | collective-permute-done | bytes 8224 | tf_op jit(solution)/shard_map/ppermute | solution.py:479
  12.7 0.7 %collective-permute-start.4 = (f32[8,512]{1,0:T(8,128)S(1)}, f32[8,512]{1,0:T(8,128)S(1)}, u32[]{:S(2)}, u32[]{:S(2)}) collective-permute-start(f32[8,512]{1,0:T(8,128)S(1)} %pair.1.refs_0_), channel_id=1, source_target_pairs={{0,12},{4,8},{8,4},{12,0},{16,28},{20,24},{24,20},{28,16},{1,13},{... | collective-permute-start | bytes 49160 | tf_op jit(solution)/shard_map/ppermute | solution.py:482
  13.4 0.8 %collective-permute-start.5 = (f32[8,512]{1,0:T(8,128)S(1)}, f32[8,512]{1,0:T(8,128)S(1)}, u32[]{:S(2)}, u32[]{:S(2)}) collective-permute-start(f32[8,512]{1,0:T(8,128)S(1)} %pair.1.refs_0_), channel_id=1, source_target_pairs={{0,4},{4,0},{8,12},{12,8},{16,20},{20,16},{24,28},{28,24},{1,5},{5... | collective-permute-start | bytes 49160 | tf_op jit(solution)/shard_map/ppermute | solution.py:482
  14.2 2.0 %collective-permute-start.6 = (f32[8,512]{1,0:T(8,128)S(1)}, f32[8,512]{1,0:T(8,128)S(1)}, u32[]{:S(2)}, u32[]{:S(2)}) collective-permute-start(f32[8,512]{1,0:T(8,128)S(1)} %pair.1.refs_0_), channel_id=1, source_target_pairs={{0,8},{4,12},{8,0},{12,4},{16,24},{20,28},{24,16},{28,20},{1,9},{5... | collective-permute-start | bytes 49160 | tf_op jit(solution)/shard_map/ppermute | solution.py:482
  16.2 1.6 %local.1 = (f32[64,512]{1,0:T(8,128)S(1)}, f32[4,32,512]{2,1,0:T(8,128)S(1)}) custom-call(s32[1]{0:T(128)} %bitcast.1.me_ref, f32[64,512]{1,0:T(8,128)S(1)} %get-tuple-element.22.z_ref, f32[20,8,512]{2,1,0:T(8,128)S(1)} %get-tuple-element.23.const_ref, f32[32,512]{1,0:T(8,128)S(1)} %get-tuple-element.24.merge_ref), custom_call_target="tpu_custom_call" | custom-call | flops 10000000 | bytes 1000000 | tf_op jit(solution)/shard_map/local/pallas_call | solution.py:494
  17.8 0.0 collective-permute-done.4.refs_1_
  17.8 0.0 collective-permute-done.5.refs_2_
  17.8 0.2 collective-permute-done.6.refs_3_
  17.9 0.5 %finish.1 = (bf16[64,512]{1,0:T(8,128)(2,1)S(1)}, bf16[64,512]{1,0:T(8,128)(2,1)S(1)}, bf16[64,512]{1,0:T(8,128)(2,1)S(1)}) custom-call(s32[1]{0:T(128)} %bitcast.place_ref, f32[64,512]{1,0:T(8,128)S(1)} %get-tuple-element.25.r_ref, f32[4,64,512]{2,1,0:T(8,128)S(1)} %get-tuple-element.21.refs_3_.w_ref, f32[4,32,512]{2,1,0:T(8,128)S(1)} %get-tuple-element.26.g_ref, ...), custom_call_target="tpu_custom_call" | custom-call | tf_op jit(solution)/shard_map/finish/pallas_call | solution.py:504
  18.4 1.5 %collective-permute-start.9 = (bf16[64,512]{1,0:T(8,128)(2,1)S(1)}, bf16[64,512]{1,0:T(8,128)(2,1)S(1)}, u32[]{:S(2)}, u32[]{:S(2)}) collective-permute-start(bf16[64,512]{1,0:T(8,128)(2,1)S(1)} %get-tuple-element.32), channel_id=1, source_target_pairs={{0,2},{1,3},{2,0},{3,1},{4,6},{5,7},{6,4},{7,5},{8,10},{9,11},{10,... | collective-permute-start | bytes 196616 | tf_op jit(solution)/shard_map/ppermute | solution.py:514
  19.9 0.0 collective-permute-start.8
  19.9 0.4 %rest.1 = (f32[64,512]{1,0:T(8,128)S(1)}, bf16[64,512]{1,0:T(8,128)(2,1)S(1)}) custom-call(s32[1]{0:T(128)} %bitcast.place_ref, bf16[64,512]{1,0:T(8,128)(2,1)S(1)} %get-tuple-element.28.residual_ref, bf16[2048,512]{1,0:T(8,128)(2,1)S(1)} %get-tuple-element.19.refs_1_.refs_2_.basis_ref), custom_call_target="tpu_custom_call" | custom-call | tf_op jit(solution)/shard_map/rest/pallas_call | solution.py:517
  20.4 0.7 %collective-permute-start.7 = (bf16[64,512]{1,0:T(8,128)(2,1)S(1)}, bf16[64,512]{1,0:T(8,128)(2,1)S(1)}, u32[]{:S(2)}, u32[]{:S(2)}) collective-permute-start(bf16[64,512]{1,0:T(8,128)(2,1)S(1)} %get-tuple-element.30), channel_id=1, source_target_pairs={{0,1},{1,0},{2,3},{3,2},{4,5},{5,4},{6,7},{7,6},{8,9},{9,8},{10,11... | collective-permute-start | bytes 196616 | tf_op jit(solution)/shard_map/ppermute | solution.py:525
  21.1 1.6 %collective-permute-done.9 = bf16[64,512]{1,0:T(8,128)(2,1)S(1)} collective-permute-done((bf16[64,512]{1,0:T(8,128)(2,1)S(1)}, bf16[64,512]{1,0:T(8,128)(2,1)S(1)}, u32[]{:S(2)}, u32[]{:S(2)}) %collective-permute-start.9) | collective-permute-done | bytes 65568 | tf_op jit(solution)/shard_map/ppermute | solution.py:514
  22.7 1.4 %collective-permute-done.8 = bf16[64,512]{1,0:T(8,128)(2,1)S(1)} collective-permute-done((bf16[64,512]{1,0:T(8,128)(2,1)S(1)}, bf16[64,512]{1,0:T(8,128)(2,1)S(1)}, u32[]{:S(2)}, u32[]{:S(2)}) %collective-permute-start.8) | collective-permute-done | bytes 65568 | tf_op jit(solution)/shard_map/ppermute | solution.py:514
  24.1 0.0 collective-permute-done.7
  24.1 0.7 %add_add_fusion = f32[64,512]{1,0:T(8,128)} fusion(bf16[64,512]{1,0:T(8,128)(2,1)S(1)} %collective-permute-done.9, bf16[64,512]{1,0:T(8,128)(2,1)S(1)} %collective-permute-done.8, f32[64,512]{1,0:T(8,128)S(1)} %get-tuple-element.29, bf16[64,512]{1,0:T(8,128)(2,1)S(1)} %collective-permute-done.7), kind=kLoop, calls=%fused_computation | loop fusion | flops 196608 | bytes 458752 | tf_op jit(solution)/shard_map/add | solution.py:527
  (1 shorter events, 0.0 us)
Async XLA Ops:
  0.0 5.7 %collective-permute-start.1 = (bf16[64,512]{1,0:T(8,128)(2,1)}, bf16[64,512]{1,0:T(8,128)(2,1)S(1)}, u32[]{:S(2)}, u32[]{:S(2)}) collective-permute-start(bf16[64,512]{1,0:T(8,128)(2,1)} %refs_2_.1), channel_id=1, source_target_pairs={{0,2},{1,3},{2,0},{3,1},{4,6},{5,7},{6,4},{7,5},{8,10},{9,11},{10,... | collective-permute-start | bytes 196616 | tf_op jit(solution)/shard_map/ppermute | solution.py:402
  3.0 2.7 %collective-permute-start.2 = (bf16[64,512]{1,0:T(8,128)(2,1)}, bf16[64,512]{1,0:T(8,128)(2,1)S(1)}, u32[]{:S(2)}, u32[]{:S(2)}) collective-permute-start(bf16[64,512]{1,0:T(8,128)(2,1)} %refs_2_.1), channel_id=1, source_target_pairs={{0,1},{1,0},{2,3},{3,2},{4,5},{5,4},{6,7},{7,6},{8,9},{9,8},{10,11... | collective-permute-start | bytes 196616 | tf_op jit(solution)/shard_map/ppermute | solution.py:402
  3.0 4.0 %collective-permute-start = (bf16[64,512]{1,0:T(8,128)(2,1)}, bf16[64,512]{1,0:T(8,128)(2,1)S(1)}, u32[]{:S(2)}, u32[]{:S(2)}) collective-permute-start(bf16[64,512]{1,0:T(8,128)(2,1)} %refs_2_.1), channel_id=1, source_target_pairs={{0,3},{1,2},{2,1},{3,0},{4,7},{5,6},{6,5},{7,4},{8,11},{9,10},{10,... | collective-permute-start | bytes 196616 | tf_op jit(solution)/shard_map/ppermute | solution.py:402
  7.2 5.5 %collective-permute-start.3 = (f32[4,512]{1,0:T(4,128)S(1)}, f32[4,512]{1,0:T(4,128)S(1)}, u32[]{:S(2)}, u32[]{:S(2)}) collective-permute-start(f32[4,512]{1,0:T(4,128)S(1)} %get-tuple-element.27.own_ref), channel_id=1, source_target_pairs={{0,24},{4,28},{8,16},{12,20},{16,8},{20,12},{24,0},{28,4},{1,25},{... | collective-permute-start | bytes 24584 | tf_op jit(solution)/shard_map/ppermute | solution.py:479
  12.7 5.1 %collective-permute-start.4 = (f32[8,512]{1,0:T(8,128)S(1)}, f32[8,512]{1,0:T(8,128)S(1)}, u32[]{:S(2)}, u32[]{:S(2)}) collective-permute-start(f32[8,512]{1,0:T(8,128)S(1)} %pair.1.refs_0_), channel_id=1, source_target_pairs={{0,12},{4,8},{8,4},{12,0},{16,28},{20,24},{24,20},{28,16},{1,13},{... | collective-permute-start | bytes 49160 | tf_op jit(solution)/shard_map/ppermute | solution.py:482
  13.4 4.4 %collective-permute-start.5 = (f32[8,512]{1,0:T(8,128)S(1)}, f32[8,512]{1,0:T(8,128)S(1)}, u32[]{:S(2)}, u32[]{:S(2)}) collective-permute-start(f32[8,512]{1,0:T(8,128)S(1)} %pair.1.refs_0_), channel_id=1, source_target_pairs={{0,4},{4,0},{8,12},{12,8},{16,20},{20,16},{24,28},{28,24},{1,5},{5... | collective-permute-start | bytes 49160 | tf_op jit(solution)/shard_map/ppermute | solution.py:482
  14.2 3.7 %collective-permute-start.6 = (f32[8,512]{1,0:T(8,128)S(1)}, f32[8,512]{1,0:T(8,128)S(1)}, u32[]{:S(2)}, u32[]{:S(2)}) collective-permute-start(f32[8,512]{1,0:T(8,128)S(1)} %pair.1.refs_0_), channel_id=1, source_target_pairs={{0,8},{4,12},{8,0},{12,4},{16,24},{20,28},{24,16},{28,20},{1,9},{5... | collective-permute-start | bytes 49160 | tf_op jit(solution)/shard_map/ppermute | solution.py:482
  18.4 4.3 %collective-permute-start.9 = (bf16[64,512]{1,0:T(8,128)(2,1)S(1)}, bf16[64,512]{1,0:T(8,128)(2,1)S(1)}, u32[]{:S(2)}, u32[]{:S(2)}) collective-permute-start(bf16[64,512]{1,0:T(8,128)(2,1)S(1)} %get-tuple-element.32), channel_id=1, source_target_pairs={{0,2},{1,3},{2,0},{3,1},{4,6},{5,7},{6,4},{7,5},{8,10},{9,11},{10,... | collective-permute-start | bytes 196616 | tf_op jit(solution)/shard_map/ppermute | solution.py:514
  19.9 4.2 %collective-permute-start.8 = (bf16[64,512]{1,0:T(8,128)(2,1)S(1)}, bf16[64,512]{1,0:T(8,128)(2,1)S(1)}, u32[]{:S(2)}, u32[]{:S(2)}) collective-permute-start(bf16[64,512]{1,0:T(8,128)(2,1)S(1)} %get-tuple-element.31), channel_id=1, source_target_pairs={{0,3},{1,2},{2,1},{3,0},{4,7},{5,6},{6,5},{7,4},{8,11},{9,10},{10,... | collective-permute-start | bytes 196616 | tf_op jit(solution)/shard_map/ppermute | solution.py:514
  20.4 3.8 %collective-permute-start.7 = (bf16[64,512]{1,0:T(8,128)(2,1)S(1)}, bf16[64,512]{1,0:T(8,128)(2,1)S(1)}, u32[]{:S(2)}, u32[]{:S(2)}) collective-permute-start(bf16[64,512]{1,0:T(8,128)(2,1)S(1)} %get-tuple-element.30), channel_id=1, source_target_pairs={{0,1},{1,0},{2,3},{3,2},{4,5},{5,4},{6,7},{7,6},{8,9},{9,8},{10,11... | collective-permute-start | bytes 196616 | tf_op jit(solution)/shard_map/ppermute | solution.py:525

commit v7 on v6

--- a/solution.py
+++ b/solution.py
@@ -449,9 +449,9 @@
             )
         ),
     )
-    last = pieces - 1
+    last = [3, 1]
     z = ()
-    for stage, group in enumerate(([0], list(range(last - 1, 0, -1)))):
+    for stage, group in enumerate(([0], [2])):
         z = pl.pallas_call(
             functools.partial(rotate_kernel, (group, stage)),
             out_shape=shape(steps, width),
@@ -462,13 +462,13 @@
         )(place, *(obs[piece] for piece in group), basis, *z)
         z = (z,)
     z, summary = pl.pallas_call(
-        functools.partial(rotate_kernel, ([last], 2)),
+        functools.partial(rotate_kernel, (last, 2)),
         out_shape=(shape(steps, width), shape(4, width)),
-        in_specs=[smem] + [vmem] * 4,
+        in_specs=[smem] + [vmem] * (3 + len(last)),
         out_specs=(vmem,) * 2,
         compiler_params=params,
         name="rotate_last",
-    )(place, obs[last], basis, *z, w)
+    )(place, *(obs[piece] for piece in last), basis, *z, w)
     pair = pl.pallas_call(
         pair_kernel,
         out_shape=shape(8, width),

time: 25.2 us -> 25.7 us (1.020)
  the two profiles are of different devices: /device:TPU:0 before, /device:TPU:19 now
where the time goes in v7:
time: 25.7 us; the launch traced here: 25.5 us
  starting transfers between devices  12.2 us (47%)
  waiting for transfers between devices  6.98 us (27%)
  Pallas kernels  4.92 us (19%)
  between operations  0.73 us (3%)
  other arithmetic  0.68 us (3%)
    ppermute x2, starting transfers between devices, shards(): lax.ppermute(part, 'mode', [(a, a ^ piece) for a in range(pieces)])  5.27 us
    ppermute x3, starting transfers between devices, shards(): lax.ppermute(pair, 'tm', [(a, a ^ step) for a in range(blocks)])  4.28 us
    ppermute x2, waiting for transfers between devices, shards(): lax.ppermute(part, 'mode', [(a, a ^ piece) for a in range(pieces)])  2.82 us
    ppermute x1, waiting for transfers between devices, shards(): lax.ppermute(summary, 'tm', [(a, a ^ MIRROR) for a in range(blocks)])  2.33 us
    ppermute x3, starting transfers between devices, exchange(): out.append(lax.ppermute(value, axis, [(a, a ^ step) for a in range(count)]))  2.31 us
    pallas_call x1, Pallas kernels, shards(): pl.pallas_call(functools.partial(coefficients_kernel, blocks), out_shape=...  1.7 us
    pallas_call x1, Pallas kernels, shards(): pl.pallas_call(functools.partial(local_kernel, blocks), out_shape=(shape(...  1.57 us
    ppermute x3, waiting for transfers between devices, shards(): lax.ppermute(pair, 'tm', [(a, a ^ step) for a in range(blocks)])  1 us
  transfers between devices with their start and end apart: 10, of which 4 were waited for; matrix products, arithmetic and copies ran while one was open for 0% of the time, Pallas kernels for 16%

profile of v7, /device:TPU:19, one launch (start us, length us, event | category | flops | bytes accessed | tf_op | source)
XLA Modules:
  0.0 25.5 jit_solution(4408608536256324898)
XLA Ops:
  0.0 1.2 %collective-permute-start.2 = (bf16[64,512]{1,0:T(8,128)(2,1)}, bf16[64,512]{1,0:T(8,128)(2,1)S(1)}, u32[]{:S(2)}, u32[]{:S(2)}) collective-permute-start(bf16[64,512]{1,0:T(8,128)(2,1)} %refs_2_.1), channel_id=1, source_target_pairs={{0,2},{1,3},{2,0},{3,1},{4,6},{5,7},{6,4},{7,5},{8,10},{9,11},{10,... | collective-permute-start | bytes 196616 | tf_op jit(solution)/shard_map/ppermute | solution.py:402
  1.2 1.1 %collective-permute-start = (bf16[64,512]{1,0:T(8,128)(2,1)}, bf16[64,512]{1,0:T(8,128)(2,1)S(1)}, u32[]{:S(2)}, u32[]{:S(2)}) collective-permute-start(bf16[64,512]{1,0:T(8,128)(2,1)} %refs_2_.1), channel_id=1, source_target_pairs={{0,3},{1,2},{2,1},{3,0},{4,7},{5,6},{6,5},{7,4},{8,11},{9,10},{10,... | collective-permute-start | bytes 196616 | tf_op jit(solution)/shard_map/ppermute | solution.py:402
  2.3 0.0 collective-permute-start.1
  3.0 1.7 %coefficients.1 = (f32[20,8,512]{2,1,0:T(8,128)S(1)}, f32[4,64,512]{2,1,0:T(8,128)S(1)}, f32[32,512]{1,0:T(8,128)S(1)}, bf16[2048,512]{1,0:T(8,128)(2,1)S(1)}, bf16[64,512]{1,0:T(8,128)(2,1)S(1)}) custom-call(f32[1]{0:T(128)S(6)} %copy.6.noise_ref, f32[1,512]{1,0:T(1,128)} %bitcast.4, f32[1,512]{1,0:T(1,128)} %bitcast.5, bf16[64,512]{1,0:T(8,128)(2,1)} %refs_2_.1, ...), custom_call_target="tpu_custom_call" | custom-call | flops 20000000 | bytes 2000000 | tf_op jit(solution)/shard_map/coefficients/pallas_call | solution.py:421
  4.7 0.2 rotate_early.2.refs_2_
  4.9 0.0 collective-permute-done.2.refs_0_
  4.9 0.2 rotate_early.3.refs_3_
  5.1 0.8 %collective-permute-done.refs_0_ = bf16[64,512]{1,0:T(8,128)(2,1)S(1)} collective-permute-done((bf16[64,512]{1,0:T(8,128)(2,1)}, bf16[64,512]{1,0:T(8,128)(2,1)S(1)}, u32[]{:S(2)}, u32[]{:S(2)}) %collective-permute-start) | collective-permute-done | bytes 65568 | tf_op jit(solution)/shard_map/ppermute | solution.py:402
  5.9 0.0 collective-permute-done.1.refs_1_
  5.9 0.3 %rotate_last.1 = (f32[64,512]{1,0:T(8,128)S(1)}, f32[4,512]{1,0:T(4,128)S(1)}) custom-call(s32[1]{0:T(128)} %bitcast.place_ref, bf16[64,512]{1,0:T(8,128)(2,1)S(1)} %collective-permute-done.refs_0_, bf16[64,512]{1,0:T(8,128)(2,1)S(1)} %collective-permute-done.1.refs_1_, bf16[2048,512]{1,0:T(8,128)(2,1)S(1)} %get-tuple-element.19.refs_1_.refs_2_.basis_ref, ...), custom_call_target="tpu_custom_call" | custom-call | tf_op jit(solution)/shard_map/rotate_last/pallas_call | solution.py:464
  6.3 0.2 collective-permute-start.3
  6.5 2.3 %collective-permute-done.3.other_ref = f32[4,512]{1,0:T(4,128)S(1)} collective-permute-done((f32[4,512]{1,0:T(4,128)S(1)}, f32[4,512]{1,0:T(4,128)S(1)}, u32[]{:S(2)}, u32[]{:S(2)}) %collective-permute-start.3) | collective-permute-done | bytes 8224 | tf_op jit(solution)/shard_map/ppermute | solution.py:479
  8.8 3.1 %collective-permute-start.4 = (f32[8,512]{1,0:T(8,128)S(1)}, f32[8,512]{1,0:T(8,128)S(1)}, u32[]{:S(2)}, u32[]{:S(2)}) collective-permute-start(f32[8,512]{1,0:T(8,128)S(1)} %pair.1.refs_0_), channel_id=1, source_target_pairs={{0,12},{4,8},{8,4},{12,0},{16,28},{20,24},{24,20},{28,16},{1,13},{... | collective-permute-start | bytes 49160 | tf_op jit(solution)/shard_map/ppermute | solution.py:482
  11.9 1.2 %collective-permute-start.5 = (f32[8,512]{1,0:T(8,128)S(1)}, f32[8,512]{1,0:T(8,128)S(1)}, u32[]{:S(2)}, u32[]{:S(2)}) collective-permute-start(f32[8,512]{1,0:T(8,128)S(1)} %pair.1.refs_0_), channel_id=1, source_target_pairs={{0,4},{4,0},{8,12},{12,8},{16,20},{20,16},{24,28},{28,24},{1,5},{5... | collective-permute-start | bytes 49160 | tf_op jit(solution)/shard_map/ppermute | solution.py:482
  13.1 0.0 collective-permute-start.6
  13.1 1.6 %local.1 = (f32[64,512]{1,0:T(8,128)S(1)}, f32[4,32,512]{2,1,0:T(8,128)S(1)}) custom-call(s32[1]{0:T(128)} %bitcast.1.me_ref, f32[64,512]{1,0:T(8,128)S(1)} %get-tuple-element.22.z_ref, f32[20,8,512]{2,1,0:T(8,128)S(1)} %get-tuple-element.23.const_ref, f32[32,512]{1,0:T(8,128)S(1)} %get-tuple-element.24.merge_ref), custom_call_target="tpu_custom_call" | custom-call | flops 10000000 | bytes 1000000 | tf_op jit(solution)/shard_map/local/pallas_call | solution.py:494
  14.7 0.0 collective-permute-done.4.refs_1_
  14.7 0.0 collective-permute-done.5.refs_2_
  14.7 1.0 %collective-permute-done.6.refs_3_ = f32[8,512]{1,0:T(8,128)S(1)} collective-permute-done((f32[8,512]{1,0:T(8,128)S(1)}, f32[8,512]{1,0:T(8,128)S(1)}, u32[]{:S(2)}, u32[]{:S(2)}) %collective-permute-start.6) | collective-permute-done | bytes 16416 | tf_op jit(solution)/shard_map/ppermute | solution.py:482
  15.7 0.5 %finish.1 = (bf16[64,512]{1,0:T(8,128)(2,1)S(1)}, bf16[64,512]{1,0:T(8,128)(2,1)S(1)}, bf16[64,512]{1,0:T(8,128)(2,1)S(1)}) custom-call(s32[1]{0:T(128)} %bitcast.place_ref, f32[64,512]{1,0:T(8,128)S(1)} %get-tuple-element.25.r_ref, f32[4,64,512]{2,1,0:T(8,128)S(1)} %get-tuple-element.21.refs_4_.w_ref, f32[4,32,512]{2,1,0:T(8,128)S(1)} %get-tuple-element.26.g_ref, ...), custom_call_target="tpu_custom_call" | custom-call | tf_op jit(solution)/shard_map/finish/pallas_call | solution.py:504
  16.2 1.2 %collective-permute-start.9 = (bf16[64,512]{1,0:T(8,128)(2,1)S(1)}, bf16[64,512]{1,0:T(8,128)(2,1)S(1)}, u32[]{:S(2)}, u32[]{:S(2)}) collective-permute-start(bf16[64,512]{1,0:T(8,128)(2,1)S(1)} %get-tuple-element.32), channel_id=1, source_target_pairs={{0,2},{1,3},{2,0},{3,1},{4,6},{5,7},{6,4},{7,5},{8,10},{9,11},{10,... | collective-permute-start | bytes 196616 | tf_op jit(solution)/shard_map/ppermute | solution.py:514
  17.3 4.1 %collective-permute-start.8 = (bf16[64,512]{1,0:T(8,128)(2,1)S(1)}, bf16[64,512]{1,0:T(8,128)(2,1)S(1)}, u32[]{:S(2)}, u32[]{:S(2)}) collective-permute-start(bf16[64,512]{1,0:T(8,128)(2,1)S(1)} %get-tuple-element.31), channel_id=1, source_target_pairs={{0,3},{1,2},{2,1},{3,0},{4,7},{5,6},{6,5},{7,4},{8,11},{9,10},{10,... | collective-permute-start | bytes 196616 | tf_op jit(solution)/shard_map/ppermute | solution.py:514
  21.4 0.4 %rest.1 = (f32[64,512]{1,0:T(8,128)S(1)}, bf16[64,512]{1,0:T(8,128)(2,1)S(1)}) custom-call(s32[1]{0:T(128)} %bitcast.place_ref, bf16[64,512]{1,0:T(8,128)(2,1)S(1)} %get-tuple-element.28.residual_ref, bf16[2048,512]{1,0:T(8,128)(2,1)S(1)} %get-tuple-element.19.refs_1_.refs_2_.basis_ref), custom_call_target="tpu_custom_call" | custom-call | tf_op jit(solution)/shard_map/rest/pallas_call | solution.py:517
  21.9 0.1 collective-permute-start.7
  22.0 0.0 collective-permute-done.9
  22.0 2.8 %collective-permute-done.8 = bf16[64,512]{1,0:T(8,128)(2,1)S(1)} collective-permute-done((bf16[64,512]{1,0:T(8,128)(2,1)S(1)}, bf16[64,512]{1,0:T(8,128)(2,1)S(1)}, u32[]{:S(2)}, u32[]{:S(2)}) %collective-permute-start.8) | collective-permute-done | bytes 65568 | tf_op jit(solution)/shard_map/ppermute | solution.py:514
  24.8 0.0 collective-permute-done.7
  24.8 0.7 %add_add_fusion = f32[64,512]{1,0:T(8,128)} fusion(bf16[64,512]{1,0:T(8,128)(2,1)S(1)} %collective-permute-done.9, bf16[64,512]{1,0:T(8,128)(2,1)S(1)} %collective-permute-done.8, f32[64,512]{1,0:T(8,128)S(1)} %get-tuple-element.29, bf16[64,512]{1,0:T(8,128)(2,1)S(1)} %collective-permute-done.7), kind=kLoop, calls=%fused_computation | loop fusion | flops 196608 | bytes 458752 | tf_op jit(solution)/shard_map/add | solution.py:527
  (1 shorter events, 0.0 us)
Async XLA Ops:
  0.0 4.9 %collective-permute-start.2 = (bf16[64,512]{1,0:T(8,128)(2,1)}, bf16[64,512]{1,0:T(8,128)(2,1)S(1)}, u32[]{:S(2)}, u32[]{:S(2)}) collective-permute-start(bf16[64,512]{1,0:T(8,128)(2,1)} %refs_2_.1), channel_id=1, source_target_pairs={{0,2},{1,3},{2,0},{3,1},{4,6},{5,7},{6,4},{7,5},{8,10},{9,11},{10,... | collective-permute-start | bytes 196616 | tf_op jit(solution)/shard_map/ppermute | solution.py:402
  1.2 4.7 %collective-permute-start = (bf16[64,512]{1,0:T(8,128)(2,1)}, bf16[64,512]{1,0:T(8,128)(2,1)S(1)}, u32[]{:S(2)}, u32[]{:S(2)}) collective-permute-start(bf16[64,512]{1,0:T(8,128)(2,1)} %refs_2_.1), channel_id=1, source_target_pairs={{0,3},{1,2},{2,1},{3,0},{4,7},{5,6},{6,5},{7,4},{8,11},{9,10},{10,... | collective-permute-start | bytes 196616 | tf_op jit(solution)/shard_map/ppermute | solution.py:402
  2.3 3.6 %collective-permute-start.1 = (bf16[64,512]{1,0:T(8,128)(2,1)}, bf16[64,512]{1,0:T(8,128)(2,1)S(1)}, u32[]{:S(2)}, u32[]{:S(2)}) collective-permute-start(bf16[64,512]{1,0:T(8,128)(2,1)} %refs_2_.1), channel_id=1, source_target_pairs={{0,1},{1,0},{2,3},{3,2},{4,5},{5,4},{6,7},{7,6},{8,9},{9,8},{10,11... | collective-permute-start | bytes 196616 | tf_op jit(solution)/shard_map/ppermute | solution.py:402
  6.3 2.6 %collective-permute-start.3 = (f32[4,512]{1,0:T(4,128)S(1)}, f32[4,512]{1,0:T(4,128)S(1)}, u32[]{:S(2)}, u32[]{:S(2)}) collective-permute-start(f32[4,512]{1,0:T(4,128)S(1)} %get-tuple-element.27.own_ref), channel_id=1, source_target_pairs={{0,24},{4,28},{8,16},{12,20},{16,8},{20,12},{24,0},{28,4},{1,25},{... | collective-permute-start | bytes 24584 | tf_op jit(solution)/shard_map/ppermute | solution.py:479
  8.8 5.9 %collective-permute-start.4 = (f32[8,512]{1,0:T(8,128)S(1)}, f32[8,512]{1,0:T(8,128)S(1)}, u32[]{:S(2)}, u32[]{:S(2)}) collective-permute-start(f32[8,512]{1,0:T(8,128)S(1)} %pair.1.refs_0_), channel_id=1, source_target_pairs={{0,12},{4,8},{8,4},{12,0},{16,28},{20,24},{24,20},{28,16},{1,13},{... | collective-permute-start | bytes 49160 | tf_op jit(solution)/shard_map/ppermute | solution.py:482
  11.9 2.8 %collective-permute-start.5 = (f32[8,512]{1,0:T(8,128)S(1)}, f32[8,512]{1,0:T(8,128)S(1)}, u32[]{:S(2)}, u32[]{:S(2)}) collective-permute-start(f32[8,512]{1,0:T(8,128)S(1)} %pair.1.refs_0_), channel_id=1, source_target_pairs={{0,4},{4,0},{8,12},{12,8},{16,20},{20,16},{24,28},{28,24},{1,5},{5... | collective-permute-start | bytes 49160 | tf_op jit(solution)/shard_map/ppermute | solution.py:482
  13.1 2.6 %collective-permute-start.6 = (f32[8,512]{1,0:T(8,128)S(1)}, f32[8,512]{1,0:T(8,128)S(1)}, u32[]{:S(2)}, u32[]{:S(2)}) collective-permute-start(f32[8,512]{1,0:T(8,128)S(1)} %pair.1.refs_0_), channel_id=1, source_target_pairs={{0,8},{4,12},{8,0},{12,4},{16,24},{20,28},{24,16},{28,20},{1,9},{5... | collective-permute-start | bytes 49160 | tf_op jit(solution)/shard_map/ppermute | solution.py:482
  16.2 5.8 %collective-permute-start.9 = (bf16[64,512]{1,0:T(8,128)(2,1)S(1)}, bf16[64,512]{1,0:T(8,128)(2,1)S(1)}, u32[]{:S(2)}, u32[]{:S(2)}) collective-permute-start(bf16[64,512]{1,0:T(8,128)(2,1)S(1)} %get-tuple-element.32), channel_id=1, source_target_pairs={{0,2},{1,3},{2,0},{3,1},{4,6},{5,7},{6,4},{7,5},{8,10},{9,11},{10,... | collective-permute-start | bytes 196616 | tf_op jit(solution)/shard_map/ppermute | solution.py:514
  17.3 7.4 %collective-permute-start.8 = (bf16[64,512]{1,0:T(8,128)(2,1)S(1)}, bf16[64,512]{1,0:T(8,128)(2,1)S(1)}, u32[]{:S(2)}, u32[]{:S(2)}) collective-permute-start(bf16[64,512]{1,0:T(8,128)(2,1)S(1)} %get-tuple-element.31), channel_id=1, source_target_pairs={{0,3},{1,2},{2,1},{3,0},{4,7},{5,6},{6,5},{7,4},{8,11},{9,10},{10,... | collective-permute-start | bytes 196616 | tf_op jit(solution)/shard_map/ppermute | solution.py:514
  21.9 2.9 %collective-permute-start.7 = (bf16[64,512]{1,0:T(8,128)(2,1)S(1)}, bf16[64,512]{1,0:T(8,128)(2,1)S(1)}, u32[]{:S(2)}, u32[]{:S(2)}) collective-permute-start(bf16[64,512]{1,0:T(8,128)(2,1)S(1)} %get-tuple-element.30), channel_id=1, source_target_pairs={{0,1},{1,0},{2,3},{3,2},{4,5},{5,4},{6,7},{7,6},{8,9},{9,8},{10,11... | collective-permute-start | bytes 196616 | tf_op jit(solution)/shard_map/ppermute | solution.py:525

commit v8 on v7

--- a/solution.py
+++ b/solution.py
@@ -449,9 +449,9 @@
             )
         ),
     )
-    last = [3, 1]
+    last = [2, 1]
     z = ()
-    for stage, group in enumerate(([0], [2])):
+    for stage, group in enumerate(([0], [3])):
         z = pl.pallas_call(
             functools.partial(rotate_kernel, (group, stage)),
             out_shape=shape(steps, width),

time: 25.7 us -> 25.9 us (level)
  the two profiles are of different devices: /device:TPU:19 before, /device:TPU:0 now
where the time goes in v8:
time: 25.9 us; the launch traced here: 25.4 us
  starting transfers between devices  12.7 us (49%)
  waiting for transfers between devices  6.45 us (25%)
  Pallas kernels  4.92 us (19%)
  between operations  0.71 us (3%)
  other arithmetic  0.68 us (3%)
    ppermute x1, starting transfers between devices, shards(): lax.ppermute(summary, 'tm', [(a, a ^ MIRROR) for a in range(blocks)])  3.83 us
    ppermute x3, starting transfers between devices, shards(): lax.ppermute(pair, 'tm', [(a, a ^ step) for a in range(blocks)])  3.49 us
    ppermute x3, starting transfers between devices, exchange(): out.append(lax.ppermute(value, axis, [(a, a ^ step) for a in range(count)]))  3.08 us
    ppermute x2, waiting for transfers between devices, shards(): lax.ppermute(part, 'mode', [(a, a ^ piece) for a in range(pieces)])  3.02 us
    pallas_call x1, Pallas kernels, shards(): pl.pallas_call(functools.partial(coefficients_kernel, blocks), out_shape=...  1.7 us
    ppermute x1, waiting for transfers between devices, shards(): lax.ppermute(summary, 'tm', [(a, a ^ MIRROR) for a in range(blocks)])  1.68 us
    ppermute x2, starting transfers between devices, shards(): lax.ppermute(part, 'mode', [(a, a ^ piece) for a in range(pieces)])  1.59 us
    pallas_call x1, Pallas kernels, shards(): pl.pallas_call(functools.partial(local_kernel, blocks), out_shape=(shape(...  1.57 us
  transfers between devices with their start and end apart: 10, of which 5 were waited for; matrix products, arithmetic and copies ran while one was open for 0% of the time, Pallas kernels for 16%

profile of v8, /device:TPU:0, one launch (start us, length us, event | category | flops | bytes accessed | tf_op | source)
XLA Modules:
  0.0 25.4 jit_solution(2929367992982231154)
XLA Ops:
  0.0 2.4 %collective-permute-start.2 = (bf16[64,512]{1,0:T(8,128)(2,1)}, bf16[64,512]{1,0:T(8,128)(2,1)S(1)}, u32[]{:S(2)}, u32[]{:S(2)}) collective-permute-start(bf16[64,512]{1,0:T(8,128)(2,1)} %refs_2_.1), channel_id=1, source_target_pairs={{0,3},{1,2},{2,1},{3,0},{4,7},{5,6},{6,5},{7,4},{8,11},{9,10},{10,... | collective-permute-start | bytes 196616 | tf_op jit(solution)/shard_map/ppermute | solution.py:402
  2.4 0.6 %collective-permute-start = (bf16[64,512]{1,0:T(8,128)(2,1)}, bf16[64,512]{1,0:T(8,128)(2,1)S(1)}, u32[]{:S(2)}, u32[]{:S(2)}) collective-permute-start(bf16[64,512]{1,0:T(8,128)(2,1)} %refs_2_.1), channel_id=1, source_target_pairs={{0,2},{1,3},{2,0},{3,1},{4,6},{5,7},{6,4},{7,5},{8,10},{9,11},{10,... | collective-permute-start | bytes 196616 | tf_op jit(solution)/shard_map/ppermute | solution.py:402
  3.0 0.1 collective-permute-start.1
  3.7 1.7 %coefficients.1 = (f32[20,8,512]{2,1,0:T(8,128)S(1)}, f32[4,64,512]{2,1,0:T(8,128)S(1)}, f32[32,512]{1,0:T(8,128)S(1)}, bf16[2048,512]{1,0:T(8,128)(2,1)S(1)}, bf16[64,512]{1,0:T(8,128)(2,1)S(1)}) custom-call(f32[1]{0:T(128)S(6)} %copy.6.noise_ref, f32[1,512]{1,0:T(1,128)} %bitcast.4, f32[1,512]{1,0:T(1,128)} %bitcast.5, bf16[64,512]{1,0:T(8,128)(2,1)} %refs_2_.1, ...), custom_call_target="tpu_custom_call" | custom-call | flops 20000000 | bytes 2000000 | tf_op jit(solution)/shard_map/coefficients/pallas_call | solution.py:421
  5.4 0.2 rotate_early.2.refs_2_
  5.7 0.0 collective-permute-done.2.refs_0_
  5.7 0.2 rotate_early.3.refs_3_
  5.9 1.4 %collective-permute-done.refs_0_ = bf16[64,512]{1,0:T(8,128)(2,1)S(1)} collective-permute-done((bf16[64,512]{1,0:T(8,128)(2,1)}, bf16[64,512]{1,0:T(8,128)(2,1)S(1)}, u32[]{:S(2)}, u32[]{:S(2)}) %collective-permute-start) | collective-permute-done | bytes 65568 | tf_op jit(solution)/shard_map/ppermute | solution.py:402
  7.3 0.0 collective-permute-done.1.refs_1_
  7.3 0.3 %rotate_last.1 = (f32[64,512]{1,0:T(8,128)S(1)}, f32[4,512]{1,0:T(4,128)S(1)}) custom-call(s32[1]{0:T(128)} %bitcast.place_ref, bf16[64,512]{1,0:T(8,128)(2,1)S(1)} %collective-permute-done.refs_0_, bf16[64,512]{1,0:T(8,128)(2,1)S(1)} %collective-permute-done.1.refs_1_, bf16[2048,512]{1,0:T(8,128)(2,1)S(1)} %get-tuple-element.19.refs_1_.refs_2_.basis_ref, ...), custom_call_target="tpu_custom_call" | custom-call | tf_op jit(solution)/shard_map/rotate_last/pallas_call | solution.py:464
  7.6 3.8 %collective-permute-start.3 = (f32[4,512]{1,0:T(4,128)S(1)}, f32[4,512]{1,0:T(4,128)S(1)}, u32[]{:S(2)}, u32[]{:S(2)}) collective-permute-start(f32[4,512]{1,0:T(4,128)S(1)} %get-tuple-element.27.own_ref), channel_id=1, source_target_pairs={{0,24},{4,28},{8,16},{12,20},{16,8},{20,12},{24,0},{28,4},{1,25},{... | collective-permute-start | bytes 24584 | tf_op jit(solution)/shard_map/ppermute | solution.py:479
  11.5 1.7 %collective-permute-done.3.other_ref = f32[4,512]{1,0:T(4,128)S(1)} collective-permute-done((f32[4,512]{1,0:T(4,128)S(1)}, f32[4,512]{1,0:T(4,128)S(1)}, u32[]{:S(2)}, u32[]{:S(2)}) %collective-permute-start.3) | collective-permute-done | bytes 8224 | tf_op jit(solution)/shard_map/ppermute | solution.py:479
  13.2 0.9 %collective-permute-start.4 = (f32[8,512]{1,0:T(8,128)S(1)}, f32[8,512]{1,0:T(8,128)S(1)}, u32[]{:S(2)}, u32[]{:S(2)}) collective-permute-start(f32[8,512]{1,0:T(8,128)S(1)} %pair.1.refs_0_), channel_id=1, source_target_pairs={{0,12},{4,8},{8,4},{12,0},{16,28},{20,24},{24,20},{28,16},{1,13},{... | collective-permute-start | bytes 49160 | tf_op jit(solution)/shard_map/ppermute | solution.py:482
  14.0 0.8 %collective-permute-start.5 = (f32[8,512]{1,0:T(8,128)S(1)}, f32[8,512]{1,0:T(8,128)S(1)}, u32[]{:S(2)}, u32[]{:S(2)}) collective-permute-start(f32[8,512]{1,0:T(8,128)S(1)} %pair.1.refs_0_), channel_id=1, source_target_pairs={{0,4},{4,0},{8,12},{12,8},{16,20},{20,16},{24,28},{28,24},{1,5},{5... | collective-permute-start | bytes 49160 | tf_op jit(solution)/shard_map/ppermute | solution.py:482
  14.8 1.8 %collective-permute-start.6 = (f32[8,512]{1,0:T(8,128)S(1)}, f32[8,512]{1,0:T(8,128)S(1)}, u32[]{:S(2)}, u32[]{:S(2)}) collective-permute-start(f32[8,512]{1,0:T(8,128)S(1)} %pair.1.refs_0_), channel_id=1, source_target_pairs={{0,8},{4,12},{8,0},{12,4},{16,24},{20,28},{24,16},{28,20},{1,9},{5... | collective-permute-start | bytes 49160 | tf_op jit(solution)/shard_map/ppermute | solution.py:482
  16.7 1.6 %local.1 = (f32[64,512]{1,0:T(8,128)S(1)}, f32[4,32,512]{2,1,0:T(8,128)S(1)}) custom-call(s32[1]{0:T(128)} %bitcast.1.me_ref, f32[64,512]{1,0:T(8,128)S(1)} %get-tuple-element.22.z_ref, f32[20,8,512]{2,1,0:T(8,128)S(1)} %get-tuple-element.23.const_ref, f32[32,512]{1,0:T(8,128)S(1)} %get-tuple-element.24.merge_ref), custom_call_target="tpu_custom_call" | custom-call | flops 10000000 | bytes 1000000 | tf_op jit(solution)/shard_map/local/pallas_call | solution.py:494
  18.2 0.0 collective-permute-done.4.refs_1_
  18.2 0.0 collective-permute-done.5.refs_2_
  18.2 0.3 %collective-permute-done.6.refs_3_ = f32[8,512]{1,0:T(8,128)S(1)} collective-permute-done((f32[8,512]{1,0:T(8,128)S(1)}, f32[8,512]{1,0:T(8,128)S(1)}, u32[]{:S(2)}, u32[]{:S(2)}) %collective-permute-start.6) | collective-permute-done | bytes 16416 | tf_op jit(solution)/shard_map/ppermute | solution.py:482
  18.6 0.5 %finish.1 = (bf16[64,512]{1,0:T(8,128)(2,1)S(1)}, bf16[64,512]{1,0:T(8,128)(2,1)S(1)}, bf16[64,512]{1,0:T(8,128)(2,1)S(1)}) custom-call(s32[1]{0:T(128)} %bitcast.place_ref, f32[64,512]{1,0:T(8,128)S(1)} %get-tuple-element.25.r_ref, f32[4,64,512]{2,1,0:T(8,128)S(1)} %get-tuple-element.21.refs_4_.w_ref, f32[4,32,512]{2,1,0:T(8,128)S(1)} %get-tuple-element.26.g_ref, ...), custom_call_target="tpu_custom_call" | custom-call | tf_op jit(solution)/shard_map/finish/pallas_call | solution.py:504
  19.0 1.6 %collective-permute-start.9 = (bf16[64,512]{1,0:T(8,128)(2,1)S(1)}, bf16[64,512]{1,0:T(8,128)(2,1)S(1)}, u32[]{:S(2)}, u32[]{:S(2)}) collective-permute-start(bf16[64,512]{1,0:T(8,128)(2,1)S(1)} %get-tuple-element.32), channel_id=1, source_target_pairs={{0,2},{1,3},{2,0},{3,1},{4,6},{5,7},{6,4},{7,5},{8,10},{9,11},{10,... | collective-permute-start | bytes 196616 | tf_op jit(solution)/shard_map/ppermute | solution.py:514
  20.6 0.0 collective-permute-start.8
  20.6 0.4 %rest.1 = (f32[64,512]{1,0:T(8,128)S(1)}, bf16[64,512]{1,0:T(8,128)(2,1)S(1)}) custom-call(s32[1]{0:T(128)} %bitcast.place_ref, bf16[64,512]{1,0:T(8,128)(2,1)S(1)} %get-tuple-element.28.residual_ref, bf16[2048,512]{1,0:T(8,128)(2,1)S(1)} %get-tuple-element.19.refs_1_.refs_2_.basis_ref), custom_call_target="tpu_custom_call" | custom-call | tf_op jit(solution)/shard_map/rest/pallas_call | solution.py:517
  21.0 0.7 %collective-permute-start.7 = (bf16[64,512]{1,0:T(8,128)(2,1)S(1)}, bf16[64,512]{1,0:T(8,128)(2,1)S(1)}, u32[]{:S(2)}, u32[]{:S(2)}) collective-permute-start(bf16[64,512]{1,0:T(8,128)(2,1)S(1)} %get-tuple-element.30), channel_id=1, source_target_pairs={{0,1},{1,0},{2,3},{3,2},{4,5},{5,4},{6,7},{7,6},{8,9},{9,8},{10,11... | collective-permute-start | bytes 196616 | tf_op jit(solution)/shard_map/ppermute | solution.py:525
  21.7 1.6 %collective-permute-done.9 = bf16[64,512]{1,0:T(8,128)(2,1)S(1)} collective-permute-done((bf16[64,512]{1,0:T(8,128)(2,1)S(1)}, bf16[64,512]{1,0:T(8,128)(2,1)S(1)}, u32[]{:S(2)}, u32[]{:S(2)}) %collective-permute-start.9) | collective-permute-done | bytes 65568 | tf_op jit(solution)/shard_map/ppermute | solution.py:514
  23.3 1.4 %collective-permute-done.8 = bf16[64,512]{1,0:T(8,128)(2,1)S(1)} collective-permute-done((bf16[64,512]{1,0:T(8,128)(2,1)S(1)}, bf16[64,512]{1,0:T(8,128)(2,1)S(1)}, u32[]{:S(2)}, u32[]{:S(2)}) %collective-permute-start.8) | collective-permute-done | bytes 65568 | tf_op jit(solution)/shard_map/ppermute | solution.py:514
  24.8 0.0 collective-permute-done.7
  24.8 0.7 %add_add_fusion = f32[64,512]{1,0:T(8,128)} fusion(bf16[64,512]{1,0:T(8,128)(2,1)S(1)} %collective-permute-done.9, bf16[64,512]{1,0:T(8,128)(2,1)S(1)} %collective-permute-done.8, f32[64,512]{1,0:T(8,128)S(1)} %get-tuple-element.29, bf16[64,512]{1,0:T(8,128)(2,1)S(1)} %collective-permute-done.7), kind=kLoop, calls=%fused_computation | loop fusion | flops 196608 | bytes 458752 | tf_op jit(solution)/shard_map/add | solution.py:527
  (1 shorter events, 0.0 us)
Async XLA Ops:
  0.0 5.7 %collective-permute-start.2 = (bf16[64,512]{1,0:T(8,128)(2,1)}, bf16[64,512]{1,0:T(8,128)(2,1)S(1)}, u32[]{:S(2)}, u32[]{:S(2)}) collective-permute-start(bf16[64,512]{1,0:T(8,128)(2,1)} %refs_2_.1), channel_id=1, source_target_pairs={{0,3},{1,2},{2,1},{3,0},{4,7},{5,6},{6,5},{7,4},{8,11},{9,10},{10,... | collective-permute-start | bytes 196616 | tf_op jit(solution)/shard_map/ppermute | solution.py:402
  2.4 4.9 %collective-permute-start = (bf16[64,512]{1,0:T(8,128)(2,1)}, bf16[64,512]{1,0:T(8,128)(2,1)S(1)}, u32[]{:S(2)}, u32[]{:S(2)}) collective-permute-start(bf16[64,512]{1,0:T(8,128)(2,1)} %refs_2_.1), channel_id=1, source_target_pairs={{0,2},{1,3},{2,0},{3,1},{4,6},{5,7},{6,4},{7,5},{8,10},{9,11},{10,... | collective-permute-start | bytes 196616 | tf_op jit(solution)/shard_map/ppermute | solution.py:402
  3.0 4.3 %collective-permute-start.1 = (bf16[64,512]{1,0:T(8,128)(2,1)}, bf16[64,512]{1,0:T(8,128)(2,1)S(1)}, u32[]{:S(2)}, u32[]{:S(2)}) collective-permute-start(bf16[64,512]{1,0:T(8,128)(2,1)} %refs_2_.1), channel_id=1, source_target_pairs={{0,1},{1,0},{2,3},{3,2},{4,5},{5,4},{6,7},{7,6},{8,9},{9,8},{10,11... | collective-permute-start | bytes 196616 | tf_op jit(solution)/shard_map/ppermute | solution.py:402
  7.6 5.5 %collective-permute-start.3 = (f32[4,512]{1,0:T(4,128)S(1)}, f32[4,512]{1,0:T(4,128)S(1)}, u32[]{:S(2)}, u32[]{:S(2)}) collective-permute-start(f32[4,512]{1,0:T(4,128)S(1)} %get-tuple-element.27.own_ref), channel_id=1, source_target_pairs={{0,24},{4,28},{8,16},{12,20},{16,8},{20,12},{24,0},{28,4},{1,25},{... | collective-permute-start | bytes 24584 | tf_op jit(solution)/shard_map/ppermute | solution.py:479
  13.2 5.1 %collective-permute-start.4 = (f32[8,512]{1,0:T(8,128)S(1)}, f32[8,512]{1,0:T(8,128)S(1)}, u32[]{:S(2)}, u32[]{:S(2)}) collective-permute-start(f32[8,512]{1,0:T(8,128)S(1)} %pair.1.refs_0_), channel_id=1, source_target_pairs={{0,12},{4,8},{8,4},{12,0},{16,28},{20,24},{24,20},{28,16},{1,13},{... | collective-permute-start | bytes 49160 | tf_op jit(solution)/shard_map/ppermute | solution.py:482
  14.0 4.2 %collective-permute-start.5 = (f32[8,512]{1,0:T(8,128)S(1)}, f32[8,512]{1,0:T(8,128)S(1)}, u32[]{:S(2)}, u32[]{:S(2)}) collective-permute-start(f32[8,512]{1,0:T(8,128)S(1)} %pair.1.refs_0_), channel_id=1, source_target_pairs={{0,4},{4,0},{8,12},{12,8},{16,20},{20,16},{24,28},{28,24},{1,5},{5... | collective-permute-start | bytes 49160 | tf_op jit(solution)/shard_map/ppermute | solution.py:482
  14.8 3.7 %collective-permute-start.6 = (f32[8,512]{1,0:T(8,128)S(1)}, f32[8,512]{1,0:T(8,128)S(1)}, u32[]{:S(2)}, u32[]{:S(2)}) collective-permute-start(f32[8,512]{1,0:T(8,128)S(1)} %pair.1.refs_0_), channel_id=1, source_target_pairs={{0,8},{4,12},{8,0},{12,4},{16,24},{20,28},{24,16},{28,20},{1,9},{5... | collective-permute-start | bytes 49160 | tf_op jit(solution)/shard_map/ppermute | solution.py:482
  19.0 4.3 %collective-permute-start.9 = (bf16[64,512]{1,0:T(8,128)(2,1)S(1)}, bf16[64,512]{1,0:T(8,128)(2,1)S(1)}, u32[]{:S(2)}, u32[]{:S(2)}) collective-permute-start(bf16[64,512]{1,0:T(8,128)(2,1)S(1)} %get-tuple-element.32), channel_id=1, source_target_pairs={{0,2},{1,3},{2,0},{3,1},{4,6},{5,7},{6,4},{7,5},{8,10},{9,11},{10,... | collective-permute-start | bytes 196616 | tf_op jit(solution)/shard_map/ppermute | solution.py:514
  20.6 4.2 %collective-permute-start.8 = (bf16[64,512]{1,0:T(8,128)(2,1)S(1)}, bf16[64,512]{1,0:T(8,128)(2,1)S(1)}, u32[]{:S(2)}, u32[]{:S(2)}) collective-permute-start(bf16[64,512]{1,0:T(8,128)(2,1)S(1)} %get-tuple-element.31), channel_id=1, source_target_pairs={{0,3},{1,2},{2,1},{3,0},{4,7},{5,6},{6,5},{7,4},{8,11},{9,10},{10,... | collective-permute-start | bytes 196616 | tf_op jit(solution)/shard_map/ppermute | solution.py:514
  21.0 3.7 %collective-permute-start.7 = (bf16[64,512]{1,0:T(8,128)(2,1)S(1)}, bf16[64,512]{1,0:T(8,128)(2,1)S(1)}, u32[]{:S(2)}, u32[]{:S(2)}) collective-permute-start(bf16[64,512]{1,0:T(8,128)(2,1)S(1)} %get-tuple-element.30), channel_id=1, source_target_pairs={{0,1},{1,0},{2,3},{3,2},{4,5},{5,4},{6,7},{7,6},{8,9},{9,8},{10,11... | collective-permute-start | bytes 196616 | tf_op jit(solution)/shard_map/ppermute | solution.py:525

commit v9 on v5

--- a/solution.py
+++ b/solution.py
@@ -188,18 +188,18 @@
 
 
 def rotate_kernel(first, place_ref, *refs):
-    pieces, others = first
+    pieces, stage = first
     obs_refs, (basis_ref, *refs) = refs[: len(pieces)], refs[len(pieces) :]
     depth = obs_refs[0].shape[1]
-    z = None if others is None else refs[0][...]
+    z = refs[0][...] if stage else None
     for piece, obs_ref in zip(pieces, obs_refs):
         begin = pl.multiple_of((place_ref[0] ^ piece) * depth, depth)
         term = jnp.dot(
             obs_ref[...], basis_ref[pl.ds(begin, depth), :], preferred_element_type=F32
         )
         z = term if z is None else z + term
-    if others is None:
-        refs[0][...] = z
+    if stage < 2:
+        refs[-1][...] = z
         return
     _, w_ref, z_ref, sum_ref = refs
     z_ref[...] = z
@@ -227,7 +227,7 @@
     )
 
 
-def pair_kernel(own_ref, other_ref, out_ref):
+def pair_kernel(_, own_ref, other_ref, out_ref):
     out_ref[0:4, :] = own_ref[...]
     out_ref[4:8, :] = other_ref[...]
 
@@ -450,31 +450,43 @@
         ),
     )
     last = pieces - 1
-    early = list(range(last))
-    z = pl.pallas_call(
-        functools.partial(rotate_kernel, (early, None)),
-        out_shape=shape(steps, width),
-        in_specs=[smem] + [vmem] * pieces,
-        out_specs=vmem,
-        compiler_params=params,
-        name="rotate_early",
-    )(place, *(obs[piece] for piece in early), basis)
+    z = ()
+    for stage, group in enumerate(([0], list(range(1, last)))):
+        z = pl.pallas_call(
+            functools.partial(rotate_kernel, (group, stage)),
+            out_shape=shape(steps, width),
+            in_specs=[smem] + [vmem] * (len(group) + 1 + len(z)),
+            out_specs=vmem,
+            compiler_params=params,
+            name="rotate_early",
+        )(place, *(obs[piece] for piece in group), basis, *z)
+        z = (z,)
     z, summary = pl.pallas_call(
-        functools.partial(rotate_kernel, ([last], early)),
+        functools.partial(rotate_kernel, ([last], 2)),
         out_shape=(shape(steps, width), shape(4, width)),
         in_specs=[smem] + [vmem] * 4,
         out_specs=(vmem,) * 2,
         compiler_params=params,
         name="rotate_last",
-    )(place, obs[last], basis, z, w)
+    )(place, obs[last], basis, *z, w)
+    local, g = pl.pallas_call(
+        functools.partial(local_kernel, blocks),
+        out_shape=(shape(steps, width), shape(4, -(-4 * (rounds + 5) // SUB) * SUB, width)),
+        in_specs=[smem] + [vmem] * 3,
+        out_specs=(vmem,) * 2,
+        scratch_shapes=[pltpu.VMEM((width // 128, steps, 128), F32)],
+        compiler_params=params,
+        cost_estimate=pl.CostEstimate(flops=10000000, bytes_accessed=1000000, transcendentals=0),
+        name="local",
+    )(me, z, const, merges)
     pair = pl.pallas_call(
         pair_kernel,
         out_shape=shape(8, width),
-        in_specs=[vmem] * 2,
+        in_specs=[vmem] * 3,
         out_specs=vmem,
         compiler_params=params,
         name="pair",
-    )(summary, lax.ppermute(summary, "tm", [(a, a ^ MIRROR) for a in range(blocks)]))
+    )(g, summary, lax.ppermute(summary, "tm", [(a, a ^ MIRROR) for a in range(blocks)]))
     sums = [pair]
     for step in NEAR:
         sums.append(lax.ppermute(pair, "tm", [(a, a ^ step) for a in range(blocks)]))
@@ -489,16 +501,6 @@
         )(me, merges, *(sums if level == 3 else (summary, sums[-1])))
         step = 1 << level
         sums.append(lax.ppermute(summary, "tm", [(a, a ^ step) for a in range(blocks)]))
-    local, g = pl.pallas_call(
-        functools.partial(local_kernel, blocks),
-        out_shape=(shape(steps, width), shape(4, -(-4 * (rounds + 5) // SUB) * SUB, width)),
-        in_specs=[smem] + [vmem] * 3,
-        out_specs=(vmem,) * 2,
-        scratch_shapes=[pltpu.VMEM((width // 128, steps, 128), F32)],
-        compiler_params=params,
-        cost_estimate=pl.CostEstimate(flops=10000000, bytes_accessed=1000000, transcendentals=0),
-        name="local",
-    )(me, z, const, merges)
     far = list(range(2, pieces)) + [1]
     near = [0]
     residual, *parts = pl.pallas_call(

time: 25.2 us -> 25.3 us (level)
    ppermute x3, waiting for transfers between devices: 0.16 us -> 1.76 us  [shards(): lax.ppermute(pair, 'tm', [(a, a ^ step) for a in range(blocks)])]
    ppermute x1, waiting for transfers between devices: 1.85 us -> 0.28 us  [shards(): lax.ppermute(summary, 'tm', [(a, a ^ MIRROR) for a in range(blocks)])]
    pallas_call x2 -> x3, Pallas kernels: 0.63 us -> 0.75 us  [the longest x2 0.5 us: shards(): pl.pallas_call(functools.partial(rotate_kernel, (group, stage)), out_shap...]
where the time goes in v9:
time: 25.3 us; the launch traced here: 25 us
  starting transfers between devices  12.4 us (49%)
  waiting for transfers between devices  6.23 us (25%)
  Pallas kernels  4.91 us (19%)
  between operations  0.71 us (3%)
  other arithmetic  0.69 us (3%)
    ppermute x1, starting transfers between devices, shards(): lax.ppermute(summary, 'tm', [(a, a ^ MIRROR) for a in range(blocks)])  3.67 us
    ppermute x3, starting transfers between devices, shards(): lax.ppermute(pair, 'tm', [(a, a ^ step) for a in range(blocks)])  3.49 us
    ppermute x3, waiting for transfers between devices, shards(): lax.ppermute(part, 'mode', [(a, a ^ piece) for a in range(pieces)])  3.25 us
    ppermute x3, starting transfers between devices, exchange(): out.append(lax.ppermute(value, axis, [(a, a ^ step) for a in range(count)]))  3.08 us
    ppermute x3, starting transfers between devices, shards(): lax.ppermute(part, 'mode', [(a, a ^ piece) for a in range(pieces)])  2.21 us
    ppermute x3, waiting for transfers between devices, shards(): lax.ppermute(pair, 'tm', [(a, a ^ step) for a in range(blocks)])  1.76 us
    pallas_call x1, Pallas kernels, shards(): pl.pallas_call(functools.partial(coefficients_kernel, blocks), out_shape=...  1.7 us
    pallas_call x1, Pallas kernels, shards(): pl.pallas_call(functools.partial(local_kernel, blocks), out_shape=(shape(...  1.57 us
  transfers between devices with their start and end apart: 10, of which 6 were waited for; matrix products, arithmetic and copies ran while one was open for 0% of the time, Pallas kernels for 16%

profile of v9, /device:TPU:0, one launch (start us, length us, event | category | flops | bytes accessed | tf_op | source)
XLA Modules:
  0.0 25.0 jit_solution(7595941986582396845)
XLA Ops:
  0.0 3.0 %collective-permute-start.2 = (bf16[64,512]{1,0:T(8,128)(2,1)}, bf16[64,512]{1,0:T(8,128)(2,1)S(1)}, u32[]{:S(2)}, u32[]{:S(2)}) collective-permute-start(bf16[64,512]{1,0:T(8,128)(2,1)} %refs_2_.1), channel_id=1, source_target_pairs={{0,2},{1,3},{2,0},{3,1},{4,6},{5,7},{6,4},{7,5},{8,10},{9,11},{10,... | collective-permute-start | bytes 196616 | tf_op jit(solution)/shard_map/ppermute | solution.py:402
  3.0 0.0 collective-permute-start.1
  3.0 0.1 collective-permute-start
  3.7 1.7 %coefficients.1 = (f32[20,8,512]{2,1,0:T(8,128)S(1)}, f32[4,64,512]{2,1,0:T(8,128)S(1)}, f32[32,512]{1,0:T(8,128)S(1)}, bf16[2048,512]{1,0:T(8,128)(2,1)S(1)}, bf16[64,512]{1,0:T(8,128)(2,1)S(1)}) custom-call(f32[1]{0:T(128)S(6)} %copy.6.noise_ref, f32[1,512]{1,0:T(1,128)} %bitcast.4, f32[1,512]{1,0:T(1,128)} %bitcast.5, bf16[64,512]{1,0:T(8,128)(2,1)} %refs_2_.1, ...), custom_call_target="tpu_custom_call" | custom-call | flops 20000000 | bytes 2000000 | tf_op jit(solution)/shard_map/coefficients/pallas_call | solution.py:421
  5.4 0.2 rotate_early.2.refs_3_
  5.7 0.0 collective-permute-done.2.refs_1_
  5.7 0.0 collective-permute-done.1.refs_0_
  5.7 0.3 %rotate_early.3.refs_2_ = f32[64,512]{1,0:T(8,128)S(1)} custom-call(s32[1]{0:T(128)} %bitcast.place_ref, bf16[64,512]{1,0:T(8,128)(2,1)S(1)} %collective-permute-done.1.refs_0_, bf16[64,512]{1,0:T(8,128)(2,1)S(1)} %collective-permute-done.2.refs_1_, bf16[2048,512]{1,0:T(8,128)(2,1)S(1)} %get-tuple-element.18.refs_1_.refs_2_.basis_ref, ...), custom_call_target="tpu_custom_call" | custom-call | tf_op jit(solution)/shard_map/rotate_early/pallas_call | solution.py:455
  6.0 0.9 %collective-permute-done.refs_0_ = bf16[64,512]{1,0:T(8,128)(2,1)S(1)} collective-permute-done((bf16[64,512]{1,0:T(8,128)(2,1)}, bf16[64,512]{1,0:T(8,128)(2,1)S(1)}, u32[]{:S(2)}, u32[]{:S(2)}) %collective-permute-start) | collective-permute-done | bytes 65568 | tf_op jit(solution)/shard_map/ppermute | solution.py:402
  6.9 0.3 %rotate_last.1 = (f32[64,512]{1,0:T(8,128)S(1)}, f32[4,512]{1,0:T(4,128)S(1)}) custom-call(s32[1]{0:T(128)} %bitcast.place_ref, bf16[64,512]{1,0:T(8,128)(2,1)S(1)} %collective-permute-done.refs_0_, bf16[2048,512]{1,0:T(8,128)(2,1)S(1)} %get-tuple-element.18.refs_1_.refs_2_.basis_ref, f32[64,512]{1,0:T(8,128)S(1)} %rotate_early.3.refs_2_, ...), custom_call_target="tpu_custom_call" | custom-call | tf_op jit(solution)/shard_map/rotate_last/pallas_call | solution.py:464
  7.2 3.7 %collective-permute-start.3 = (f32[4,512]{1,0:T(4,128)S(1)}, f32[4,512]{1,0:T(4,128)S(1)}, u32[]{:S(2)}, u32[]{:S(2)}) collective-permute-start(f32[4,512]{1,0:T(4,128)S(1)} %get-tuple-element.26.own_ref), channel_id=1, source_target_pairs={{0,24},{4,28},{8,16},{12,20},{16,8},{20,12},{24,0},{28,4},{1,25},{... | collective-permute-start | bytes 24584 | tf_op jit(solution)/shard_map/ppermute | solution.py:489
  10.9 1.6 %local.1 = (f32[64,512]{1,0:T(8,128)S(1)}, f32[4,32,512]{2,1,0:T(8,128)S(1)}) custom-call(s32[1]{0:T(128)} %bitcast.1.me_ref, f32[64,512]{1,0:T(8,128)S(1)} %get-tuple-element.21.z_ref, f32[20,8,512]{2,1,0:T(8,128)S(1)} %get-tuple-element.22.const_ref, f32[32,512]{1,0:T(8,128)S(1)} %get-tuple-element.23.merge_ref), custom_call_target="tpu_custom_call" | custom-call | flops 10000000 | bytes 1000000 | tf_op jit(solution)/shard_map/local/pallas_call | solution.py:472
  12.4 0.3 %collective-permute-done.3.other_ref = f32[4,512]{1,0:T(4,128)S(1)} collective-permute-done((f32[4,512]{1,0:T(4,128)S(1)}, f32[4,512]{1,0:T(4,128)S(1)}, u32[]{:S(2)}, u32[]{:S(2)}) %collective-permute-start.3) | collective-permute-done | bytes 8224 | tf_op jit(solution)/shard_map/ppermute | solution.py:489
  12.7 0.7 %collective-permute-start.6 = (f32[8,512]{1,0:T(8,128)S(1)}, f32[8,512]{1,0:T(8,128)S(1)}, u32[]{:S(2)}, u32[]{:S(2)}) collective-permute-start(f32[8,512]{1,0:T(8,128)S(1)} %pair.1.refs_0_), channel_id=1, source_target_pairs={{0,12},{4,8},{8,4},{12,0},{16,28},{20,24},{24,20},{28,16},{1,13},{... | collective-permute-start | bytes 49160 | tf_op jit(solution)/shard_map/ppermute | solution.py:492
  13.4 0.8 %collective-permute-start.5 = (f32[8,512]{1,0:T(8,128)S(1)}, f32[8,512]{1,0:T(8,128)S(1)}, u32[]{:S(2)}, u32[]{:S(2)}) collective-permute-start(f32[8,512]{1,0:T(8,128)S(1)} %pair.1.refs_0_), channel_id=1, source_target_pairs={{0,4},{4,0},{8,12},{12,8},{16,20},{20,16},{24,28},{28,24},{1,5},{5... | collective-permute-start | bytes 49160 | tf_op jit(solution)/shard_map/ppermute | solution.py:492
  14.2 2.0 %collective-permute-start.4 = (f32[8,512]{1,0:T(8,128)S(1)}, f32[8,512]{1,0:T(8,128)S(1)}, u32[]{:S(2)}, u32[]{:S(2)}) collective-permute-start(f32[8,512]{1,0:T(8,128)S(1)} %pair.1.refs_0_), channel_id=1, source_target_pairs={{0,8},{4,12},{8,0},{12,4},{16,24},{20,28},{24,16},{28,20},{1,9},{5... | collective-permute-start | bytes 49160 | tf_op jit(solution)/shard_map/ppermute | solution.py:492
  16.2 1.1 %collective-permute-done.6.refs_3_ = f32[8,512]{1,0:T(8,128)S(1)} collective-permute-done((f32[8,512]{1,0:T(8,128)S(1)}, f32[8,512]{1,0:T(8,128)S(1)}, u32[]{:S(2)}, u32[]{:S(2)}) %collective-permute-start.6) | collective-permute-done | bytes 16416 | tf_op jit(solution)/shard_map/ppermute | solution.py:492
  17.3 0.0 collective-permute-done.5.refs_2_
  17.3 0.6 %collective-permute-done.4.refs_1_ = f32[8,512]{1,0:T(8,128)S(1)} collective-permute-done((f32[8,512]{1,0:T(8,128)S(1)}, f32[8,512]{1,0:T(8,128)S(1)}, u32[]{:S(2)}, u32[]{:S(2)}) %collective-permute-start.4) | collective-permute-done | bytes 16416 | tf_op jit(solution)/shard_map/ppermute | solution.py:492
  18.0 0.6 %finish.1 = (bf16[64,512]{1,0:T(8,128)(2,1)S(1)}, bf16[64,512]{1,0:T(8,128)(2,1)S(1)}, bf16[64,512]{1,0:T(8,128)(2,1)S(1)}, bf16[64,512]{1,0:T(8,128)(2,1)S(1)}) custom-call(s32[1]{0:T(128)} %bitcast.place_ref, f32[64,512]{1,0:T(8,128)S(1)} %get-tuple-element.24.r_ref, f32[4,64,512]{2,1,0:T(8,128)S(1)} %get-tuple-element.20.refs_3_.w_ref, ...), custom_call_target="tpu_custom_call" | custom-call | tf_op jit(solution)/shard_map/finish/pallas_call | solution.py:506
  18.6 1.5 %collective-permute-start.7 = (bf16[64,512]{1,0:T(8,128)(2,1)S(1)}, bf16[64,512]{1,0:T(8,128)(2,1)S(1)}, u32[]{:S(2)}, u32[]{:S(2)}) collective-permute-start(bf16[64,512]{1,0:T(8,128)(2,1)S(1)} %get-tuple-element.28), channel_id=1, source_target_pairs={{0,2},{1,3},{2,0},{3,1},{4,6},{5,7},{6,4},{7,5},{8,10},{9,11},{10,... | collective-permute-start | bytes 196616 | tf_op jit(solution)/shard_map/ppermute | solution.py:516
  20.1 0.0 collective-permute-start.8
  20.1 0.7 %collective-permute-start.9 = (bf16[64,512]{1,0:T(8,128)(2,1)S(1)}, bf16[64,512]{1,0:T(8,128)(2,1)S(1)}, u32[]{:S(2)}, u32[]{:S(2)}) collective-permute-start(bf16[64,512]{1,0:T(8,128)(2,1)S(1)} %get-tuple-element.30), channel_id=1, source_target_pairs={{0,1},{1,0},{2,3},{3,2},{4,5},{5,4},{6,7},{7,6},{8,9},{9,8},{10,11... | collective-permute-start | bytes 196616 | tf_op jit(solution)/shard_map/ppermute | solution.py:516
  20.8 0.3 %rest.1 = f32[64,512]{1,0:T(8,128)S(1)} custom-call(s32[1]{0:T(128)} %bitcast.place_ref, bf16[64,512]{1,0:T(8,128)(2,1)S(1)} %get-tuple-element.27.residual_ref, bf16[2048,512]{1,0:T(8,128)(2,1)S(1)} %get-tuple-element.18.refs_1_.refs_2_.basis_ref), custom_call_target="tpu_custom_call" | custom-call | flops 80000000 | bytes 1500000 | tf_op jit(solution)/shard_map/rest/pallas_call | solution.py:519
  21.0 1.8 %collective-permute-done.7 = bf16[64,512]{1,0:T(8,128)(2,1)S(1)} collective-permute-done((bf16[64,512]{1,0:T(8,128)(2,1)S(1)}, bf16[64,512]{1,0:T(8,128)(2,1)S(1)}, u32[]{:S(2)}, u32[]{:S(2)}) %collective-permute-start.7) | collective-permute-done | bytes 65568 | tf_op jit(solution)/shard_map/ppermute | solution.py:516
  22.9 1.4 %collective-permute-done.8 = bf16[64,512]{1,0:T(8,128)(2,1)S(1)} collective-permute-done((bf16[64,512]{1,0:T(8,128)(2,1)S(1)}, bf16[64,512]{1,0:T(8,128)(2,1)S(1)}, u32[]{:S(2)}, u32[]{:S(2)}) %collective-permute-start.8) | collective-permute-done | bytes 65568 | tf_op jit(solution)/shard_map/ppermute | solution.py:516
  24.3 0.0 collective-permute-done.9
  24.3 0.7 %convert_add_fusion = f32[64,512]{1,0:T(8,128)} fusion(bf16[64,512]{1,0:T(8,128)(2,1)S(1)} %collective-permute-done.9, bf16[64,512]{1,0:T(8,128)(2,1)S(1)} %collective-permute-done.8, f32[64,512]{1,0:T(8,128)S(1)} %rest.1, bf16[64,512]{1,0:T(8,128)(2,1)S(1)} %collective-permute-done.7), kind=kLoop, calls=%fused_computation | loop fusion | flops 196608 | bytes 458752 | tf_op jit(solution)/shard_map/add | solution.py:529
  (1 shorter events, 0.0 us)
Async XLA Ops:
  0.0 5.7 %collective-permute-start.2 = (bf16[64,512]{1,0:T(8,128)(2,1)}, bf16[64,512]{1,0:T(8,128)(2,1)S(1)}, u32[]{:S(2)}, u32[]{:S(2)}) collective-permute-start(bf16[64,512]{1,0:T(8,128)(2,1)} %refs_2_.1), channel_id=1, source_target_pairs={{0,2},{1,3},{2,0},{3,1},{4,6},{5,7},{6,4},{7,5},{8,10},{9,11},{10,... | collective-permute-start | bytes 196616 | tf_op jit(solution)/shard_map/ppermute | solution.py:402
  3.0 2.7 %collective-permute-start.1 = (bf16[64,512]{1,0:T(8,128)(2,1)}, bf16[64,512]{1,0:T(8,128)(2,1)S(1)}, u32[]{:S(2)}, u32[]{:S(2)}) collective-permute-start(bf16[64,512]{1,0:T(8,128)(2,1)} %refs_2_.1), channel_id=1, source_target_pairs={{0,1},{1,0},{2,3},{3,2},{4,5},{5,4},{6,7},{7,6},{8,9},{9,8},{10,11... | collective-permute-start | bytes 196616 | tf_op jit(solution)/shard_map/ppermute | solution.py:402
  3.0 4.0 %collective-permute-start = (bf16[64,512]{1,0:T(8,128)(2,1)}, bf16[64,512]{1,0:T(8,128)(2,1)S(1)}, u32[]{:S(2)}, u32[]{:S(2)}) collective-permute-start(bf16[64,512]{1,0:T(8,128)(2,1)} %refs_2_.1), channel_id=1, source_target_pairs={{0,3},{1,2},{2,1},{3,0},{4,7},{5,6},{6,5},{7,4},{8,11},{9,10},{10,... | collective-permute-start | bytes 196616 | tf_op jit(solution)/shard_map/ppermute | solution.py:402
  7.2 5.5 %collective-permute-start.3 = (f32[4,512]{1,0:T(4,128)S(1)}, f32[4,512]{1,0:T(4,128)S(1)}, u32[]{:S(2)}, u32[]{:S(2)}) collective-permute-start(f32[4,512]{1,0:T(4,128)S(1)} %get-tuple-element.26.own_ref), channel_id=1, source_target_pairs={{0,24},{4,28},{8,16},{12,20},{16,8},{20,12},{24,0},{28,4},{1,25},{... | collective-permute-start | bytes 24584 | tf_op jit(solution)/shard_map/ppermute | solution.py:489
  12.7 4.6 %collective-permute-start.6 = (f32[8,512]{1,0:T(8,128)S(1)}, f32[8,512]{1,0:T(8,128)S(1)}, u32[]{:S(2)}, u32[]{:S(2)}) collective-permute-start(f32[8,512]{1,0:T(8,128)S(1)} %pair.1.refs_0_), channel_id=1, source_target_pairs={{0,12},{4,8},{8,4},{12,0},{16,28},{20,24},{24,20},{28,16},{1,13},{... | collective-permute-start | bytes 49160 | tf_op jit(solution)/shard_map/ppermute | solution.py:492
  13.4 3.9 %collective-permute-start.5 = (f32[8,512]{1,0:T(8,128)S(1)}, f32[8,512]{1,0:T(8,128)S(1)}, u32[]{:S(2)}, u32[]{:S(2)}) collective-permute-start(f32[8,512]{1,0:T(8,128)S(1)} %pair.1.refs_0_), channel_id=1, source_target_pairs={{0,4},{4,0},{8,12},{12,8},{16,20},{20,16},{24,28},{28,24},{1,5},{5... | collective-permute-start | bytes 49160 | tf_op jit(solution)/shard_map/ppermute | solution.py:492
  14.2 3.7 %collective-permute-start.4 = (f32[8,512]{1,0:T(8,128)S(1)}, f32[8,512]{1,0:T(8,128)S(1)}, u32[]{:S(2)}, u32[]{:S(2)}) collective-permute-start(f32[8,512]{1,0:T(8,128)S(1)} %pair.1.refs_0_), channel_id=1, source_target_pairs={{0,8},{4,12},{8,0},{12,4},{16,24},{20,28},{24,16},{28,20},{1,9},{5... | collective-permute-start | bytes 49160 | tf_op jit(solution)/shard_map/ppermute | solution.py:492
  18.6 4.3 %collective-permute-start.7 = (bf16[64,512]{1,0:T(8,128)(2,1)S(1)}, bf16[64,512]{1,0:T(8,128)(2,1)S(1)}, u32[]{:S(2)}, u32[]{:S(2)}) collective-permute-start(bf16[64,512]{1,0:T(8,128)(2,1)S(1)} %get-tuple-element.28), channel_id=1, source_target_pairs={{0,2},{1,3},{2,0},{3,1},{4,6},{5,7},{6,4},{7,5},{8,10},{9,11},{10,... | collective-permute-start | bytes 196616 | tf_op jit(solution)/shard_map/ppermute | solution.py:516
  20.1 4.2 %collective-permute-start.8 = (bf16[64,512]{1,0:T(8,128)(2,1)S(1)}, bf16[64,512]{1,0:T(8,128)(2,1)S(1)}, u32[]{:S(2)}, u32[]{:S(2)}) collective-permute-start(bf16[64,512]{1,0:T(8,128)(2,1)S(1)} %get-tuple-element.29), channel_id=1, source_target_pairs={{0,3},{1,2},{2,1},{3,0},{4,7},{5,6},{6,5},{7,4},{8,11},{9,10},{10,... | collective-permute-start | bytes 196616 | tf_op jit(solution)/shard_map/ppermute | solution.py:516
  20.1 4.2 %collective-permute-start.9 = (bf16[64,512]{1,0:T(8,128)(2,1)S(1)}, bf16[64,512]{1,0:T(8,128)(2,1)S(1)}, u32[]{:S(2)}, u32[]{:S(2)}) collective-permute-start(bf16[64,512]{1,0:T(8,128)(2,1)S(1)} %get-tuple-element.30), channel_id=1, source_target_pairs={{0,1},{1,0},{2,3},{3,2},{4,5},{5,4},{6,7},{7,6},{8,9},{9,8},{10,11... | collective-permute-start | bytes 196616 | tf_op jit(solution)/shard_map/ppermute | solution.py:516

commit v10 on v6

--- a/solution.py
+++ b/solution.py
@@ -10,7 +10,7 @@
 
 F32 = jnp.float32
 SUB = 8
-MIRROR, NEAR = 6, (3, 1, 2)
+MIRROR, NEAR = 4, (3, 2, 1)
 GROUP = (0, MIRROR) + tuple(step ^ other for step in NEAR for other in (0, MIRROR))
 VMEM_LIMIT = 24 * 1024 * 1024
 

time: 25.2 us -> 25.5 us (1.012); the launches traced: 24.8 us -> 25.4 us
  waiting for transfers between devices: 5.98 us -> 7.56 us
  starting transfers between devices: 12.5 us -> 11.5 us
    ppermute x3, waiting for transfers between devices: 0.16 us -> 1.63 us  [shards(): lax.ppermute(pair, 'tm', [(a, a ^ step) for a in range(blocks)])]
    ppermute x1, starting transfers between devices: 3.67 us -> 2.65 us  [shards(): lax.ppermute(summary, 'tm', [(a, a ^ MIRROR) for a in range(blocks)])]
  transfers between devices with their start and end apart: 10 -> 10, of which waited for: 5 -> 6; matrix products, arithmetic and copies ran while one was open for 0% -> 0% of each run, Pallas kernels for 17% -> 17%
where the time goes in v10:
time: 25.5 us; the launch traced here: 25.4 us
  starting transfers between devices  11.5 us (45%)
  waiting for transfers between devices  7.56 us (30%)
  Pallas kernels  4.92 us (19%)
  between operations  0.71 us (3%)
  other arithmetic  0.68 us (3%)
    ppermute x3, starting transfers between devices, shards(): lax.ppermute(pair, 'tm', [(a, a ^ step) for a in range(blocks)])  3.49 us
    ppermute x3, starting transfers between devices, exchange(): out.append(lax.ppermute(value, axis, [(a, a ^ step) for a in range(count)]))  3.08 us
    ppermute x2, waiting for transfers between devices, shards(): lax.ppermute(part, 'mode', [(a, a ^ piece) for a in range(pieces)])  3.03 us
    ppermute x1, starting transfers between devices, shards(): lax.ppermute(summary, 'tm', [(a, a ^ MIRROR) for a in range(blocks)])  2.65 us
    ppermute x1, waiting for transfers between devices, shards(): lax.ppermute(summary, 'tm', [(a, a ^ MIRROR) for a in range(blocks)])  1.96 us
    pallas_call x1, Pallas kernels, shards(): pl.pallas_call(functools.partial(coefficients_kernel, blocks), out_shape=...  1.7 us
    ppermute x3, waiting for transfers between devices, shards(): lax.ppermute(pair, 'tm', [(a, a ^ step) for a in range(blocks)])  1.63 us
    pallas_call x1, Pallas kernels, shards(): pl.pallas_call(functools.partial(local_kernel, blocks), out_shape=(shape(...  1.57 us
  transfers between devices with their start and end apart: 10, of which 6 were waited for; matrix products, arithmetic and copies ran while one was open for 0% of the time, Pallas kernels for 17%

profile of v10, /device:TPU:0, one launch (start us, length us, event | category | flops | bytes accessed | tf_op | source)
XLA Modules:
  0.0 25.4 jit_solution(13487446115421758612)
XLA Ops:
  0.0 3.0 %collective-permute-start.1 = (bf16[64,512]{1,0:T(8,128)(2,1)}, bf16[64,512]{1,0:T(8,128)(2,1)S(1)}, u32[]{:S(2)}, u32[]{:S(2)}) collective-permute-start(bf16[64,512]{1,0:T(8,128)(2,1)} %refs_2_.1), channel_id=1, source_target_pairs={{0,2},{1,3},{2,0},{3,1},{4,6},{5,7},{6,4},{7,5},{8,10},{9,11},{10,... | collective-permute-start | bytes 196616 | tf_op jit(solution)/shard_map/ppermute | solution.py:402
  3.0 0.0 collective-permute-start.2
  3.0 0.1 collective-permute-start
  3.7 1.7 %coefficients.1 = (f32[20,8,512]{2,1,0:T(8,128)S(1)}, f32[4,64,512]{2,1,0:T(8,128)S(1)}, f32[32,512]{1,0:T(8,128)S(1)}, bf16[2048,512]{1,0:T(8,128)(2,1)S(1)}, bf16[64,512]{1,0:T(8,128)(2,1)S(1)}) custom-call(f32[1]{0:T(128)S(6)} %copy.6.noise_ref, f32[1,512]{1,0:T(1,128)} %bitcast.4, f32[1,512]{1,0:T(1,128)} %bitcast.5, bf16[64,512]{1,0:T(8,128)(2,1)} %refs_2_.1, ...), custom_call_target="tpu_custom_call" | custom-call | flops 20000000 | bytes 2000000 | tf_op jit(solution)/shard_map/coefficients/pallas_call | solution.py:421
  5.4 0.2 rotate_early.2.refs_3_
  5.7 0.0 collective-permute-done.1.refs_0_
  5.7 0.0 collective-permute-done.2.refs_1_
  5.7 0.3 %rotate_early.3.refs_2_ = f32[64,512]{1,0:T(8,128)S(1)} custom-call(s32[1]{0:T(128)} %bitcast.place_ref, bf16[64,512]{1,0:T(8,128)(2,1)S(1)} %collective-permute-done.1.refs_0_, bf16[64,512]{1,0:T(8,128)(2,1)S(1)} %collective-permute-done.2.refs_1_, bf16[2048,512]{1,0:T(8,128)(2,1)S(1)} %get-tuple-element.19.refs_1_.refs_2_.basis_ref, ...), custom_call_target="tpu_custom_call" | custom-call | tf_op jit(solution)/shard_map/rotate_early/pallas_call | solution.py:455
  6.0 0.9 %collective-permute-done.refs_0_ = bf16[64,512]{1,0:T(8,128)(2,1)S(1)} collective-permute-done((bf16[64,512]{1,0:T(8,128)(2,1)}, bf16[64,512]{1,0:T(8,128)(2,1)S(1)}, u32[]{:S(2)}, u32[]{:S(2)}) %collective-permute-start) | collective-permute-done | bytes 65568 | tf_op jit(solution)/shard_map/ppermute | solution.py:402
  6.9 0.3 rotate_last.1
  7.2 2.7 %collective-permute-start.3 = (f32[4,512]{1,0:T(4,128)S(1)}, f32[4,512]{1,0:T(4,128)S(1)}, u32[]{:S(2)}, u32[]{:S(2)}) collective-permute-start(f32[4,512]{1,0:T(4,128)S(1)} %get-tuple-element.27.own_ref), channel_id=1, source_target_pairs={{0,16},{4,20},{8,24},{12,28},{16,0},{20,4},{24,8},{28,12},{1,17},{... | collective-permute-start | bytes 24584 | tf_op jit(solution)/shard_map/ppermute | solution.py:479
  9.8 2.0 %collective-permute-done.3.other_ref = f32[4,512]{1,0:T(4,128)S(1)} collective-permute-done((f32[4,512]{1,0:T(4,128)S(1)}, f32[4,512]{1,0:T(4,128)S(1)}, u32[]{:S(2)}, u32[]{:S(2)}) %collective-permute-start.3) | collective-permute-done | bytes 8224 | tf_op jit(solution)/shard_map/ppermute | solution.py:479
  11.8 2.5 %collective-permute-start.4 = (f32[8,512]{1,0:T(8,128)S(1)}, f32[8,512]{1,0:T(8,128)S(1)}, u32[]{:S(2)}, u32[]{:S(2)}) collective-permute-start(f32[8,512]{1,0:T(8,128)S(1)} %pair.1.refs_0_), channel_id=1, source_target_pairs={{0,12},{4,8},{8,4},{12,0},{16,28},{20,24},{24,20},{28,16},{1,13},{... | collective-permute-start | bytes 49160 | tf_op jit(solution)/shard_map/ppermute | solution.py:482
  14.3 0.4 %collective-permute-start.5 = (f32[8,512]{1,0:T(8,128)S(1)}, f32[8,512]{1,0:T(8,128)S(1)}, u32[]{:S(2)}, u32[]{:S(2)}) collective-permute-start(f32[8,512]{1,0:T(8,128)S(1)} %pair.1.refs_0_), channel_id=1, source_target_pairs={{0,8},{4,12},{8,0},{12,4},{16,24},{20,28},{24,16},{28,20},{1,9},{5... | collective-permute-start | bytes 49160 | tf_op jit(solution)/shard_map/ppermute | solution.py:482
  14.8 0.5 %collective-permute-start.6 = (f32[8,512]{1,0:T(8,128)S(1)}, f32[8,512]{1,0:T(8,128)S(1)}, u32[]{:S(2)}, u32[]{:S(2)}) collective-permute-start(f32[8,512]{1,0:T(8,128)S(1)} %pair.1.refs_0_), channel_id=1, source_target_pairs={{0,4},{4,0},{8,12},{12,8},{16,20},{20,16},{24,28},{28,24},{1,5},{5... | collective-permute-start | bytes 49160 | tf_op jit(solution)/shard_map/ppermute | solution.py:482
  15.3 1.6 %local.1 = (f32[64,512]{1,0:T(8,128)S(1)}, f32[4,32,512]{2,1,0:T(8,128)S(1)}) custom-call(s32[1]{0:T(128)} %bitcast.1.me_ref, f32[64,512]{1,0:T(8,128)S(1)} %get-tuple-element.22.z_ref, f32[20,8,512]{2,1,0:T(8,128)S(1)} %get-tuple-element.23.const_ref, f32[32,512]{1,0:T(8,128)S(1)} %get-tuple-element.24.merge_ref), custom_call_target="tpu_custom_call" | custom-call | flops 10000000 | bytes 1000000 | tf_op jit(solution)/shard_map/local/pallas_call | solution.py:494
  16.9 0.0 collective-permute-done.4.refs_1_
  16.9 1.2 %collective-permute-done.5.refs_2_ = f32[8,512]{1,0:T(8,128)S(1)} collective-permute-done((f32[8,512]{1,0:T(8,128)S(1)}, f32[8,512]{1,0:T(8,128)S(1)}, u32[]{:S(2)}, u32[]{:S(2)}) %collective-permute-start.5) | collective-permute-done | bytes 16416 | tf_op jit(solution)/shard_map/ppermute | solution.py:482
  18.0 0.4 %collective-permute-done.6.refs_3_ = f32[8,512]{1,0:T(8,128)S(1)} collective-permute-done((f32[8,512]{1,0:T(8,128)S(1)}, f32[8,512]{1,0:T(8,128)S(1)}, u32[]{:S(2)}, u32[]{:S(2)}) %collective-permute-start.6) | collective-permute-done | bytes 16416 | tf_op jit(solution)/shard_map/ppermute | solution.py:482
  18.5 0.5 %finish.1 = (bf16[64,512]{1,0:T(8,128)(2,1)S(1)}, bf16[64,512]{1,0:T(8,128)(2,1)S(1)}, bf16[64,512]{1,0:T(8,128)(2,1)S(1)}) custom-call(s32[1]{0:T(128)} %bitcast.place_ref, f32[64,512]{1,0:T(8,128)S(1)} %get-tuple-element.25.r_ref, f32[4,64,512]{2,1,0:T(8,128)S(1)} %get-tuple-element.21.refs_3_.w_ref, f32[4,32,512]{2,1,0:T(8,128)S(1)} %get-tuple-element.26.g_ref, ...), custom_call_target="tpu_custom_call" | custom-call | tf_op jit(solution)/shard_map/finish/pallas_call | solution.py:504
  19.0 1.5 %collective-permute-start.9 = (bf16[64,512]{1,0:T(8,128)(2,1)S(1)}, bf16[64,512]{1,0:T(8,128)(2,1)S(1)}, u32[]{:S(2)}, u32[]{:S(2)}) collective-permute-start(bf16[64,512]{1,0:T(8,128)(2,1)S(1)} %get-tuple-element.32), channel_id=1, source_target_pairs={{0,2},{1,3},{2,0},{3,1},{4,6},{5,7},{6,4},{7,5},{8,10},{9,11},{10,... | collective-permute-start | bytes 196616 | tf_op jit(solution)/shard_map/ppermute | solution.py:514
  20.5 0.0 collective-permute-start.8
  20.5 0.4 %rest.1 = (f32[64,512]{1,0:T(8,128)S(1)}, bf16[64,512]{1,0:T(8,128)(2,1)S(1)}) custom-call(s32[1]{0:T(128)} %bitcast.place_ref, bf16[64,512]{1,0:T(8,128)(2,1)S(1)} %get-tuple-element.28.residual_ref, bf16[2048,512]{1,0:T(8,128)(2,1)S(1)} %get-tuple-element.19.refs_1_.refs_2_.basis_ref), custom_call_target="tpu_custom_call" | custom-call | tf_op jit(solution)/shard_map/rest/pallas_call | solution.py:517
  20.9 0.7 %collective-permute-start.7 = (bf16[64,512]{1,0:T(8,128)(2,1)S(1)}, bf16[64,512]{1,0:T(8,128)(2,1)S(1)}, u32[]{:S(2)}, u32[]{:S(2)}) collective-permute-start(bf16[64,512]{1,0:T(8,128)(2,1)S(1)} %get-tuple-element.30), channel_id=1, source_target_pairs={{0,1},{1,0},{2,3},{3,2},{4,5},{5,4},{6,7},{7,6},{8,9},{9,8},{10,11... | collective-permute-start | bytes 196616 | tf_op jit(solution)/shard_map/ppermute | solution.py:525
  21.7 1.6 %collective-permute-done.9 = bf16[64,512]{1,0:T(8,128)(2,1)S(1)} collective-permute-done((bf16[64,512]{1,0:T(8,128)(2,1)S(1)}, bf16[64,512]{1,0:T(8,128)(2,1)S(1)}, u32[]{:S(2)}, u32[]{:S(2)}) %collective-permute-start.9) | collective-permute-done | bytes 65568 | tf_op jit(solution)/shard_map/ppermute | solution.py:514
  23.3 1.4 %collective-permute-done.8 = bf16[64,512]{1,0:T(8,128)(2,1)S(1)} collective-permute-done((bf16[64,512]{1,0:T(8,128)(2,1)S(1)}, bf16[64,512]{1,0:T(8,128)(2,1)S(1)}, u32[]{:S(2)}, u32[]{:S(2)}) %collective-permute-start.8) | collective-permute-done | bytes 65568 | tf_op jit(solution)/shard_map/ppermute | solution.py:514
  24.7 0.0 collective-permute-done.7
  24.7 0.7 %add_add_fusion = f32[64,512]{1,0:T(8,128)} fusion(bf16[64,512]{1,0:T(8,128)(2,1)S(1)} %collective-permute-done.9, bf16[64,512]{1,0:T(8,128)(2,1)S(1)} %collective-permute-done.8, f32[64,512]{1,0:T(8,128)S(1)} %get-tuple-element.29, bf16[64,512]{1,0:T(8,128)(2,1)S(1)} %collective-permute-done.7), kind=kLoop, calls=%fused_computation | loop fusion | flops 196608 | bytes 458752 | tf_op jit(solution)/shard_map/add | solution.py:527
  (1 shorter events, 0.0 us)
Async XLA Ops:
  0.0 5.7 %collective-permute-start.1 = (bf16[64,512]{1,0:T(8,128)(2,1)}, bf16[64,512]{1,0:T(8,128)(2,1)S(1)}, u32[]{:S(2)}, u32[]{:S(2)}) collective-permute-start(bf16[64,512]{1,0:T(8,128)(2,1)} %refs_2_.1), channel_id=1, source_target_pairs={{0,2},{1,3},{2,0},{3,1},{4,6},{5,7},{6,4},{7,5},{8,10},{9,11},{10,... | collective-permute-start | bytes 196616 | tf_op jit(solution)/shard_map/ppermute | solution.py:402
  3.0 2.7 %collective-permute-start.2 = (bf16[64,512]{1,0:T(8,128)(2,1)}, bf16[64,512]{1,0:T(8,128)(2,1)S(1)}, u32[]{:S(2)}, u32[]{:S(2)}) collective-permute-start(bf16[64,512]{1,0:T(8,128)(2,1)} %refs_2_.1), channel_id=1, source_target_pairs={{0,1},{1,0},{2,3},{3,2},{4,5},{5,4},{6,7},{7,6},{8,9},{9,8},{10,11... | collective-permute-start | bytes 196616 | tf_op jit(solution)/shard_map/ppermute | solution.py:402
  3.0 4.0 %collective-permute-start = (bf16[64,512]{1,0:T(8,128)(2,1)}, bf16[64,512]{1,0:T(8,128)(2,1)S(1)}, u32[]{:S(2)}, u32[]{:S(2)}) collective-permute-start(bf16[64,512]{1,0:T(8,128)(2,1)} %refs_2_.1), channel_id=1, source_target_pairs={{0,3},{1,2},{2,1},{3,0},{4,7},{5,6},{6,5},{7,4},{8,11},{9,10},{10,... | collective-permute-start | bytes 196616 | tf_op jit(solution)/shard_map/ppermute | solution.py:402
  7.2 4.6 %collective-permute-start.3 = (f32[4,512]{1,0:T(4,128)S(1)}, f32[4,512]{1,0:T(4,128)S(1)}, u32[]{:S(2)}, u32[]{:S(2)}) collective-permute-start(f32[4,512]{1,0:T(4,128)S(1)} %get-tuple-element.27.own_ref), channel_id=1, source_target_pairs={{0,16},{4,20},{8,24},{12,28},{16,0},{20,4},{24,8},{28,12},{1,17},{... | collective-permute-start | bytes 24584 | tf_op jit(solution)/shard_map/ppermute | solution.py:479
  11.8 5.1 %collective-permute-start.4 = (f32[8,512]{1,0:T(8,128)S(1)}, f32[8,512]{1,0:T(8,128)S(1)}, u32[]{:S(2)}, u32[]{:S(2)}) collective-permute-start(f32[8,512]{1,0:T(8,128)S(1)} %pair.1.refs_0_), channel_id=1, source_target_pairs={{0,12},{4,8},{8,4},{12,0},{16,28},{20,24},{24,20},{28,16},{1,13},{... | collective-permute-start | bytes 49160 | tf_op jit(solution)/shard_map/ppermute | solution.py:482
  14.3 3.7 %collective-permute-start.5 = (f32[8,512]{1,0:T(8,128)S(1)}, f32[8,512]{1,0:T(8,128)S(1)}, u32[]{:S(2)}, u32[]{:S(2)}) collective-permute-start(f32[8,512]{1,0:T(8,128)S(1)} %pair.1.refs_0_), channel_id=1, source_target_pairs={{0,8},{4,12},{8,0},{12,4},{16,24},{20,28},{24,16},{28,20},{1,9},{5... | collective-permute-start | bytes 49160 | tf_op jit(solution)/shard_map/ppermute | solution.py:482
  14.8 3.7 %collective-permute-start.6 = (f32[8,512]{1,0:T(8,128)S(1)}, f32[8,512]{1,0:T(8,128)S(1)}, u32[]{:S(2)}, u32[]{:S(2)}) collective-permute-start(f32[8,512]{1,0:T(8,128)S(1)} %pair.1.refs_0_), channel_id=1, source_target_pairs={{0,4},{4,0},{8,12},{12,8},{16,20},{20,16},{24,28},{28,24},{1,5},{5... | collective-permute-start | bytes 49160 | tf_op jit(solution)/shard_map/ppermute | solution.py:482
  19.0 4.3 %collective-permute-start.9 = (bf16[64,512]{1,0:T(8,128)(2,1)S(1)}, bf16[64,512]{1,0:T(8,128)(2,1)S(1)}, u32[]{:S(2)}, u32[]{:S(2)}) collective-permute-start(bf16[64,512]{1,0:T(8,128)(2,1)S(1)} %get-tuple-element.32), channel_id=1, source_target_pairs={{0,2},{1,3},{2,0},{3,1},{4,6},{5,7},{6,4},{7,5},{8,10},{9,11},{10,... | collective-permute-start | bytes 196616 | tf_op jit(solution)/shard_map/ppermute | solution.py:514
  20.5 4.2 %collective-permute-start.8 = (bf16[64,512]{1,0:T(8,128)(2,1)S(1)}, bf16[64,512]{1,0:T(8,128)(2,1)S(1)}, u32[]{:S(2)}, u32[]{:S(2)}) collective-permute-start(bf16[64,512]{1,0:T(8,128)(2,1)S(1)} %get-tuple-element.31), channel_id=1, source_target_pairs={{0,3},{1,2},{2,1},{3,0},{4,7},{5,6},{6,5},{7,4},{8,11},{9,10},{10,... | collective-permute-start | bytes 196616 | tf_op jit(solution)/shard_map/ppermute | solution.py:514
  20.9 3.8 %collective-permute-start.7 = (bf16[64,512]{1,0:T(8,128)(2,1)S(1)}, bf16[64,512]{1,0:T(8,128)(2,1)S(1)}, u32[]{:S(2)}, u32[]{:S(2)}) collective-permute-start(bf16[64,512]{1,0:T(8,128)(2,1)S(1)} %get-tuple-element.30), channel_id=1, source_target_pairs={{0,1},{1,0},{2,3},{3,2},{4,5},{5,4},{6,7},{7,6},{8,9},{9,8},{10,11... | collective-permute-start | bytes 196616 | tf_op jit(solution)/shard_map/ppermute | solution.py:525
